TPU v7x, 512 devices: a whole 4x4x16 slice. The times are simulated.
512 devices in a mesh: dp: 16 (over x, z_hi), rows: 32 (over y, z_lo, core).
Axes of the slice: x: 4, y: 4, z: 16 (z_hi: 4, z_lo: 4; z = z_hi * 4 + z_lo), core: 2. Of those that a mesh axis runs over, the one named last changes fastest.
Arguments:
- cotangent: bfloat16 [64, 64, 128, 128], P('dp', 'rows'), may hold values from -6 to 6
- inputs: bfloat16 [16, 128, 64, 256], P('dp', 'rows'), may hold values from -6 to 6
- w_first: bfloat16 [3, 3, 256, 256], replicated, may hold values from -0.125 to 0.125
- bias_first: float32 [256], replicated, may hold values from -3 to 3
- w_second: bfloat16 [3, 3, 256, 128], replicated, may hold values from -0.125 to 0.125
Outputs:
- grad_input: bfloat16 [16, 128, 64, 256], P('dp', 'rows')
- grad_w_first: float32 [2304, 256], P('dp')
- grad_w_second: float32 [2304, 128], P('dp')
- grad_bias: float32 [256], P('dp')
All inputs are finite; a program needn't handle non-finite values.
Results may differ from a plain program's by a relative error of at most 0.0075.
Values may be sent and summed in bfloat16 or wider, within the bound.
No kernel may reach another device: no remote copies, remote signals or barrier semaphores. Data moves between devices by JAX's collectives and lax.ppermute only.
A program may use at most 64 MiB of HBM per device.

v0:
```python
import jax
import jax.numpy as jnp
from jax import lax
from jax.sharding import PartitionSpec as P


def passed_along(value, axis, by):
    devices = lax.axis_size(axis)
    pairs = [(i, i + by) for i in range(devices) if 0 <= i + by < devices]
    return lax.ppermute(value, axis, pairs)


def from_partner(value, axis, distance):
    mask = 2**distance
    pairs = [(source, source ^ mask) for source in range(lax.axis_size(axis))]
    return lax.ppermute(value, axis, pairs)


def with_halo(value, sides, width):
    for axis, dim in sides:
        devices, length = (lax.axis_size(axis), value.shape[dim])
        up = [(i, (i + 1) % devices) for i in range(devices - 1)]
        down = [(j, i) for i, j in up]
        last = lax.slice_in_dim(value, length - width, length, axis=dim)
        first = lax.slice_in_dim(value, 0, width, axis=dim)
        before = lax.ppermute(last, axis, up)
        after = lax.ppermute(first, axis, down)
        value = jnp.concatenate([before, value, after], axis=dim)
    return value


def pad_columns(values):
    return jnp.pad(values, ((0, 0), (0, 0), (1, 1), (0, 0)))


def conv_apply(padded, weight):
    rows_out = padded.shape[1] - 2
    cols_out = padded.shape[2] - 2
    chan_in = padded.shape[3]
    total = jnp.zeros((padded.shape[0] * rows_out * cols_out, weight.shape[3]), jnp.float32)
    for offset_y in range(3):
        for offset_x in range(3):
            window = padded[
                :, offset_y : offset_y + rows_out, offset_x : offset_x + cols_out
            ].reshape(-1, chan_in)
            total = total + jnp.dot(
                window, weight[offset_y, offset_x], preferred_element_type=jnp.float32
            )
    return total.reshape(padded.shape[0], rows_out, cols_out, weight.shape[3])


def conv_adjoint(padded, weight):
    return conv_apply(padded, jnp.transpose(weight[::-1, ::-1], (0, 1, 3, 2)))


def weight_grad(padded, gradient):
    rows_out = gradient.shape[1]
    cols_out = gradient.shape[2]
    chan_in = padded.shape[3]
    flat_grad = gradient.reshape(-1, gradient.shape[3])
    taps = []
    for offset_y in range(3):
        for offset_x in range(3):
            window = padded[
                :, offset_y : offset_y + rows_out, offset_x : offset_x + cols_out
            ].reshape(-1, chan_in)
            taps.append(
                lax.dot_general(
                    window, flat_grad, (((0,), (0,)), ((), ())), preferred_element_type=jnp.float32
                )
            )
    return jnp.stack(taps).reshape(3, 3, chan_in, gradient.shape[3])


def silu_slope(preact):
    sigma = jax.nn.sigmoid(preact)
    return sigma * (1.0 + preact * (1.0 - sigma))


def regroup_four(pieces, device_rank, swapper):
    layout = pieces.reshape((2, 2) + pieces.shape[1:])
    for level in (0, 1):
        own_bit = device_rank // (1 << level) % 2
        position = 1 - level
        lower_half = lax.index_in_dim(layout, 0, position, keepdims=False)
        upper_half = lax.index_in_dim(layout, 1, position, keepdims=False)
        keep_part = jnp.where(own_bit == 0, lower_half, upper_half)
        send_part = jnp.where(own_bit == 0, upper_half, lower_half)
        received = swapper(send_part, level)
        new_lower = jnp.where(own_bit == 0, keep_part, received)
        new_upper = jnp.where(own_bit == 0, received, keep_part)
        layout = jnp.stack([new_lower, new_upper], axis=position)
    return layout.reshape(pieces.shape)


def shards(cotangent, inputs, w_first, bias_first, w_second):
    device_rank = lax.axis_index("rows")
    edge_above = passed_along(inputs[:, -1:], "rows", 4)
    edge_below = passed_along(inputs[:, :1], "rows", -4)
    padded_in = pad_columns(jnp.concatenate([edge_above, inputs, edge_below], axis=1))
    preact = conv_apply(padded_in, w_first) + bias_first
    activation = jax.nn.silu(preact).astype(jnp.bfloat16)
    slab_rows = activation.shape[1]
    cols_low = activation.shape[2]
    chan_low = activation.shape[3]
    piece_rows = slab_rows // 4

    def send_act(values, level):
        return from_partner(values, "rows", level)

    regrouped = regroup_four(
        activation.reshape(4, piece_rows, cols_low, chan_low), device_rank, send_act
    )
    widened = with_halo(regrouped, (("rows", 1),), 1)
    upsampled = jnp.repeat(jnp.repeat(widened, 2, axis=1), 2, axis=2)[:, 1:-1]
    padded_cot = pad_columns(with_halo(cotangent, (("rows", 1),), 1))
    grad_up = conv_adjoint(padded_cot, w_second)
    raw_second = weight_grad(pad_columns(upsampled), cotangent)
    image_count, rows_high, cols_high, chan_high = cotangent.shape
    grad_act = grad_up.reshape(image_count, rows_high // 2, 2, cols_low, 2, chan_low).sum(
        axis=(2, 4)
    )

    def send_grad(values, level):
        return from_partner(values, "rows", level)

    returned = regroup_four(grad_act, device_rank, send_grad)
    grad_slab = returned.reshape(1, slab_rows, cols_low, chan_low)
    delta = (grad_slab * silu_slope(preact)).astype(jnp.bfloat16)
    raw_bias = jnp.sum(delta, axis=(0, 1, 2), dtype=jnp.float32)
    raw_first = weight_grad(padded_in, delta)
    delta_top = passed_along(delta[:, -1:], "rows", 4)
    delta_bottom = passed_along(delta[:, :1], "rows", -4)
    padded_delta = pad_columns(jnp.concatenate([delta_top, delta, delta_bottom], axis=1))
    grad_input = conv_adjoint(padded_delta, w_first).astype(jnp.bfloat16)
    flat_first = raw_first.reshape(9 * chan_low, chan_low)
    flat_second = raw_second.reshape(9 * chan_low, chan_high)
    summed_first, summed_second, summed_bias = lax.psum((flat_first, flat_second, raw_bias), "rows")
    total_first, total_second, total_bias = (
        lax.psum_scatter(summed_first, "dp", scatter_dimension=0, tiled=True),
        lax.psum_scatter(summed_second, "dp", scatter_dimension=0, tiled=True),
        lax.psum_scatter(summed_bias, "dp", scatter_dimension=0, tiled=True),
    )
    pixel_high = lax.axis_size("dp") * image_count * rows_high * lax.axis_size("rows") * cols_high
    pixel_low = pixel_high // 4
    scale_low = pixel_low ** (-0.5)
    scale_high = pixel_high ** (-0.5)
    return (grad_input, total_first * scale_low, total_second * scale_high, total_bias * scale_low)


def solution(mesh):
    in_specs = (P("dp", "rows", None, None), P("dp", "rows", None, None), P(), P(), P())
    out_specs = (P("dp", "rows", None, None), P("dp", None), P("dp", None), P("dp"))
    return jax.shard_map(shards, mesh=mesh, in_specs=in_specs, out_specs=out_specs, check_vma=False)
```

profile of v0, /device:TPU:1, one launch (start us, length us, event | category | flops | bytes accessed | tf_op | source)
XLA Modules:
  0.0 622.8 jit_solution(11963084722178128225)
XLA Ops:
  7.2 0.8 fusion.99
  8.0 1.3 collective-permute-start.5
  9.3 6.4 %collective-permute-start.4 = (bf16[1,1,64,256]{3,2,1,0:T(8,128)(2,1)S(1)}, bf16[1,1,64,256]{3,2,1,0:T(8,128)(2,1)S(1)}, u32[]{:S(2)}, u32[]{:S(2)}) collective-permute-start(bf16[1,1,64,256]{3,2,1,0:T(8,128)(2,1)S(1)} %get-tuple-element.50), channel_id=1, source_target_pairs={{0,4},{1,5},{2,6},{3,7},{4,8},{5,9},{6,10},{7,11},{8,12},{9,13},{1... | collective-permute-start | bytes 98312 | tf_op jit(solution)/shard_map/ppermute | solution.py:10
  15.7 1.7 fusion.95
  17.4 7.9 %collective-permute-start.1 = (bf16[4,1,128,128]{3,2,1,0:T(8,128)(2,1)}, bf16[4,1,128,128]{3,2,1,0:T(8,128)(2,1)}, u32[]{:S(2)}, u32[]{:S(2)}) collective-permute-start(bf16[4,1,128,128]{3,2,1,0:T(8,128)(2,1)} %get-tuple-element.27), channel_id=1, source_target_pairs={{1,0},{2,1},{3,2},{4,3},{5,4},{6,5},{7,6},{8,7},{9,8},{10,9},{11,1... | collective-permute-start | bytes 393224 | tf_op jit(solution)/shard_map/ppermute | solution.py:27
  25.2 1.9 collective-permute-start
  27.2 1.1 reverse_bitcast_fusion.1
  28.4 0.7 fusion.97
  29.2 0.4 copy-done.1
  29.8 0.7 pad_maximum_fusion.6
  31.5 0.9 convolution_add_fusion.15
  32.4 1.1 fusion.27
  34.5 1.0 pad_maximum_fusion.1
  37.6 1.6 reshape_reshape.15
  39.2 2.0 reduce_sum.18
  41.2 3.2 collective-permute-start.2
  44.6 0.8 collective-permute-done.2
  45.5 1.9 collective-permute-start.3
  47.6 4.5 collective-permute-done.3
  52.3 3.1 collective-permute-start.8
  55.4 0.9 collective-permute-done.8
  56.3 1.9 collective-permute-start.9
  58.2 3.1 collective-permute-done.9
  61.4 3.4 collective-permute-start.11
  64.8 2.2 collective-permute-start.10
  66.9 0.7 collective-permute-done.11
  67.6 1.2 collective-permute-done.10
  69.4 0.4 broadcast_in_dim.8
  69.9 1.3 slice.379
  71.2 1.6 fusion.93
  72.8 1.8 copy.79
  74.9 0.7 copy-done.13
  75.9 0.4 fusion.19
  76.3 0.4 fusion.18
  79.1 1.0 copy-done.4
  80.4 0.6 copy-done.6
  82.9 1.4 copy-done.3
  84.4 1.3 dynamic-slice
  86.5 1.3 collective-permute-start.7
  87.8 4.9 collective-permute-start.6
  92.8 49.3 %all-reduce.4 = f32[256]{0:T(256)S(1)} all-reduce(f32[256]{0:T(256)S(1)} %get-tuple-element.6), channel_id=4, replica_groups=mesh['dp'=16,'rows'=32] {'dp'}, use_global_device_ids=true, to_apply=%region_7.8.clone | all-reduce | flops 256 | bytes 2048
  142.2 75.9 %psum.26 = f32[16]{0:T(128)S(1)} all-reduce(f32[16]{0:T(128)S(1)} %dynamic-slice.1), channel_id=1, replica_groups=mesh['dp'=16,'rows'=32] {'rows'}, use_global_device_ids=true, to_apply=%region_6.7 | all-reduce | flops 16 | bytes 128 | tf_op jit(solution)/shard_map/psum | solution.py:138
  218.1 0.5 broadcast_multiply_fusion.2
  220.7 116.0 %reduce-scatter.3.cloned.1.call-done = f32[144,256]{1,0:T(8,128)} async-done(((f32[2304,256]{1,0:T(8,128)}), f32[144,256]{1,0:T(8,128)}) %reduce-scatter.3.cloned.1.call-update) | async-done | bytes 147472 | tf_op jit(solution)/shard_map/reduce_scatter | solution.py:140
  336.7 0.9 fusion.12
  337.6 275.6 %all-reduce.8.cloned.1.call-done = (f32[144,256]{1,0:T(8,128)}, f32[144,128]{1,0:T(8,128)}) async-done(((f32[144,256]{1,0:T(8,128)}, f32[144,128]{1,0:T(8,128)}), (f32[144,256]{1,0:T(8,128)}, f32[144,128]{1,0:T(8,128)})) %all-reduce.8.cloned.1.call-update) | async-done | bytes 221200 | tf_op jit(solution)/shard_map/psum | solution.py:138
  613.2 1.6 broadcast_multiply_fusion
  614.7 1.5 broadcast_multiply_fusion.1
  (102 shorter events, 13.1 us)
Async XLA Ops:
  7.2 21.2 %copy-start.2 = (bf16[1,4,64,256]{3,2,1,0:T(8,128)(2,1)S(1)}, bf16[1,4,64,256]{3,2,1,0:T(8,128)(2,1)}, u32[]{:S(2)}) copy-start(bf16[1,4,64,256]{3,2,1,0:T(8,128)(2,1)} %param.6) | copy-start | bytes 393220
  7.2 213.5 %reduce-scatter.5.cloned.1.call-start = ((), (), s32[]{:S(2)}) async-start(), calls=%async_computation.3 | async-start | bytes 1253376 | tf_op jit(solution)/shard_map/reduce_scatter | solution.py:141
  8.0 20.3 %collective-permute-start.5 = (bf16[1,1,64,256]{3,2,1,0:T(8,128)(2,1)S(1)}, bf16[1,1,64,256]{3,2,1,0:T(8,128)(2,1)S(1)}, u32[]{:S(2)}, u32[]{:S(2)}) collective-permute-start(bf16[1,1,64,256]{3,2,1,0:T(8,128)(2,1)S(1)} %get-tuple-element.51), channel_id=1, source_target_pairs={{4,0},{5,1},{6,2},{7,3},{8,4},{9,5},{10,6},{11,7},{12,8},{13,9},{1... | collective-permute-start | bytes 98312 | tf_op jit(solution)/shard_map/ppermute | solution.py:10
  9.3 19.0 %collective-permute-start.4 = (bf16[1,1,64,256]{3,2,1,0:T(8,128)(2,1)S(1)}, bf16[1,1,64,256]{3,2,1,0:T(8,128)(2,1)S(1)}, u32[]{:S(2)}, u32[]{:S(2)}) collective-permute-start(bf16[1,1,64,256]{3,2,1,0:T(8,128)(2,1)S(1)} %get-tuple-element.50), channel_id=1, source_target_pairs={{0,4},{1,5},{2,6},{3,7},{4,8},{5,9},{6,10},{7,11},{8,12},{9,13},{1... | collective-permute-start | bytes 98312 | tf_op jit(solution)/shard_map/ppermute | solution.py:10
  17.4 15.0 %collective-permute-start.1 = (bf16[4,1,128,128]{3,2,1,0:T(8,128)(2,1)}, bf16[4,1,128,128]{3,2,1,0:T(8,128)(2,1)}, u32[]{:S(2)}, u32[]{:S(2)}) collective-permute-start(bf16[4,1,128,128]{3,2,1,0:T(8,128)(2,1)} %get-tuple-element.27), channel_id=1, source_target_pairs={{1,0},{2,1},{3,2},{4,3},{5,4},{6,5},{7,6},{8,7},{9,8},{10,9},{11,1... | collective-permute-start | bytes 393224 | tf_op jit(solution)/shard_map/ppermute | solution.py:27
  25.2 7.2 %collective-permute-start = (bf16[4,1,128,128]{3,2,1,0:T(8,128)(2,1)}, bf16[4,1,128,128]{3,2,1,0:T(8,128)(2,1)}, u32[]{:S(2)}, u32[]{:S(2)}) collective-permute-start(bf16[4,1,128,128]{3,2,1,0:T(8,128)(2,1)} %get-tuple-element.26), channel_id=1, source_target_pairs={{0,1},{1,2},{2,3},{3,4},{4,5},{5,6},{6,7},{7,8},{8,9},{9,10},{10,1... | collective-permute-start | bytes 393224 | tf_op jit(solution)/shard_map/ppermute | solution.py:26
  28.3 1.3 copy-start.1
  30.5 0.6 copy-start.5
  31.1 1.3 copy-start
  39.2 5.3 copy-start.10
  41.2 6.2 copy-start.7
  41.2 6.2 copy-start.9
  41.2 4.2 collective-permute-start.2
  45.4 6.7 %copy-start.14 = (f32[256]{0:T(256)S(1)}, f32[256]{0:T(256)}, u32[]{:S(2)}) copy-start(f32[256]{0:T(256)} %param.8) | copy-start | bytes 3076
  45.5 6.6 %collective-permute-start.3 = (f32[2,1,64,256]{3,2,0,1:T(8,128)S(1)}, f32[2,1,64,256]{3,2,0,1:T(8,128)S(1)}, u32[]{:S(2)}, u32[]{:S(2)}) collective-permute-start(f32[2,1,64,256]{3,2,0,1:T(8,128)S(1)} %fusion.38), channel_id=1, source_target_pairs={{0,2},{1,3},{2,0},{3,1},{4,6},{5,7},{6,4},{7,5},{8,10},{9,11},{10,... | collective-permute-start | bytes 393224 | tf_op jit(solution)/shard_map/ppermute | solution.py:16
  52.3 4.0 collective-permute-start.8
  56.3 5.0 collective-permute-start.9
  61.4 6.3 %collective-permute-start.11 = (bf16[4,1,64,256]{3,2,0,1:T(8,128)(2,1)S(1)}, bf16[4,1,64,256]{3,2,0,1:T(8,128)(2,1)S(1)}, u32[]{:S(2)}, u32[]{:S(2)}) collective-permute-start(bf16[4,1,64,256]{3,2,0,1:T(8,128)(2,1)S(1)} %bitcast.493), channel_id=1, source_target_pairs={{1,0},{2,1},{3,2},{4,3},{5,4},{6,5},{7,6},{8,7},{9,8},{10,9},{11,1... | collective-permute-start | bytes 393224 | tf_op jit(solution)/shard_map/ppermute | solution.py:27
  64.8 4.1 collective-permute-start.10
  74.5 1.0 copy-start.13
  75.9 1.0 copy-start.12
  77.3 1.0 copy-start.11
  79.1 1.0 copy-start.4
  80.1 0.9 copy-start.6
  80.1 256.6 %reduce-scatter.3.cloned.1.call-start = ((), (), s32[]{:S(2)}) async-start(), calls=%async_computation.2 | async-start | bytes 2506752 | tf_op jit(solution)/shard_map/reduce_scatter | solution.py:140
  81.5 0.9 copy-start.8
  82.9 1.4 copy-start.3
  84.3 528.9 %all-reduce.8.cloned.1.call-start = ((), (), s32[]{:S(2)}) async-start(), calls=%async_computation.4 | async-start | bytes 442368 | tf_op jit(solution)/shard_map/psum | solution.py:138
  86.5 132.1 %collective-permute-start.7 = (bf16[1,1,64,256]{3,2,1,0:T(8,128)(2,1)S(1)}, bf16[1,1,64,256]{3,2,1,0:T(8,128)(2,1)S(1)}, u32[]{:S(2)}, u32[]{:S(2)}) collective-permute-start(bf16[1,1,64,256]{3,2,1,0:T(8,128)(2,1)S(1)} %get-tuple-element.47), channel_id=1, source_target_pairs={{4,0},{5,1},{6,2},{7,3},{8,4},{9,5},{10,6},{11,7},{12,8},{13,9},{1... | collective-permute-start | bytes 98312 | tf_op jit(solution)/shard_map/ppermute | solution.py:10
  87.8 130.8 %collective-permute-start.6 = (bf16[1,1,64,256]{3,2,1,0:T(8,128)(2,1)S(1)}, bf16[1,1,64,256]{3,2,1,0:T(8,128)(2,1)S(1)}, u32[]{:S(2)}, u32[]{:S(2)}) collective-permute-start(bf16[1,1,64,256]{3,2,1,0:T(8,128)(2,1)S(1)} %get-tuple-element.46), channel_id=1, source_target_pairs={{0,4},{1,5},{2,6},{3,7},{4,8},{5,9},{6,10},{7,11},{8,12},{9,13},{1... | collective-permute-start | bytes 98312 | tf_op jit(solution)/shard_map/ppermute | solution.py:10
Sparse Core Ops, SparseCore 0:
  80.2 122.5 reduce-scatter.4
  207.0 129.6 reduce-scatter.2
  339.7 273.4 all-reduce.7
where the time goes:
time: 624 us; the launch traced here: 623 us
  waiting for transfers between devices  403 us (65%)
  blocking collectives  125 us (20%)
  starting transfers between devices  39.4 us (6%)
  local copies, waits for them, and re-layouts  18.2 us (3%)
  between operations  15.2 us (2%)
  matrix products  12.9 us (2%)
  other arithmetic  9.23 us (1%)
    psum x1, waiting for transfers between devices, shards(): lax.psum((flat_first, flat_second, raw_bias), 'rows')  276 us
    reduce_scatter x1, waiting for transfers between devices, shards(): lax.psum_scatter(summed_first, 'dp', scatter_dimension=0, tiled=True)  116 us
    psum x1, blocking collectives, shards(): lax.psum((flat_first, flat_second, raw_bias), 'rows')  75.9 us
    unnamed x1, blocking collectives  49.3 us
    ppermute x4, starting transfers between devices, passed_along(): return lax.ppermute(value, axis, pairs)  13.8 us
  transfers between devices with their start and end apart: 15, of which 8 were waited for; matrix products, arithmetic and copies ran while one was open for 2% of the time, Pallas kernels for 0%

commit v1 on v0

v1 whole, which is shorter than its diff:
```python
import jax
import jax.numpy as jnp
from jax import lax
from jax.experimental import pallas as pl
from jax.experimental.pallas import tpu as pltpu
from jax.sharding import PartitionSpec as P

F32 = jnp.float32
BF16 = jnp.bfloat16
COLS = 64
C1 = 256
C2 = 128
ROWS = 4
PIX = ROWS * COLS
SLICE = 144
PACK = 448
HALF = PACK // 2


def dot(a, b, contract):
    return lax.dot_general(a, b, (contract, ((), ())), preferred_element_type=F32)


NN = ((1,), (0,))
NT = ((1,), (1,))
TN = ((0,), (0,))


def shifted(value, by):
    length = value.shape[0]
    column = lax.broadcasted_iota(jnp.int32, value.shape, 0) % COLS
    rolled = pltpu.roll(value, (-by) % length, 0)
    inside = (column + by >= 0) & (column + by < COLS)
    return jnp.where(inside, rolled, 0.0)


def put(packed, band, tap, value):
    first = tap * C1
    row = 0
    while row < C1:
        d, inner = divmod(first + row, SLICE)
        place = band * SLICE + inner
        count = min(C1 - row, SLICE - inner, HALF - place % HALF)
        half, place = divmod(place, HALF)
        packed[half, d, place : place + count, :] = value[row : row + count, :]
        row += count


def body(
    core, x, above, below, cot, w1, bias, w2,
    grad_x, edge_up, edge_down, keep, send,
    xs, cpad, boxes, ds, packed, sems,
):
    xs[1, 0:COLS, 0:C2] = above[1, 0:COLS, :]
    xs[1, 0:COLS, C2:C1] = above[1, COLS : 2 * COLS, :]
    xs[1, COLS : COLS + PIX, :] = x[...]
    xs[1, COLS + PIX :, 0:C2] = below[1, 0:COLS, :]
    xs[1, COLS + PIX :, C2:C1] = below[1, COLS : 2 * COLS, :]
    wide = xs[1].astype(F32)
    xs[0] = shifted(wide, -1).astype(BF16)
    xs[2] = shifted(wide, 1).astype(BF16)

    preact = jnp.broadcast_to(bias[...], (PIX, C1))
    for p in range(3):
        for q in range(3):
            preact = preact + dot(xs[q, p * COLS : p * COLS + PIX, :], w1[3 * p + q], NN)
    sigma = 1.0 / (1.0 + jnp.exp(-preact))
    act = (preact * sigma).astype(BF16)
    slope = sigma * (1.0 + preact * (1.0 - sigma))

    cpad[0:128, :] = above[0]
    cpad[128 : 128 * 9, :] = cot[...]
    cpad[128 * 9 :, :] = below[0]
    out_row = lax.broadcasted_iota(jnp.int32, (3 * COLS, 256), 0)
    column = lax.broadcasted_iota(jnp.int32, (3 * COLS, 256), 1) % 128
    left = 2 * (out_row % COLS) + 1 - out_row // COLS
    pick = ((column == left) | (column == left + 1)).astype(F32).astype(BF16)
    for h in range(-1, 8):
        sums = dot(pick, cpad[128 * (h + 1) : 128 * (h + 3), :], NN).astype(BF16)
        for p in range(3):
            if (h + p - 1) % 2 == 0 and 0 <= (h + p - 1) // 2 < ROWS:
                i = (h + p - 1) // 2
                for q in range(3):
                    t = 3 * p + q
                    boxes[COLS * i : COLS * (i + 1), C2 * t : C2 * (t + 1)] = sums[
                        COLS * q : COLS * (q + 1), :
                    ]
    grad_act = jnp.zeros((PIX, C1), F32)
    for t in range(9):
        grad_act = grad_act + dot(boxes[:, C2 * t : C2 * (t + 1)], w2[t], NT)
    second = dot(act, boxes[...], TN).astype(BF16)
    for t in range(9):
        put(packed, 2, t, second[:, C2 * t : C2 * (t + 1)])

    delta = (grad_act * slope).astype(BF16)
    wide = delta.astype(F32)
    ds[0] = shifted(wide, 1).astype(BF16)
    ds[1] = delta
    ds[2] = shifted(wide, -1).astype(BF16)

    total = jnp.sum(wide, axis=0, keepdims=True).astype(BF16).astype(F32)
    owner = lax.broadcasted_iota(jnp.int32, (16, C1), 0)
    channel = lax.broadcasted_iota(jnp.int32, (16, C1), 1)
    spread = jnp.where(channel // 16 == owner, jnp.broadcast_to(total, (16, C1)), 0.0)
    source = lax.broadcasted_iota(jnp.int32, (C1, 128), 0)
    lane = lax.broadcasted_iota(jnp.int32, (C1, 128), 1)
    fold = (source % 16 == lane).astype(F32).astype(BF16)
    folded = dot(spread.astype(BF16), fold, NN)
    row = lax.broadcasted_iota(jnp.int32, (16, 16, 128), 1)
    band = jnp.where(row == 0, jnp.broadcast_to(folded[:, None, :], (16, 16, 128)), 0.0)
    packed[1, :, HALF - 16 :, :] = band.astype(BF16)

    for p in range(3):
        lhs = xs[1, p * COLS : p * COLS + PIX, :]
        for q in range(3):
            part = dot(lhs, ds[q], TN).astype(BF16)
            put(packed, 0, 3 * p + q, part[:, 0:C2])
            put(packed, 1, 3 * p + q, part[:, C2:C1])

    mine = core[0]
    keep_copy = pltpu.make_async_copy(packed.at[mine], keep, sems.at[0])
    send_copy = pltpu.make_async_copy(packed.at[1 - mine], send, sems.at[1])
    send_copy.start()
    keep_copy.start()

    parts = []
    for p in range(3):
        part = jnp.zeros((PIX, C1), F32)
        for q in range(3):
            part = part + dot(ds[q], w1[3 * p + q], NT)
        parts.append(part)
    zero = jnp.zeros((COLS, C1), F32)
    rows = [
        sum(
            (parts[p][COLS * (r - p) : COLS * (r - p + 1)] for p in range(3) if 0 <= r - p < ROWS),
            zero,
        )
        for r in range(ROWS + 2)
    ]
    edge_up[...] = rows[0].astype(BF16)
    for r in range(ROWS):
        grad_x[COLS * r : COLS * (r + 1), :] = rows[r + 1].astype(BF16)
    edge_down[...] = rows[ROWS + 1].astype(BF16)
    send_copy.wait()
    keep_copy.wait()


def local_work(core, x, above, below, cot, w1, bias, w2):
    vmem = pl.BlockSpec(memory_space=pltpu.VMEM)
    hbm = pl.BlockSpec(memory_space=pl.ANY)
    return pl.pallas_call(
        body,
        out_shape=(
            jax.ShapeDtypeStruct((PIX, C1), BF16),
            jax.ShapeDtypeStruct((COLS, C1), BF16),
            jax.ShapeDtypeStruct((COLS, C1), BF16),
            jax.ShapeDtypeStruct((16, HALF, 128), BF16),
            jax.ShapeDtypeStruct((16, HALF, 128), BF16),
        ),
        in_specs=[pl.BlockSpec(memory_space=pltpu.SMEM)] + [vmem] * 7,
        out_specs=(vmem, vmem, vmem, hbm, hbm),
        scratch_shapes=[
            pltpu.VMEM((3, PIX + 2 * COLS, C1), BF16),
            pltpu.VMEM((128 * 10, C2), BF16),
            pltpu.VMEM((PIX, 9 * C2), BF16),
            pltpu.VMEM((3, PIX, C1), BF16),
            pltpu.VMEM((2, 16, HALF, 128), BF16),
            pltpu.SemaphoreType.DMA((2,)),
        ],
        compiler_params=pltpu.CompilerParams(vmem_limit_bytes=40 * 2**20),
        cost_estimate=pl.CostEstimate(
            flops=1_600_000_000, bytes_accessed=5_000_000, transcendentals=70_000
        ),
        name="local_work",
    )(core, x, above, below, cot, w1, bias, w2)


FOUR = range(4)


def place(x, z_hi, y, z_lo, core):
    return (x * 4 + z_hi) * 32 + y * 8 + z_lo * 2 + core


PLANE = [
    [place(x, zh, y, zl, c) for x in FOUR for y in FOUR]
    for zh in FOUR
    for zl in FOUR
    for c in range(2)
]
COLUMN = [
    [place(x, zh, y, zl, c) for zh in FOUR for zl in FOUR]
    for x in FOUR
    for y in FOUR
    for c in range(2)
]
SHARE = [[y * 8 + zl * 2 + c for c in range(2) for y in FOUR] for zl in FOUR]
QUADS = [[4 * j + b for b in FOUR] for j in range(8)]


def added(pieces):
    return jnp.sum(pieces.astype(F32), axis=0).astype(BF16)


def shards(cotangent, inputs, w_first, bias_first, w_second):
    rank = lax.axis_index("rows")
    down = [(i, i + 4) for i in range(28)]
    up = [(i + 4, i) for i in range(28)]
    x = inputs[0]

    cot = lax.all_to_all(cotangent, "rows", 0, 0, axis_index_groups=QUADS)
    cot = cot.reshape(8, 128, C2)

    def halo(cot_row, x_row):
        return jnp.stack([cot_row, jnp.concatenate([x_row[:, :C2], x_row[:, C2:]], axis=0)])

    above = lax.ppermute(halo(cot[7], x[3]), "rows", down)
    below = lax.ppermute(halo(cot[0], x[0]), "rows", up)
    core = (rank % 2).astype(jnp.int32).reshape(1)
    grad_x, edge_up, edge_down, keep, send = local_work(
        core,
        x.reshape(PIX, C1),
        above,
        below,
        cot.reshape(8 * 128, C2),
        w_first.reshape(9, C1, C1),
        bias_first.reshape(1, C1),
        w_second.reshape(9, C1, C2),
    )
    received = lax.ppermute(send, "rows", [(i, i ^ 1) for i in range(32)])
    from_above = lax.ppermute(edge_down, "rows", down)
    from_below = lax.ppermute(edge_up, "rows", up)

    pair = (keep.astype(F32) + received.astype(F32)).astype(BF16)
    pair = pair.reshape(4, 4, 4, 56, 128).transpose(0, 2, 1, 3, 4).reshape(16, 4, 56, 128)
    both = ("dp", "rows")
    plane = added(lax.all_to_all(pair, both, 0, 0, axis_index_groups=PLANE))
    spread = jnp.broadcast_to(plane[:, None], (4, 4, 56, 128)).reshape(16, 56, 128)
    piece = added(lax.all_to_all(spread, both, 0, 0, axis_index_groups=COLUMN))
    copies = jnp.broadcast_to(piece[None], (8, 56, 128))
    full = lax.all_to_all(copies, "rows", 0, 0, axis_index_groups=SHARE)
    full = full.reshape(PACK, 128).astype(F32)

    pixels_low = lax.axis_size("dp") * lax.axis_size("rows") * PIX
    scale_low = pixels_low ** (-0.5)
    scale_high = (4 * pixels_low) ** (-0.5)
    grad_first = jnp.concatenate([full[:SLICE], full[SLICE : 2 * SLICE]], axis=1) * scale_low
    grad_second = full[2 * SLICE : 3 * SLICE] * scale_high
    grad_bias = full[3 * SLICE, :16] * scale_low

    zero = jnp.zeros((2, COLS, C1), F32)
    fix = jnp.concatenate([from_above[None].astype(F32), zero, from_below[None].astype(F32)])
    grad_input = (grad_x.reshape(ROWS, COLS, C1).astype(F32) + fix).astype(BF16)
    return grad_input[None], grad_first, grad_second, grad_bias


def solution(mesh):
    in_specs = (P("dp", "rows", None, None), P("dp", "rows", None, None), P(), P(), P())
    out_specs = (P("dp", "rows", None, None), P("dp", None), P("dp", None), P("dp"))
    return jax.shard_map(shards, mesh=mesh, in_specs=in_specs, out_specs=out_specs, check_vma=False)
```

time: 624 us -> 100 us (0.16)
  waiting for transfers between devices: 403 us -> 25.2 us
  blocking collectives: 125 us -> 18.9 us
  local copies, waits for them, and re-layouts: 18.2 us -> 3.42 us
  between operations: 15.2 us -> 0.81 us
  matrix products: 12.9 us -> 0 us
    psum x1 -> x0, waiting for transfers between devices: 276 us -> none  [shards(): lax.psum((flat_first, flat_second, raw_bias), 'rows')]
    reduce_scatter x2 -> x0, waiting for transfers between devices: 116 us -> none  [the longest x1 116 us: shards(): lax.psum_scatter(summed_first, 'dp', scatter_dimension=0, tiled=True)]
    psum x1 -> x0, blocking collectives: 75.9 us -> none  [shards(): lax.psum((flat_first, flat_second, raw_bias), 'rows')]
    unnamed x1 -> x0, blocking collectives: 49.3 us -> none
    all_to_all x0 -> x3, starting transfers between devices: none -> 34 us  [the longest x1 13.5 us: shards(): piece = added(lax.all_to_all(spread, both, 0, 0, axis_index_groups=COLUMN))]
    ppermute x12 -> x5, starting transfers between devices: 39.3 us -> 10.8 us  [the longest x1 4.16 us: shards(): from_above = lax.ppermute(edge_down, 'rows', down)]
    all_to_all x0 -> x1, blocking collectives: none -> 18.9 us  [shards(): plane = added(lax.all_to_all(pair, both, 0, 0, axis_index_groups=PLANE))]
    dot_general x45 -> x0, matrix products: 12.9 us -> none  [the longest x27 7.65 us: conv_apply(): jnp.dot(window, weight[offset_y, offset_x], preferred_element_type=jnp.fl...]
  transfers between devices with their start and end apart: 15 -> 8, of which waited for: 8 -> 6; matrix products, arithmetic and copies ran while one was open for 2% -> 2% of each run, Pallas kernels for 0% -> 0%
where the time goes in v1:
time: 100 us; the launch traced here: 99.7 us
  starting transfers between devices  44.8 us (45%)
  waiting for transfers between devices  25.2 us (25%)
  blocking collectives  18.9 us (19%)
  Pallas kernels  3.46 us (3%)
  local copies, waits for them, and re-layouts  3.42 us (3%)
  other arithmetic  3.06 us (3%)
    all_to_all x1, blocking collectives, shards(): plane = added(lax.all_to_all(pair, both, 0, 0, axis_index_groups=PLANE))  18.9 us
    all_to_all x1, starting transfers between devices, shards(): piece = added(lax.all_to_all(spread, both, 0, 0, axis_index_groups=COLUMN))  13.5 us
    all_to_all x1, starting transfers between devices, shards(): cot = lax.all_to_all(cotangent, 'rows', 0, 0, axis_index_groups=QUADS)  10.4 us
    all_to_all x1, starting transfers between devices, shards(): full = lax.all_to_all(copies, 'rows', 0, 0, axis_index_groups=SHARE)  10.1 us
    ppermute x1, waiting for transfers between devices, shards(): below = lax.ppermute(halo(cot[0], x[0]), 'rows', up)  6.52 us
    ppermute x1, waiting for transfers between devices, shards(): from_below = lax.ppermute(edge_up, 'rows', up)  6.13 us
    all_to_all x1, waiting for transfers between devices, shards(): full = lax.all_to_all(copies, 'rows', 0, 0, axis_index_groups=SHARE)  4.36 us
    all_to_all x1, waiting for transfers between devices, shards(): cot = lax.all_to_all(cotangent, 'rows', 0, 0, axis_index_groups=QUADS)  4.35 us
  transfers between devices with their start and end apart: 8, of which 6 were waited for; matrix products, arithmetic and copies ran while one was open for 2% of the time, Pallas kernels for 0%

profile of v1, /device:TPU:1, one launch (start us, length us, event | category | flops | bytes accessed | tf_op | source)
XLA Modules:
  0.0 99.7 jit_solution(13708524081459622249)
XLA Ops:
  0.6 0.0 copy-start
  0.6 0.0 copy-start.3
  0.7 0.0 copy-start.1
  0.7 10.4 %all-to-all-start = ((bf16[4,2,128,128]{3,2,1,0:T(8,128)(2,1)}), bf16[4,2,128,128]{3,2,1,0:T(8,128)(2,1)S(1)}, u32[]{:S(2)}, u32[]{:S(2)}) async-start(bf16[4,2,128,128]{3,2,1,0:T(8,128)(2,1)} %param.5), calls=%async_computation | async-start | bytes 524288 | tf_op jit(solution)/shard_map/all_to_all | solution.py:211
  11.1 0.8 slice_bitcast_fusion
  11.9 4.4 %all-to-all-done = bf16[4,2,128,128]{3,2,1,0:T(8,128)(2,1)S(1)} async-done(((bf16[4,2,128,128]{3,2,1,0:T(8,128)(2,1)}), bf16[4,2,128,128]{3,2,1,0:T(8,128)(2,1)S(1)}, u32[]{:S(2)}, u32[]{:S(2)}) %all-to-all-start) | async-done | bytes 262176 | tf_op jit(solution)/shard_map/all_to_all | solution.py:211
  16.2 1.3 %collective-permute-start = (bf16[2,128,128]{2,1,0:T(8,128)(2,1)S(1)}, bf16[2,128,128]{2,1,0:T(8,128)(2,1)S(1)}, u32[]{:S(2)}, u32[]{:S(2)}) collective-permute-start(bf16[2,128,128]{2,1,0:T(8,128)(2,1)S(1)} %pad_maximum_fusion), channel_id=1, source_target_pairs={{0,4},{1,5},{2,6},{3,7},{4,8},{5,9},{6,10},{7,11},{8,12},{9,13},{1... | collective-permute-start | bytes 196616 | tf_op jit(solution)/shard_map/ppermute | solution.py:217
  17.6 1.3 %collective-permute-start.1 = (bf16[2,128,128]{2,1,0:T(8,128)(2,1)S(1)}, bf16[2,128,128]{2,1,0:T(8,128)(2,1)S(1)}, u32[]{:S(2)}, u32[]{:S(2)}) collective-permute-start(bf16[2,128,128]{2,1,0:T(8,128)(2,1)S(1)} %pad_maximum_fusion.1), channel_id=1, source_target_pairs={{4,0},{5,1},{6,2},{7,3},{8,4},{9,5},{10,6},{11,7},{12,8},{13,9},{1... | collective-permute-start | bytes 196616 | tf_op jit(solution)/shard_map/ppermute | solution.py:218
  18.9 0.0 collective-permute-done.above
  18.9 6.5 %collective-permute-done.1.below = bf16[2,128,128]{2,1,0:T(8,128)(2,1)S(1)} collective-permute-done((bf16[2,128,128]{2,1,0:T(8,128)(2,1)S(1)}, bf16[2,128,128]{2,1,0:T(8,128)(2,1)S(1)}, u32[]{:S(2)}, u32[]{:S(2)}) %collective-permute-start.1) | collective-permute-done | bytes 65568 | tf_op jit(solution)/shard_map/ppermute | solution.py:218
  25.4 0.0 copy-done
  25.4 0.0 copy-done.3
  25.4 0.0 copy-done.1
  25.4 0.0 copy-start.2
  25.4 1.1 %copy-done.2 = bf16[3,3,256,128]{3,2,1,0:T(8,128)(2,1)S(1)} copy-done((bf16[3,3,256,128]{3,2,1,0:T(8,128)(2,1)S(1)}, bf16[3,3,256,128]{3,2,1,0:T(8,128)(2,1)}, u32[]{:S(2)}) %copy-start.2) | copy-done | bytes 589848
  26.5 3.5 %local_work.1 = (bf16[256,256]{1,0:T(8,128)(2,1)S(1)}, bf16[64,256]{1,0:T(8,128)(2,1)S(1)}, bf16[64,256]{1,0:T(8,128)(2,1)S(1)}, bf16[16,224,128]{2,1,0:T(8,128)(2,1)S(1)}, bf16[16,224,128]{2,1,0:T(8,128)(2,1)S(1)}) custom-call(s32[1]{0:T(128)} %bitcast.core, bf16[256,256]{1,0:T(8,128)(2,1)S(1)} %bitcast.36, ...), custom_call_target="tpu_custom_call" | custom-call | flops 1600000000 | bytes 5000000 | tf_op jit(solution)/shard_map/local_work/pallas_call | solution.py:151
  29.9 2.8 %collective-permute-start.4 = (bf16[16,224,128]{2,1,0:T(8,128)(2,1)S(1)}, bf16[16,224,128]{2,1,0:T(8,128)(2,1)S(1)}, u32[]{:S(2)}, u32[]{:S(2)}) collective-permute-start(bf16[16,224,128]{2,1,0:T(8,128)(2,1)S(1)} %get-tuple-element.13), channel_id=1, source_target_pairs={{0,1},{1,0},{2,3},{3,2},{4,5},{5,4},{6,7},{7,6},{8,9},{9,8},{10,11... | collective-permute-start | bytes 2752520 | tf_op jit(solution)/shard_map/ppermute | solution.py:230
  32.7 2.1 %collective-permute-done.4 = bf16[16,224,128]{2,1,0:T(8,128)(2,1)S(1)} collective-permute-done((bf16[16,224,128]{2,1,0:T(8,128)(2,1)S(1)}, bf16[16,224,128]{2,1,0:T(8,128)(2,1)S(1)}, u32[]{:S(2)}, u32[]{:S(2)}) %collective-permute-start.4) | collective-permute-done | bytes 917536 | tf_op jit(solution)/shard_map/ppermute | solution.py:230
  34.8 0.2 add_convert_fusion
  35.0 0.1 copy.10
  35.1 18.9 %all_to_all.20 = bf16[16,4,56,128]{3,2,1,0:T(8,128)(2,1)S(1)} all-to-all(bf16[16,4,56,128]{3,2,1,0:T(8,128)(2,1)S(1)} %bitcast.40), channel_id=1, replica_groups={{0,8,16,24,128,136,144,152,256,264,272,280,384,392,400,408},{1,9,17,25,..., dimensions={0} | all-to-all | bytes 1835008 | tf_op jit(solution)/shard_map/all_to_all | solution.py:237
  54.0 0.1 reduce_sum.24
  54.1 0.7 broadcast_in_dim.7
  54.9 13.5 %all-to-all-start.2 = ((bf16[16,56,128]{2,1,0:T(8,128)(2,1)}), bf16[16,56,128]{2,1,0:T(8,128)(2,1)S(1)}, u32[]{:S(2)}, u32[]{:S(2)}) async-start(bf16[16,56,128]{2,1,0:T(8,128)(2,1)} %bitcast.17), calls=%async_computation.2 | async-start | bytes 458752 | tf_op jit(solution)/shard_map/all_to_all | solution.py:239
  68.4 4.2 %collective-permute-start.2 = (bf16[64,256]{1,0:T(8,128)(2,1)S(1)}, bf16[64,256]{1,0:T(8,128)(2,1)S(1)}, u32[]{:S(2)}, u32[]{:S(2)}) collective-permute-start(bf16[64,256]{1,0:T(8,128)(2,1)S(1)} %get-tuple-element.10), channel_id=1, source_target_pairs={{0,4},{1,5},{2,6},{3,7},{4,8},{5,9},{6,10},{7,11},{8,12},{9,13},{1... | collective-permute-start | bytes 98312 | tf_op jit(solution)/shard_map/ppermute | solution.py:231
  72.6 0.1 pad.3.clone
  72.6 1.3 %collective-permute-start.3 = (bf16[64,256]{1,0:T(8,128)(2,1)S(1)}, bf16[64,256]{1,0:T(8,128)(2,1)S(1)}, u32[]{:S(2)}, u32[]{:S(2)}) collective-permute-start(bf16[64,256]{1,0:T(8,128)(2,1)S(1)} %get-tuple-element.11), channel_id=1, source_target_pairs={{4,0},{5,1},{6,2},{7,3},{8,4},{9,5},{10,6},{11,7},{12,8},{13,9},{1... | collective-permute-start | bytes 98312 | tf_op jit(solution)/shard_map/ppermute | solution.py:232
  73.9 1.8 %collective-permute-done.2 = bf16[64,256]{1,0:T(8,128)(2,1)S(1)} collective-permute-done((bf16[64,256]{1,0:T(8,128)(2,1)S(1)}, bf16[64,256]{1,0:T(8,128)(2,1)S(1)}, u32[]{:S(2)}, u32[]{:S(2)}) %collective-permute-start.2) | collective-permute-done | bytes 32800 | tf_op jit(solution)/shard_map/ppermute | solution.py:231
  75.7 6.1 %collective-permute-done.3 = bf16[64,256]{1,0:T(8,128)(2,1)S(1)} collective-permute-done((bf16[64,256]{1,0:T(8,128)(2,1)S(1)}, bf16[64,256]{1,0:T(8,128)(2,1)S(1)}, u32[]{:S(2)}, u32[]{:S(2)}) %collective-permute-start.3) | collective-permute-done | bytes 32800 | tf_op jit(solution)/shard_map/ppermute | solution.py:232
  81.9 0.0 all-to-all-done.2
  81.9 0.7 broadcast_in_dim.8
  82.6 10.1 %all-to-all-start.3 = ((bf16[8,56,128]{2,1,0:T(8,128)(2,1)}), bf16[8,56,128]{2,1,0:T(8,128)(2,1)S(1)}, u32[]{:S(2)}, u32[]{:S(2)}) async-start(bf16[8,56,128]{2,1,0:T(8,128)(2,1)} %broadcast_in_dim.8), calls=%async_computation.3 | async-start | bytes 229376 | tf_op jit(solution)/shard_map/all_to_all | solution.py:241
  92.7 0.7 fusion
  93.4 4.4 %all-to-all-done.3 = bf16[8,56,128]{2,1,0:T(8,128)(2,1)S(1)} async-done(((bf16[8,56,128]{2,1,0:T(8,128)(2,1)}), bf16[8,56,128]{2,1,0:T(8,128)(2,1)S(1)}, u32[]{:S(2)}, u32[]{:S(2)}) %all-to-all-start.3) | async-done | bytes 114720 | tf_op jit(solution)/shard_map/all_to_all | solution.py:241
  97.8 0.5 fusion.1
  98.3 0.6 slice_multiply_fusion
  99.0 0.7 maximum_multiply_fusion
  (11 shorter events, 0.1 us)
Async XLA Ops:
  0.6 24.8 %copy-start = (bf16[1,4,64,256]{3,2,1,0:T(8,128)(2,1)S(1)}, bf16[1,4,64,256]{3,2,1,0:T(8,128)(2,1)}, u32[]{:S(2)}) copy-start(bf16[1,4,64,256]{3,2,1,0:T(8,128)(2,1)} %param.6) | copy-start | bytes 393220
  0.6 24.8 %copy-start.3 = (f32[256]{0:T(256)S(1)}, f32[256]{0:T(256)}, u32[]{:S(2)}) copy-start(f32[256]{0:T(256)} %param.8) | copy-start | bytes 3076
  0.7 24.8 %copy-start.1 = (bf16[3,3,256,256]{3,2,1,0:T(8,128)(2,1)S(1)}, bf16[3,3,256,256]{3,2,1,0:T(8,128)(2,1)}, u32[]{:S(2)}) copy-start(bf16[3,3,256,256]{3,2,1,0:T(8,128)(2,1)} %param.7) | copy-start | bytes 3538948
  0.7 15.6 %all-to-all-start = ((bf16[4,2,128,128]{3,2,1,0:T(8,128)(2,1)}), bf16[4,2,128,128]{3,2,1,0:T(8,128)(2,1)S(1)}, u32[]{:S(2)}, u32[]{:S(2)}) async-start(bf16[4,2,128,128]{3,2,1,0:T(8,128)(2,1)} %param.5), calls=%async_computation | async-start | bytes 524288 | tf_op jit(solution)/shard_map/all_to_all | solution.py:211
  16.2 2.6 %collective-permute-start = (bf16[2,128,128]{2,1,0:T(8,128)(2,1)S(1)}, bf16[2,128,128]{2,1,0:T(8,128)(2,1)S(1)}, u32[]{:S(2)}, u32[]{:S(2)}) collective-permute-start(bf16[2,128,128]{2,1,0:T(8,128)(2,1)S(1)} %pad_maximum_fusion), channel_id=1, source_target_pairs={{0,4},{1,5},{2,6},{3,7},{4,8},{5,9},{6,10},{7,11},{8,12},{9,13},{1... | collective-permute-start | bytes 196616 | tf_op jit(solution)/shard_map/ppermute | solution.py:217
  17.6 7.8 %collective-permute-start.1 = (bf16[2,128,128]{2,1,0:T(8,128)(2,1)S(1)}, bf16[2,128,128]{2,1,0:T(8,128)(2,1)S(1)}, u32[]{:S(2)}, u32[]{:S(2)}) collective-permute-start(bf16[2,128,128]{2,1,0:T(8,128)(2,1)S(1)} %pad_maximum_fusion.1), channel_id=1, source_target_pairs={{4,0},{5,1},{6,2},{7,3},{8,4},{9,5},{10,6},{11,7},{12,8},{13,9},{1... | collective-permute-start | bytes 196616 | tf_op jit(solution)/shard_map/ppermute | solution.py:218
  25.4 1.1 %copy-start.2 = (bf16[3,3,256,128]{3,2,1,0:T(8,128)(2,1)S(1)}, bf16[3,3,256,128]{3,2,1,0:T(8,128)(2,1)}, u32[]{:S(2)}) copy-start(bf16[3,3,256,128]{3,2,1,0:T(8,128)(2,1)} %param.9) | copy-start | bytes 1769476
  29.9 4.9 %collective-permute-start.4 = (bf16[16,224,128]{2,1,0:T(8,128)(2,1)S(1)}, bf16[16,224,128]{2,1,0:T(8,128)(2,1)S(1)}, u32[]{:S(2)}, u32[]{:S(2)}) collective-permute-start(bf16[16,224,128]{2,1,0:T(8,128)(2,1)S(1)} %get-tuple-element.13), channel_id=1, source_target_pairs={{0,1},{1,0},{2,3},{3,2},{4,5},{5,4},{6,7},{7,6},{8,9},{9,8},{10,11... | collective-permute-start | bytes 2752520 | tf_op jit(solution)/shard_map/ppermute | solution.py:230
  54.9 27.0 %all-to-all-start.2 = ((bf16[16,56,128]{2,1,0:T(8,128)(2,1)}), bf16[16,56,128]{2,1,0:T(8,128)(2,1)S(1)}, u32[]{:S(2)}, u32[]{:S(2)}) async-start(bf16[16,56,128]{2,1,0:T(8,128)(2,1)} %bitcast.17), calls=%async_computation.2 | async-start | bytes 458752 | tf_op jit(solution)/shard_map/all_to_all | solution.py:239
  68.4 7.3 %collective-permute-start.2 = (bf16[64,256]{1,0:T(8,128)(2,1)S(1)}, bf16[64,256]{1,0:T(8,128)(2,1)S(1)}, u32[]{:S(2)}, u32[]{:S(2)}) collective-permute-start(bf16[64,256]{1,0:T(8,128)(2,1)S(1)} %get-tuple-element.10), channel_id=1, source_target_pairs={{0,4},{1,5},{2,6},{3,7},{4,8},{5,9},{6,10},{7,11},{8,12},{9,13},{1... | collective-permute-start | bytes 98312 | tf_op jit(solution)/shard_map/ppermute | solution.py:231
  72.6 9.2 %collective-permute-start.3 = (bf16[64,256]{1,0:T(8,128)(2,1)S(1)}, bf16[64,256]{1,0:T(8,128)(2,1)S(1)}, u32[]{:S(2)}, u32[]{:S(2)}) collective-permute-start(bf16[64,256]{1,0:T(8,128)(2,1)S(1)} %get-tuple-element.11), channel_id=1, source_target_pairs={{4,0},{5,1},{6,2},{7,3},{8,4},{9,5},{10,6},{11,7},{12,8},{13,9},{1... | collective-permute-start | bytes 98312 | tf_op jit(solution)/shard_map/ppermute | solution.py:232
  82.6 15.2 %all-to-all-start.3 = ((bf16[8,56,128]{2,1,0:T(8,128)(2,1)}), bf16[8,56,128]{2,1,0:T(8,128)(2,1)S(1)}, u32[]{:S(2)}, u32[]{:S(2)}) async-start(bf16[8,56,128]{2,1,0:T(8,128)(2,1)} %broadcast_in_dim.8), calls=%async_computation.3 | async-start | bytes 229376 | tf_op jit(solution)/shard_map/all_to_all | solution.py:241

commit v2 on v1

v2 whole, which is shorter than its diff:
```python
import jax
import jax.numpy as jnp
from jax import lax
from jax.experimental import pallas as pl
from jax.experimental.pallas import tpu as pltpu
from jax.sharding import PartitionSpec as P

F32 = jnp.float32
BF16 = jnp.bfloat16
COLS = 64
C1 = 256
C2 = 128
ROWS = 4
PIX = ROWS * COLS
SLICE = 144
PIECE = 32
PIECES = 16
PACK = PIECE * PIECES


def dot(a, b, contract):
    return lax.dot_general(a, b, (contract, ((), ())), preferred_element_type=F32)


NN = ((1,), (0,))
NT = ((1,), (1,))
TN = ((0,), (0,))


def shifted(value, by):
    length = value.shape[0]
    column = lax.broadcasted_iota(jnp.int32, value.shape, 0) % COLS
    rolled = pltpu.roll(value, (-by) % length, 0)
    inside = (column + by >= 0) & (column + by < COLS)
    return jnp.where(inside, rolled, 0.0)


def spot(d, row):
    piece, inner = divmod(row, PIECE)
    half, rest = divmod(piece, PIECES // 2)
    x, z_hi = divmod(d, 4)
    return half, x * (PIECES // 2) + rest, z_hi, inner


def put(packed, band, tap, value):
    row = 0
    while row < C1:
        d, inner = divmod(tap * C1 + row, SLICE)
        half, chunk, z_hi, at = spot(d, band * SLICE + inner)
        count = min(C1 - row, SLICE - inner, PIECE - at)
        packed[half, chunk, z_hi, at : at + count, :] = value[row : row + count, :]
        row += count


def pick_columns():
    out_row = lax.broadcasted_iota(jnp.int32, (3 * COLS, 256), 0)
    column = lax.broadcasted_iota(jnp.int32, (3 * COLS, 256), 1) % 128
    left = 2 * (out_row % COLS) + 1 - out_row // COLS
    return ((column == left) | (column == left + 1)).astype(F32).astype(BF16)


def silu_parts(preact):
    sigma = 1.0 / (1.0 + jnp.exp(-preact))
    return preact * sigma, sigma * (1.0 + preact * (1.0 - sigma))


def main_body(
    core, above, below, cot, x_hbm, w1_hbm, bias_hbm, w2_hbm,
    delta_out, delta_first, delta_last, keep, send,
    xs, cpad, boxes, ds, packed, x, w1, bias, w2, sems,
):
    w2_copy = pltpu.make_async_copy(w2_hbm, w2, sems.at[2])
    w2_copy.start()
    x_copy = pltpu.make_async_copy(x_hbm, x, sems.at[3])
    x_copy.start()
    bias_copy = pltpu.make_async_copy(bias_hbm, bias, sems.at[4])
    bias_copy.start()
    w1_copy = pltpu.make_async_copy(w1_hbm, w1, sems.at[5])
    w1_copy.start()

    cpad[0:128, :] = above[0]
    cpad[128 : 128 * 9, :] = cot[...]
    cpad[128 * 9 :, :] = below[0]
    pick = pick_columns()
    for h in range(-1, 8):
        sums = dot(pick, cpad[128 * (h + 1) : 128 * (h + 3), :], NN).astype(BF16)
        for p in range(3):
            if (h + p - 1) % 2 == 0 and 0 <= (h + p - 1) // 2 < ROWS:
                i = (h + p - 1) // 2
                for q in range(3):
                    t = 3 * p + q
                    boxes[COLS * i : COLS * (i + 1), C2 * t : C2 * (t + 1)] = sums[
                        COLS * q : COLS * (q + 1), :
                    ]
    w2_copy.wait()
    grad_act = jnp.zeros((PIX, C1), F32)
    for t in range(9):
        grad_act = grad_act + dot(boxes[:, C2 * t : C2 * (t + 1)], w2[t], NT)

    x_copy.wait()
    xs[1, 0:COLS, 0:C2] = above[1, 0:COLS, :]
    xs[1, 0:COLS, C2:C1] = above[1, COLS : 2 * COLS, :]
    xs[1, COLS : COLS + PIX, :] = x[...]
    xs[1, COLS + PIX :, 0:C2] = below[1, 0:COLS, :]
    xs[1, COLS + PIX :, C2:C1] = below[1, COLS : 2 * COLS, :]
    wide = xs[1].astype(F32)
    xs[0] = shifted(wide, -1).astype(BF16)
    xs[2] = shifted(wide, 1).astype(BF16)
    bias_copy.wait()
    w1_copy.wait()
    preact = jnp.broadcast_to(bias[...], (PIX, C1))
    for p in range(3):
        for q in range(3):
            preact = preact + dot(xs[q, p * COLS : p * COLS + PIX, :], w1[3 * p + q], NN)
    act, slope = silu_parts(preact)
    second = dot(act.astype(BF16), boxes[...], TN).astype(BF16)
    for t in range(9):
        put(packed, 2, t, second[:, C2 * t : C2 * (t + 1)])

    delta = (grad_act * slope).astype(BF16)
    delta_out[...] = delta
    delta_first[...] = delta[0:COLS]
    delta_last[...] = delta[PIX - COLS : PIX]
    wide = delta.astype(F32)
    ds[0] = shifted(wide, 1).astype(BF16)
    ds[1] = delta
    ds[2] = shifted(wide, -1).astype(BF16)

    total = jnp.sum(wide, axis=0, keepdims=True).astype(BF16).astype(F32)
    owner = lax.broadcasted_iota(jnp.int32, (16, C1), 0)
    channel = lax.broadcasted_iota(jnp.int32, (16, C1), 1)
    spread = jnp.where(channel // 16 == owner, jnp.broadcast_to(total, (16, C1)), 0.0)
    source = lax.broadcasted_iota(jnp.int32, (C1, 128), 0)
    lane = lax.broadcasted_iota(jnp.int32, (C1, 128), 1)
    fold = (source % 16 == lane).astype(F32).astype(BF16)
    folded = dot(spread.astype(BF16), fold, NN)
    row = lax.broadcasted_iota(jnp.int32, (16, 16, 128), 1)
    band = jnp.where(row == 0, jnp.broadcast_to(folded[:, None, :], (16, 16, 128)), 0.0)
    band = band.astype(BF16)
    empty = jnp.zeros((16, 128), BF16)
    for d in range(16):
        for row in range(3 * SLICE, PACK, 16):
            half, chunk, z_hi, at = spot(d, row)
            packed[half, chunk, z_hi, at : at + 16, :] = band[d] if row == 3 * SLICE else empty

    for p in range(3):
        lhs = xs[1, p * COLS : p * COLS + PIX, :]
        for q in range(3):
            part = dot(lhs, ds[q], TN).astype(BF16)
            put(packed, 0, 3 * p + q, part[:, 0:C2])
            put(packed, 1, 3 * p + q, part[:, C2:C1])

    mine = core[0]
    send_copy = pltpu.make_async_copy(packed.at[1 - mine], send, sems.at[1])
    send_copy.start()
    keep_copy = pltpu.make_async_copy(packed.at[mine], keep, sems.at[0])
    keep_copy.start()
    send_copy.wait()
    keep_copy.wait()


VMEM = pl.BlockSpec(memory_space=pltpu.VMEM)
HBM = pl.BlockSpec(memory_space=pltpu.HBM)
SMEM = pl.BlockSpec(memory_space=pltpu.SMEM)
ANYWHERE = pl.BlockSpec(memory_space=pl.ANY)


def main_work(core, above, below, cot, x, w1, bias, w2):
    parts = (2 * PIECES, 4, PIECE, 128)
    return pl.pallas_call(
        main_body,
        out_shape=(
            jax.ShapeDtypeStruct((PIX, C1), BF16),
            jax.ShapeDtypeStruct((COLS, C1), BF16),
            jax.ShapeDtypeStruct((COLS, C1), BF16),
            jax.ShapeDtypeStruct(parts, BF16),
            jax.ShapeDtypeStruct(parts, BF16),
        ),
        in_specs=[SMEM] + [VMEM] * 3 + [HBM] * 4,
        out_specs=(VMEM, VMEM, VMEM, ANYWHERE, ANYWHERE),
        scratch_shapes=[
            pltpu.VMEM((3, PIX + 2 * COLS, C1), BF16),
            pltpu.VMEM((128 * 10, C2), BF16),
            pltpu.VMEM((PIX, 9 * C2), BF16),
            pltpu.VMEM((3, PIX, C1), BF16),
            pltpu.VMEM((2,) + parts, BF16),
            pltpu.VMEM((PIX, C1), BF16),
            pltpu.VMEM((9, C1, C1), BF16),
            pltpu.VMEM((1, C1), F32),
            pltpu.VMEM((9, C1, C2), BF16),
            pltpu.SemaphoreType.DMA((6,)),
        ],
        compiler_params=pltpu.CompilerParams(vmem_limit_bytes=12 * 2**20),
        cost_estimate=pl.CostEstimate(
            flops=1_100_000_000, bytes_accessed=5_000_000, transcendentals=70_000
        ),
        name="main_work",
    )(core, above, below, cot, x, w1, bias, w2)


def input_body(delta, above, below, w1_hbm, grad_x, ext, ds, w1, sem):
    w1_copy = pltpu.make_async_copy(w1_hbm, w1, sem)
    w1_copy.start()
    ext[0:COLS, :] = above[...]
    ext[COLS : COLS + PIX, :] = delta[...]
    ext[COLS + PIX :, :] = below[...]
    wide = ext[...].astype(F32)
    ds[0] = shifted(wide, 1).astype(BF16)
    ds[1] = ext[...]
    ds[2] = shifted(wide, -1).astype(BF16)
    w1_copy.wait()
    total = jnp.zeros((PIX, C1), F32)
    for p in range(3):
        for q in range(3):
            at = COLS * (2 - p)
            total = total + dot(ds[q, at : at + PIX, :], w1[3 * p + q], NT)
    grad_x[...] = total.astype(BF16)


def input_work(delta, above, below, w1):
    return pl.pallas_call(
        input_body,
        out_shape=jax.ShapeDtypeStruct((PIX, C1), BF16),
        in_specs=[VMEM] * 3 + [HBM],
        out_specs=VMEM,
        scratch_shapes=[
            pltpu.VMEM((PIX + 2 * COLS, C1), BF16),
            pltpu.VMEM((3, PIX + 2 * COLS, C1), BF16),
            pltpu.VMEM((9, C1, C1), BF16),
            pltpu.SemaphoreType.DMA,
        ],
        compiler_params=pltpu.CompilerParams(vmem_limit_bytes=12 * 2**20),
        cost_estimate=pl.CostEstimate(
            flops=300_000_000, bytes_accessed=2_000_000, transcendentals=0
        ),
        name="input_work",
    )(delta, above, below, w1)


def unpack(scale_low, scale_high, full, first, second, bias):
    def rows(start):
        return full[start : start + SLICE, :].astype(F32)

    first[:, 0:C2] = rows(0) * scale_low
    first[:, C2:C1] = rows(SLICE) * scale_low
    second[...] = rows(2 * SLICE) * scale_high
    bias[...] = full[3 * SLICE : 3 * SLICE + 16, :].astype(F32)[0:1, 0:16] * scale_low


def results(full, scale_low, scale_high):
    return pl.pallas_call(
        lambda *refs: unpack(scale_low, scale_high, *refs),
        out_shape=(
            jax.ShapeDtypeStruct((SLICE, C1), F32),
            jax.ShapeDtypeStruct((SLICE, C2), F32),
            jax.ShapeDtypeStruct((1, 16), F32),
        ),
        in_specs=[pl.BlockSpec(memory_space=pltpu.VMEM)],
        out_specs=(pl.BlockSpec(memory_space=pltpu.VMEM),) * 3,
        name="unpack",
    )(full)


FOUR = range(4)
TWO = range(2)


def place(x, z_hi, y, zb, za, core):
    return (x * 4 + z_hi) * 32 + y * 8 + zb * 4 + za * 2 + core


BLOCK = [
    [place(x, zh, y, zb, za, c) for x in FOUR for y in FOUR for za in TWO]
    for zh in FOUR
    for zb in TWO
    for c in TWO
]
COLUMN = [
    [place(x, zh, y, zb, za, c) for zh in FOUR for zb in TWO]
    for x in FOUR
    for y in FOUR
    for za in TWO
    for c in TWO
]
SHARE = [[place(0, 0, y, zb, za, c) for c in TWO for y in FOUR for za in TWO] for zb in TWO]
QUADS = [[4 * j + b for b in FOUR] for j in range(8)]


def added(pieces):
    return jnp.sum(pieces.astype(F32), axis=0).astype(BF16)


def shards(cotangent, inputs, w_first, bias_first, w_second):
    rank = lax.axis_index("rows")
    down = [(i, i + 4) for i in range(28)]
    up = [(i + 4, i) for i in range(28)]
    both = ("dp", "rows")
    x = inputs[0]

    cot = lax.all_to_all(cotangent, "rows", 0, 0, axis_index_groups=QUADS)
    cot = cot.reshape(8, 128, C2)

    def halo(cot_rows, x_row):
        row = jnp.concatenate([x_row[:, :C2], x_row[:, C2:]], axis=0)
        return jnp.concatenate([cot_rows, row[None]])

    above = lax.ppermute(halo(cot[7:8], x[3]), "rows", down)
    below = lax.ppermute(halo(cot[0:1], x[0]), "rows", up)
    core = (rank % 2).astype(jnp.int32).reshape(1)
    x_flat, w1, bias, w2 = (
        pltpu.with_memory_space_constraint(value, pltpu.HBM)
        for value in (
            x.reshape(PIX, C1),
            w_first.reshape(9, C1, C1),
            bias_first.reshape(1, C1),
            w_second.reshape(9, C1, C2),
        )
    )
    cot = cot.reshape(8 * 128, C2)
    delta, delta_first, delta_last, keep, send = main_work(
        core, above, below, cot, x_flat, w1, bias, w2
    )
    received = lax.ppermute(send, "rows", [(i, i ^ 1) for i in range(32)])
    from_above = lax.ppermute(delta_last, "rows", down)
    from_below = lax.ppermute(delta_first, "rows", up)

    pair = (keep.astype(F32) + received.astype(F32)).astype(BF16)
    block = lax.all_to_all(pair, both, 0, 0, axis_index_groups=BLOCK)
    block, from_above, from_below = lax.optimization_barrier((block, from_above, from_below))
    block = added(block)
    grad_x = input_work(delta, from_above, from_below, w1)
    spread = jnp.broadcast_to(block[:, None], (4, 2, PIECE, 128)).reshape(8, PIECE, 128)
    column = lax.all_to_all(spread, both, 0, 0, axis_index_groups=COLUMN)
    column, grad_x = lax.optimization_barrier((column, grad_x))
    piece = added(column)
    copies = jnp.broadcast_to(piece[None], (PIECES, PIECE, 128))
    full = lax.all_to_all(copies, "rows", 0, 0, axis_index_groups=SHARE)

    pixels_low = lax.axis_size("dp") * lax.axis_size("rows") * PIX
    scale_low = pixels_low ** (-0.5)
    scale_high = (4 * pixels_low) ** (-0.5)
    grad_first, grad_second, grad_bias = results(full.reshape(PACK, 128), scale_low, scale_high)
    grad_input = grad_x.reshape(1, ROWS, COLS, C1)
    return grad_input, grad_first, grad_second, grad_bias.reshape(16)


def solution(mesh):
    in_specs = (P("dp", "rows", None, None), P("dp", "rows", None, None), P(), P(), P())
    out_specs = (P("dp", "rows", None, None), P("dp", None), P("dp", None), P("dp"))
    return jax.shard_map(shards, mesh=mesh, in_specs=in_specs, out_specs=out_specs, check_vma=False)
```

time: 100 us -> 99.9 us (level)
  waiting for transfers between devices: 25.2 us -> 36.9 us
  blocking collectives: 18.9 us -> 12.2 us
  starting transfers between devices: 44.8 us -> 38.6 us
  Pallas kernels: 3.46 us -> 7.77 us
  local copies, waits for them, and re-layouts: 3.42 us -> 1.45 us
  other arithmetic: 3.06 us -> 1.56 us
    all_to_all x2, waiting for transfers between devices: 4.36 us -> 17.2 us  [the longest x1 9.7 us: shards(): column = lax.all_to_all(spread, both, 0, 0, axis_index_groups=COLUMN)]
    all_to_all x1, blocking collectives: 18.9 us -> 12.2 us  [shards(): full = lax.all_to_all(copies, 'rows', 0, 0, axis_index_groups=SHARE)]
    all_to_all x2, starting transfers between devices: 23.6 us -> 18 us  [the longest x1 12.7 us: shards(): column = lax.all_to_all(spread, both, 0, 0, axis_index_groups=COLUMN)]
    pallas_call x1 -> x3, Pallas kernels: 3.46 us -> 7.77 us  [the longest x1 3.73 us: main_work(): pl.pallas_call(main_body, out_shape=(jax.ShapeDtypeStruct((PIX, C1), BF16...]
    mul x3 -> x0, other arithmetic: 1.84 us -> none  [the longest x1 0.68 us: shards(): jnp.concatenate([full[:SLICE], full[SLICE:2 * SLICE]], axis=1) * scale_low]
    ppermute x4, waiting for transfers between devices: 14.4 us -> 13.1 us  [the longest x1 6.6 us: shards(): from_above = lax.ppermute(delta_last, 'rows', down)]
    convert_element_type x1, other arithmetic: 0.24 us -> 1.36 us  [shards(): pair = (keep.astype(F32) + received.astype(F32)).astype(BF16)]
    unnamed x8 -> x0, local copies, waits for them, and re-layouts: 1.07 us -> none
  transfers between devices with their start and end apart: 8 -> 8, of which waited for: 6 -> 6; matrix products, arithmetic and copies ran while one was open for 2% -> 1% of each run, Pallas kernels for 0% -> 2%
where the time goes in v2:
time: 99.9 us; the launch traced here: 99.2 us
  starting transfers between devices  38.6 us (39%)
  waiting for transfers between devices  36.9 us (37%)
  blocking collectives  12.2 us (12%)
  Pallas kernels  7.77 us (8%)
  other arithmetic  1.56 us (2%)
  local copies, waits for them, and re-layouts  1.45 us (1%)
    all_to_all x1, starting transfers between devices, shards(): column = lax.all_to_all(spread, both, 0, 0, axis_index_groups=COLUMN)  12.7 us
    all_to_all x1, blocking collectives, shards(): full = lax.all_to_all(copies, 'rows', 0, 0, axis_index_groups=SHARE)  12.2 us
    all_to_all x1, starting transfers between devices, shards(): cot = lax.all_to_all(cotangent, 'rows', 0, 0, axis_index_groups=QUADS)  10.3 us
    all_to_all x1, waiting for transfers between devices, shards(): column = lax.all_to_all(spread, both, 0, 0, axis_index_groups=COLUMN)  9.7 us
    all_to_all x1, waiting for transfers between devices, shards(): block = lax.all_to_all(pair, both, 0, 0, axis_index_groups=BLOCK)  7.48 us
    ppermute x1, waiting for transfers between devices, shards(): from_above = lax.ppermute(delta_last, 'rows', down)  6.6 us
    ppermute x1, waiting for transfers between devices, shards(): below = lax.ppermute(halo(cot[0:1], x[0]), 'rows', up)  6.52 us
    all_to_all x1, starting transfers between devices, shards(): block = lax.all_to_all(pair, both, 0, 0, axis_index_groups=BLOCK)  5.27 us
  transfers between devices with their start and end apart: 8, of which 6 were waited for; matrix products, arithmetic and copies ran while one was open for 1% of the time, Pallas kernels for 2%

profile of v2, /device:TPU:1, one launch (start us, length us, event | category | flops | bytes accessed | tf_op | source)
XLA Modules:
  0.0 99.2 jit_solution(1631175938191397307)
XLA Ops:
  0.6 10.3 %all-to-all-start = ((bf16[4,2,128,128]{3,2,1,0:T(8,128)(2,1)}), bf16[4,2,128,128]{3,2,1,0:T(8,128)(2,1)S(1)}, u32[]{:S(2)}, u32[]{:S(2)}) async-start(bf16[4,2,128,128]{3,2,1,0:T(8,128)(2,1)} %param.5), calls=%async_computation | async-start | bytes 524288 | tf_op jit(solution)/shard_map/all_to_all | solution.py:300
  10.9 0.8 slice_bitcast_fusion
  11.7 4.4 %all-to-all-done = bf16[4,2,128,128]{3,2,1,0:T(8,128)(2,1)S(1)} async-done(((bf16[4,2,128,128]{3,2,1,0:T(8,128)(2,1)}), bf16[4,2,128,128]{3,2,1,0:T(8,128)(2,1)S(1)}, u32[]{:S(2)}, u32[]{:S(2)}) %all-to-all-start) | async-done | bytes 262176 | tf_op jit(solution)/shard_map/all_to_all | solution.py:300
  16.1 1.3 %collective-permute-start = (bf16[2,128,128]{2,1,0:T(8,128)(2,1)S(1)}, bf16[2,128,128]{2,1,0:T(8,128)(2,1)S(1)}, u32[]{:S(2)}, u32[]{:S(2)}) collective-permute-start(bf16[2,128,128]{2,1,0:T(8,128)(2,1)S(1)} %pad_maximum_fusion), channel_id=1, source_target_pairs={{0,4},{1,5},{2,6},{3,7},{4,8},{5,9},{6,10},{7,11},{8,12},{9,13},{1... | collective-permute-start | bytes 196616 | tf_op jit(solution)/shard_map/ppermute | solution.py:307
  17.4 1.3 %collective-permute-start.1 = (bf16[2,128,128]{2,1,0:T(8,128)(2,1)S(1)}, bf16[2,128,128]{2,1,0:T(8,128)(2,1)S(1)}, u32[]{:S(2)}, u32[]{:S(2)}) collective-permute-start(bf16[2,128,128]{2,1,0:T(8,128)(2,1)S(1)} %pad_maximum_fusion.1), channel_id=1, source_target_pairs={{4,0},{5,1},{6,2},{7,3},{8,4},{9,5},{10,6},{11,7},{12,8},{13,9},{1... | collective-permute-start | bytes 196616 | tf_op jit(solution)/shard_map/ppermute | solution.py:308
  18.7 0.0 collective-permute-done.above
  18.7 6.5 %collective-permute-done.1.below = bf16[2,128,128]{2,1,0:T(8,128)(2,1)S(1)} collective-permute-done((bf16[2,128,128]{2,1,0:T(8,128)(2,1)S(1)}, bf16[2,128,128]{2,1,0:T(8,128)(2,1)S(1)}, u32[]{:S(2)}, u32[]{:S(2)}) %collective-permute-start.1) | collective-permute-done | bytes 65568 | tf_op jit(solution)/shard_map/ppermute | solution.py:308
  25.2 3.7 %main_work.1 = (bf16[256,256]{1,0:T(8,128)(2,1)S(1)}, bf16[64,256]{1,0:T(8,128)(2,1)S(1)}, bf16[64,256]{1,0:T(8,128)(2,1)S(1)}, bf16[32,4,32,128]{3,2,1,0:T(8,128)(2,1)S(1)}, bf16[32,4,32,128]{3,2,1,0:T(8,128)(2,1)S(1)}) custom-call(s32[1]{0:T(128)} %bitcast.core, bf16[2,128,128]{2,1,0:T(8,128)(2,1)S(1)} %collective-permute-done.above, ...), custom_call_target="tpu_custom_call" | custom-call | flops 1100000000 | bytes 5000000 | tf_op jit(solution)/shard_map/main_work/pallas_call | solution.py:170
  29.0 2.8 %collective-permute-start.2 = (bf16[32,4,32,128]{3,2,1,0:T(8,128)(2,1)S(1)}, bf16[32,4,32,128]{3,2,1,0:T(8,128)(2,1)S(1)}, u32[]{:S(2)}, u32[]{:S(2)}) collective-permute-start(bf16[32,4,32,128]{3,2,1,0:T(8,128)(2,1)S(1)} %get-tuple-element.18), channel_id=1, source_target_pairs={{0,1},{1,0},{2,3},{3,2},{4,5},{5,4},{6,7},{7,6},{8,9},{9,8},{10,11... | collective-permute-start | bytes 3145736 | tf_op jit(solution)/shard_map/ppermute | solution.py:323
  31.8 2.3 %collective-permute-done.2 = bf16[32,4,32,128]{3,2,1,0:T(8,128)(2,1)S(1)} collective-permute-done((bf16[32,4,32,128]{3,2,1,0:T(8,128)(2,1)S(1)}, bf16[32,4,32,128]{3,2,1,0:T(8,128)(2,1)S(1)}, u32[]{:S(2)}, u32[]{:S(2)}) %collective-permute-start.2) | collective-permute-done | bytes 1048608 | tf_op jit(solution)/shard_map/ppermute | solution.py:323
  34.0 1.4 %add_convert_fusion = bf16[32,4,32,128]{3,2,1,0:T(8,128)(2,1)} fusion(bf16[32,4,32,128]{3,2,1,0:T(8,128)(2,1)S(1)} %collective-permute-done.2, bf16[32,4,32,128]{3,2,1,0:T(8,128)(2,1)S(1)} %get-tuple-element.17), kind=kLoop, calls=%fused_computation | loop fusion | flops 2097152 | bytes 3145728 | tf_op jit(solution)/shard_map/convert_element_type | solution.py:327
  35.4 5.3 %all-to-all-start.1 = ((bf16[32,4,32,128]{3,2,1,0:T(8,128)(2,1)}), bf16[32,4,32,128]{3,2,1,0:T(8,128)(2,1)S(1)}, u32[]{:S(2)}, u32[]{:S(2)}) async-start(bf16[32,4,32,128]{3,2,1,0:T(8,128)(2,1)} %add_convert_fusion), calls=%async_computation.1 | async-start | bytes 2097152 | tf_op jit(solution)/shard_map/all_to_all | solution.py:328
  40.7 3.7 %collective-permute-start.3 = (bf16[64,256]{1,0:T(8,128)(2,1)S(1)}, bf16[64,256]{1,0:T(8,128)(2,1)S(1)}, u32[]{:S(2)}, u32[]{:S(2)}) collective-permute-start(bf16[64,256]{1,0:T(8,128)(2,1)S(1)} %get-tuple-element.19), channel_id=1, source_target_pairs={{0,4},{1,5},{2,6},{3,7},{4,8},{5,9},{6,10},{7,11},{8,12},{9,13},{1... | collective-permute-start | bytes 98312 | tf_op jit(solution)/shard_map/ppermute | solution.py:324
  44.4 1.3 %collective-permute-start.4 = (bf16[64,256]{1,0:T(8,128)(2,1)S(1)}, bf16[64,256]{1,0:T(8,128)(2,1)S(1)}, u32[]{:S(2)}, u32[]{:S(2)}) collective-permute-start(bf16[64,256]{1,0:T(8,128)(2,1)S(1)} %get-tuple-element.20), channel_id=1, source_target_pairs={{4,0},{5,1},{6,2},{7,3},{8,4},{9,5},{10,6},{11,7},{12,8},{13,9},{1... | collective-permute-start | bytes 98312 | tf_op jit(solution)/shard_map/ppermute | solution.py:325
  45.7 6.6 %collective-permute-done.3.above = bf16[64,256]{1,0:T(8,128)(2,1)S(1)} collective-permute-done((bf16[64,256]{1,0:T(8,128)(2,1)S(1)}, bf16[64,256]{1,0:T(8,128)(2,1)S(1)}, u32[]{:S(2)}, u32[]{:S(2)}) %collective-permute-start.3) | collective-permute-done | bytes 32800 | tf_op jit(solution)/shard_map/ppermute | solution.py:324
  52.3 0.0 collective-permute-done.4.below
  52.3 7.5 %all-to-all-done.1 = bf16[32,4,32,128]{3,2,1,0:T(8,128)(2,1)S(1)} async-done(((bf16[32,4,32,128]{3,2,1,0:T(8,128)(2,1)}), bf16[32,4,32,128]{3,2,1,0:T(8,128)(2,1)S(1)}, u32[]{:S(2)}, u32[]{:S(2)}) %all-to-all-start.1) | async-done | bytes 1048608 | tf_op jit(solution)/shard_map/all_to_all | solution.py:328
  59.7 0.2 reduce_sum.24
  59.9 0.6 broadcast_in_dim.20
  60.5 12.7 %all-to-all-start.2 = ((bf16[8,32,128]{2,1,0:T(8,128)(2,1)}), bf16[8,32,128]{2,1,0:T(8,128)(2,1)S(1)}, u32[]{:S(2)}, u32[]{:S(2)}) async-start(bf16[8,32,128]{2,1,0:T(8,128)(2,1)} %bitcast.11), calls=%async_computation.2 | async-start | bytes 131072 | tf_op jit(solution)/shard_map/all_to_all | solution.py:333
  73.2 2.4 %input_work.1 = bf16[256,256]{1,0:T(8,128)(2,1)} custom-call(bf16[256,256]{1,0:T(8,128)(2,1)S(1)} %get-tuple-element.22.delta, bf16[64,256]{1,0:T(8,128)(2,1)S(1)} %collective-permute-done.3.above, bf16[64,256]{1,0:T(8,128)(2,1)S(1)} %collective-permute-done.4.below, bf16[9,256,256]{2,1,0:T(8,128)(2,1)} %bitcast.22), custom_call_target="tpu_custom_call" | custom-call | flops 300000000 | bytes 2000000 | tf_op jit(solution)/shard_map/input_work/pallas_call | solution.py:221
  75.7 9.7 %all-to-all-done.2 = bf16[8,32,128]{2,1,0:T(8,128)(2,1)S(1)} async-done(((bf16[8,32,128]{2,1,0:T(8,128)(2,1)}), bf16[8,32,128]{2,1,0:T(8,128)(2,1)S(1)}, u32[]{:S(2)}, u32[]{:S(2)}) %all-to-all-start.2) | async-done | bytes 65568 | tf_op jit(solution)/shard_map/all_to_all | solution.py:333
  85.4 12.2 %all_to_all.20 = bf16[16,32,128]{2,1,0:T(8,128)(2,1)} all-to-all(bf16[16,32,128]{2,1,0:T(8,128)(2,1)S(1)} %broadcast_in_dim.21), channel_id=1, replica_groups={{0,2,8,10,16,18,24,26,1,3,9,11,17,19,25,27},{4,6,12,14,20,22,28,30,5,7,..., dimensions={0} | all-to-all | bytes 262144 | tf_op jit(solution)/shard_map/all_to_all | solution.py:337
  97.6 1.6 %unpack.1 = (f32[144,256]{1,0:T(8,128)}, f32[144,128]{1,0:T(8,128)}, f32[1,16]{1,0:T(1,128)}) custom-call(bf16[512,128]{1,0:T(8,128)(2,1)} %bitcast.23), custom_call_target="tpu_custom_call" | custom-call | tf_op jit(solution)/shard_map/unpack/pallas_call | solution.py:251
  (8 shorter events, 0.1 us)
Async XLA Ops:
  0.6 15.4 %all-to-all-start = ((bf16[4,2,128,128]{3,2,1,0:T(8,128)(2,1)}), bf16[4,2,128,128]{3,2,1,0:T(8,128)(2,1)S(1)}, u32[]{:S(2)}, u32[]{:S(2)}) async-start(bf16[4,2,128,128]{3,2,1,0:T(8,128)(2,1)} %param.5), calls=%async_computation | async-start | bytes 524288 | tf_op jit(solution)/shard_map/all_to_all | solution.py:300
  16.1 2.6 %collective-permute-start = (bf16[2,128,128]{2,1,0:T(8,128)(2,1)S(1)}, bf16[2,128,128]{2,1,0:T(8,128)(2,1)S(1)}, u32[]{:S(2)}, u32[]{:S(2)}) collective-permute-start(bf16[2,128,128]{2,1,0:T(8,128)(2,1)S(1)} %pad_maximum_fusion), channel_id=1, source_target_pairs={{0,4},{1,5},{2,6},{3,7},{4,8},{5,9},{6,10},{7,11},{8,12},{9,13},{1... | collective-permute-start | bytes 196616 | tf_op jit(solution)/shard_map/ppermute | solution.py:307
  17.4 7.8 %collective-permute-start.1 = (bf16[2,128,128]{2,1,0:T(8,128)(2,1)S(1)}, bf16[2,128,128]{2,1,0:T(8,128)(2,1)S(1)}, u32[]{:S(2)}, u32[]{:S(2)}) collective-permute-start(bf16[2,128,128]{2,1,0:T(8,128)(2,1)S(1)} %pad_maximum_fusion.1), channel_id=1, source_target_pairs={{4,0},{5,1},{6,2},{7,3},{8,4},{9,5},{10,6},{11,7},{12,8},{13,9},{1... | collective-permute-start | bytes 196616 | tf_op jit(solution)/shard_map/ppermute | solution.py:308
  29.0 5.1 %collective-permute-start.2 = (bf16[32,4,32,128]{3,2,1,0:T(8,128)(2,1)S(1)}, bf16[32,4,32,128]{3,2,1,0:T(8,128)(2,1)S(1)}, u32[]{:S(2)}, u32[]{:S(2)}) collective-permute-start(bf16[32,4,32,128]{3,2,1,0:T(8,128)(2,1)S(1)} %get-tuple-element.18), channel_id=1, source_target_pairs={{0,1},{1,0},{2,3},{3,2},{4,5},{5,4},{6,7},{7,6},{8,9},{9,8},{10,11... | collective-permute-start | bytes 3145736 | tf_op jit(solution)/shard_map/ppermute | solution.py:323
  35.4 24.4 %all-to-all-start.1 = ((bf16[32,4,32,128]{3,2,1,0:T(8,128)(2,1)}), bf16[32,4,32,128]{3,2,1,0:T(8,128)(2,1)S(1)}, u32[]{:S(2)}, u32[]{:S(2)}) async-start(bf16[32,4,32,128]{3,2,1,0:T(8,128)(2,1)} %add_convert_fusion), calls=%async_computation.1 | async-start | bytes 2097152 | tf_op jit(solution)/shard_map/all_to_all | solution.py:328
  40.7 11.6 %collective-permute-start.3 = (bf16[64,256]{1,0:T(8,128)(2,1)S(1)}, bf16[64,256]{1,0:T(8,128)(2,1)S(1)}, u32[]{:S(2)}, u32[]{:S(2)}) collective-permute-start(bf16[64,256]{1,0:T(8,128)(2,1)S(1)} %get-tuple-element.19), channel_id=1, source_target_pairs={{0,4},{1,5},{2,6},{3,7},{4,8},{5,9},{6,10},{7,11},{8,12},{9,13},{1... | collective-permute-start | bytes 98312 | tf_op jit(solution)/shard_map/ppermute | solution.py:324
  44.4 7.9 %collective-permute-start.4 = (bf16[64,256]{1,0:T(8,128)(2,1)S(1)}, bf16[64,256]{1,0:T(8,128)(2,1)S(1)}, u32[]{:S(2)}, u32[]{:S(2)}) collective-permute-start(bf16[64,256]{1,0:T(8,128)(2,1)S(1)} %get-tuple-element.20), channel_id=1, source_target_pairs={{4,0},{5,1},{6,2},{7,3},{8,4},{9,5},{10,6},{11,7},{12,8},{13,9},{1... | collective-permute-start | bytes 98312 | tf_op jit(solution)/shard_map/ppermute | solution.py:325
  60.5 24.8 %all-to-all-start.2 = ((bf16[8,32,128]{2,1,0:T(8,128)(2,1)}), bf16[8,32,128]{2,1,0:T(8,128)(2,1)S(1)}, u32[]{:S(2)}, u32[]{:S(2)}) async-start(bf16[8,32,128]{2,1,0:T(8,128)(2,1)} %bitcast.11), calls=%async_computation.2 | async-start | bytes 131072 | tf_op jit(solution)/shard_map/all_to_all | solution.py:333

commit v3 on v2

--- a/solution.py
+++ b/solution.py
@@ -64,26 +64,46 @@
     return preact * sigma, sigma * (1.0 + preact * (1.0 - sigma))
 
 
-def main_body(
-    core, above, below, cot, x_hbm, w1_hbm, bias_hbm, w2_hbm,
-    delta_out, delta_first, delta_last, keep, send,
-    xs, cpad, boxes, ds, packed, x, w1, bias, w2, sems,
-):
-    w2_copy = pltpu.make_async_copy(w2_hbm, w2, sems.at[2])
-    w2_copy.start()
-    x_copy = pltpu.make_async_copy(x_hbm, x, sems.at[3])
-    x_copy.start()
-    bias_copy = pltpu.make_async_copy(bias_hbm, bias, sems.at[4])
-    bias_copy.start()
-    w1_copy = pltpu.make_async_copy(w1_hbm, w1, sems.at[5])
-    w1_copy.start()
-
-    cpad[0:128, :] = above[0]
-    cpad[128 : 128 * 9, :] = cot[...]
-    cpad[128 * 9 :, :] = below[0]
+def start(source, target, sem):
+    copy = pltpu.make_async_copy(source, target, sem)
+    copy.start()
+    return copy
+
+
+def conv_body(x_hbm, w1_hbm, bias_hbm, preact, w1_edge, xs, x, w1, bias, sems):
+    x_copy = start(x_hbm, x, sems.at[0])
+    bias_copy = start(bias_hbm, bias, sems.at[1])
+    w1_copy = start(w1_hbm, w1, sems.at[2])
+    x_copy.wait()
+    wide = x[...].astype(F32)
+    xs[0] = shifted(wide, -1).astype(BF16)
+    xs[1] = x[...]
+    xs[2] = shifted(wide, 1).astype(BF16)
+    bias_copy.wait()
+    w1_copy.wait()
+    same = jnp.broadcast_to(bias[...], (PIX, C1))
+    lower = jnp.zeros((PIX - COLS, C1), F32)
+    upper = jnp.zeros((PIX - COLS, C1), F32)
+    for q in range(3):
+        lower = lower + dot(xs[q, 0 : PIX - COLS, :], w1[q], NN)
+        same = same + dot(xs[q], w1[3 + q], NN)
+        upper = upper + dot(xs[q, COLS:PIX, :], w1[6 + q], NN)
+    preact[0:COLS, :] = same[0:COLS] + upper[0:COLS]
+    middle = slice(COLS, PIX - COLS)
+    preact[middle, :] = same[middle] + upper[COLS:] + lower[: PIX - 2 * COLS]
+    preact[PIX - COLS :, :] = same[PIX - COLS :] + lower[PIX - 2 * COLS :]
+    w1_edge[0:3] = w1[0:3]
+    w1_edge[3:6] = w1[6:9]
+
+
+def boxes_body(cot, w2_hbm, boxes, grad_act, w2_edge, w2, sem):
+    w2_copy = start(w2_hbm, w2, sem)
     pick = pick_columns()
-    for h in range(-1, 8):
-        sums = dot(pick, cpad[128 * (h + 1) : 128 * (h + 3), :], NN).astype(BF16)
+    zero = jnp.zeros((COLS, 3 * C2), BF16)
+    boxes[0:COLS, 6 * C2 :] = zero
+    boxes[PIX - COLS :, 0 : 3 * C2] = zero
+    for h in range(7):
+        sums = dot(pick, cot[128 * h : 128 * (h + 2), :], NN).astype(BF16)
         for p in range(3):
             if (h + p - 1) % 2 == 0 and 0 <= (h + p - 1) // 2 < ROWS:
                 i = (h + p - 1) // 2
@@ -93,31 +113,55 @@
                         COLS * q : COLS * (q + 1), :
                     ]
     w2_copy.wait()
-    grad_act = jnp.zeros((PIX, C1), F32)
+    total = jnp.zeros((PIX, C1), F32)
     for t in range(9):
-        grad_act = grad_act + dot(boxes[:, C2 * t : C2 * (t + 1)], w2[t], NT)
-
-    x_copy.wait()
-    xs[1, 0:COLS, 0:C2] = above[1, 0:COLS, :]
-    xs[1, 0:COLS, C2:C1] = above[1, COLS : 2 * COLS, :]
-    xs[1, COLS : COLS + PIX, :] = x[...]
-    xs[1, COLS + PIX :, 0:C2] = below[1, 0:COLS, :]
-    xs[1, COLS + PIX :, C2:C1] = below[1, COLS : 2 * COLS, :]
-    wide = xs[1].astype(F32)
-    xs[0] = shifted(wide, -1).astype(BF16)
-    xs[2] = shifted(wide, 1).astype(BF16)
-    bias_copy.wait()
-    w1_copy.wait()
-    preact = jnp.broadcast_to(bias[...], (PIX, C1))
-    for p in range(3):
+        total = total + dot(boxes[:, C2 * t : C2 * (t + 1)], w2[t], NT)
+    grad_act[...] = total
+    w2_edge[0:3] = w2[6:9]
+    w2_edge[3:6] = w2[0:3]
+
+
+def main_body(
+    core, above, below, cot, preact_in, boxes_in, grad_act_in, w1_edge, w2_edge, x_hbm,
+    delta_out, delta_first, delta_last, packed, send,
+    x, boxes, ds, preact, grad_act, sems,
+):
+    x_copy = start(x_hbm, x.at[COLS : COLS + PIX], sems.at[4])
+
+    boxes[...] = boxes_in[...]
+    grad_act[...] = grad_act_in[...]
+    preact[...] = preact_in[...]
+    pick = pick_columns()
+    first, last = slice(0, COLS), slice(PIX - COLS, PIX)
+    for rows, p, pair in (
+        (first, 2, (above[0], cot[0:128, :])),
+        (last, 0, (cot[128 * 7 : 128 * 8, :], below[0])),
+    ):
+        sums = dot(pick, jnp.concatenate(pair), NN).astype(BF16)
         for q in range(3):
-            preact = preact + dot(xs[q, p * COLS : p * COLS + PIX, :], w1[3 * p + q], NN)
-    act, slope = silu_parts(preact)
+            t = 3 * p + q
+            boxes[rows, C2 * t : C2 * (t + 1)] = sums[COLS * q : COLS * (q + 1), :]
+    for at, halo in ((0, above), (COLS + PIX, below)):
+        x[at : at + COLS, 0:C2] = halo[1, 0:COLS, :]
+        x[at : at + COLS, C2:C1] = halo[1, COLS : 2 * COLS, :]
+    for side, rows, p in ((0, first, 2), (1, last, 0)):
+        part = grad_act[rows, :]
+        for q in range(3):
+            t = 3 * p + q
+            part = part + dot(boxes[rows, C2 * t : C2 * (t + 1)], w2_edge[3 * side + q], NT)
+        grad_act[rows, :] = part
+    for side, rows, at in ((0, first, 0), (1, last, COLS + PIX)):
+        wide = x[at : at + COLS, :].astype(F32)
+        part = preact[rows, :]
+        for q in range(3):
+            part = part + dot(shifted(wide, q - 1).astype(BF16), w1_edge[3 * side + q], NN)
+        preact[rows, :] = part
+    act, slope = silu_parts(preact[...])
     second = dot(act.astype(BF16), boxes[...], TN).astype(BF16)
     for t in range(9):
         put(packed, 2, t, second[:, C2 * t : C2 * (t + 1)])
 
-    delta = (grad_act * slope).astype(BF16)
+    delta = (grad_act[...] * slope).astype(BF16)
     delta_out[...] = delta
     delta_first[...] = delta[0:COLS]
     delta_last[...] = delta[PIX - COLS : PIX]
@@ -143,20 +187,22 @@
             half, chunk, z_hi, at = spot(d, row)
             packed[half, chunk, z_hi, at : at + 16, :] = band[d] if row == 3 * SLICE else empty
 
+    mine = core[0]
+    copies = []
+    x_copy.wait()
     for p in range(3):
-        lhs = xs[1, p * COLS : p * COLS + PIX, :]
+        lhs = x[p * COLS : p * COLS + PIX, :]
         for q in range(3):
+            tap = 3 * p + q
             part = dot(lhs, ds[q], TN).astype(BF16)
-            put(packed, 0, 3 * p + q, part[:, 0:C2])
-            put(packed, 1, 3 * p + q, part[:, C2:C1])
-
-    mine = core[0]
-    send_copy = pltpu.make_async_copy(packed.at[1 - mine], send, sems.at[1])
-    send_copy.start()
-    keep_copy = pltpu.make_async_copy(packed.at[mine], keep, sems.at[0])
-    keep_copy.start()
-    send_copy.wait()
-    keep_copy.wait()
+            put(packed, 0, tap, part[:, 0:C2])
+            put(packed, 1, tap, part[:, C2:C1])
+            if tap in (2, 4, 6, 8):
+                n = tap // 2 - 1
+                chunks = pl.ds(n * (PIECES // 2), PIECES // 2)
+                copies.append(start(packed.at[1 - mine, chunks], send.at[chunks], sems.at[n]))
+    for copy in copies:
+        copy.wait()
 
 
 VMEM = pl.BlockSpec(memory_space=pltpu.VMEM)
@@ -165,37 +211,120 @@
 ANYWHERE = pl.BlockSpec(memory_space=pl.ANY)
 
 
-def main_work(core, above, below, cot, x, w1, bias, w2):
-    parts = (2 * PIECES, 4, PIECE, 128)
+def conv_work(x, w1, bias):
+    return pl.pallas_call(
+        conv_body,
+        out_shape=(
+            jax.ShapeDtypeStruct((PIX, C1), F32),
+            jax.ShapeDtypeStruct((6, C1, C1), BF16),
+        ),
+        in_specs=[HBM] * 3,
+        out_specs=(VMEM, VMEM),
+        scratch_shapes=[
+            pltpu.VMEM((3, PIX, C1), BF16),
+            pltpu.VMEM((PIX, C1), BF16),
+            pltpu.VMEM((9, C1, C1), BF16),
+            pltpu.VMEM((1, C1), F32),
+            pltpu.SemaphoreType.DMA((3,)),
+        ],
+        compiler_params=pltpu.CompilerParams(vmem_limit_bytes=12 * 2**20),
+        cost_estimate=pl.CostEstimate(
+            flops=300_000_000, bytes_accessed=1_500_000, transcendentals=0
+        ),
+        name="conv_work",
+    )(x, w1, bias)
+
+
+def boxes_work(cot, w2):
+    return pl.pallas_call(
+        boxes_body,
+        out_shape=(
+            jax.ShapeDtypeStruct((PIX, 9 * C2), BF16),
+            jax.ShapeDtypeStruct((PIX, C1), F32),
+            jax.ShapeDtypeStruct((6, C1, C2), BF16),
+        ),
+        in_specs=[VMEM, HBM],
+        out_specs=(VMEM, VMEM, VMEM),
+        scratch_shapes=[pltpu.VMEM((9, C1, C2), BF16), pltpu.SemaphoreType.DMA],
+        compiler_params=pltpu.CompilerParams(vmem_limit_bytes=12 * 2**20),
+        cost_estimate=pl.CostEstimate(
+            flops=300_000_000, bytes_accessed=1_500_000, transcendentals=0
+        ),
+        name="boxes_work",
+    )(cot, w2)
+
+
+PARTS = (2 * PIECES, 4, PIECE, 128)
+
+
+def main_work(core, above, below, cot, preact, boxes, grad_act, w1_edge, w2_edge, x):
     return pl.pallas_call(
         main_body,
         out_shape=(
             jax.ShapeDtypeStruct((PIX, C1), BF16),
             jax.ShapeDtypeStruct((COLS, C1), BF16),
             jax.ShapeDtypeStruct((COLS, C1), BF16),
-            jax.ShapeDtypeStruct(parts, BF16),
-            jax.ShapeDtypeStruct(parts, BF16),
-        ),
-        in_specs=[SMEM] + [VMEM] * 3 + [HBM] * 4,
-        out_specs=(VMEM, VMEM, VMEM, ANYWHERE, ANYWHERE),
+            jax.ShapeDtypeStruct((2,) + PARTS, BF16),
+            jax.ShapeDtypeStruct(PARTS, BF16),
+        ),
+        in_specs=[SMEM] + [VMEM] * 8 + [HBM],
+        out_specs=(VMEM, VMEM, VMEM, VMEM, ANYWHERE),
         scratch_shapes=[
-            pltpu.VMEM((3, PIX + 2 * COLS, C1), BF16),
-            pltpu.VMEM((128 * 10, C2), BF16),
+            pltpu.VMEM((PIX + 2 * COLS, C1), BF16),
             pltpu.VMEM((PIX, 9 * C2), BF16),
             pltpu.VMEM((3, PIX, C1), BF16),
-            pltpu.VMEM((2,) + parts, BF16),
-            pltpu.VMEM((PIX, C1), BF16),
-            pltpu.VMEM((9, C1, C1), BF16),
-            pltpu.VMEM((1, C1), F32),
-            pltpu.VMEM((9, C1, C2), BF16),
-            pltpu.SemaphoreType.DMA((6,)),
+            pltpu.VMEM((PIX, C1), F32),
+            pltpu.VMEM((PIX, C1), F32),
+            pltpu.SemaphoreType.DMA((5,)),
         ],
-        compiler_params=pltpu.CompilerParams(vmem_limit_bytes=12 * 2**20),
+        compiler_params=pltpu.CompilerParams(vmem_limit_bytes=16 * 2**20),
         cost_estimate=pl.CostEstimate(
-            flops=1_100_000_000, bytes_accessed=5_000_000, transcendentals=70_000
+            flops=600_000_000, bytes_accessed=5_000_000, transcendentals=70_000
         ),
         name="main_work",
-    )(core, above, below, cot, x, w1, bias, w2)
+    )(core, above, below, cot, preact, boxes, grad_act, w1_edge, w2_edge, x)
+
+
+def pair_body(core, packed, received, pair, total, sems):
+    mine = core[0]
+    copies = []
+    for n in range(4):
+        chunks = pl.ds(n * (PIECES // 2), PIECES // 2)
+        total[chunks] = packed[mine, chunks] + received[chunks]
+        copies.append(start(total.at[chunks], pair.at[chunks], sems.at[n]))
+    for copy in copies:
+        copy.wait()
+
+
+def pair_work(core, packed, received):
+    return pl.pallas_call(
+        pair_body,
+        out_shape=jax.ShapeDtypeStruct(PARTS, BF16),
+        in_specs=[SMEM, VMEM, VMEM],
+        out_specs=ANYWHERE,
+        scratch_shapes=[pltpu.VMEM(PARTS, BF16), pltpu.SemaphoreType.DMA((4,))],
+        compiler_params=pltpu.CompilerParams(vmem_limit_bytes=8 * 2**20),
+        name="pair_work",
+    )(core, packed, received)
+
+
+def sum_body(copies, pieces, out):
+    total = pieces[0].astype(F32)
+    for n in range(1, pieces.shape[0]):
+        total = total + pieces[n].astype(F32)
+    for n in range(copies):
+        out[n] = total.astype(BF16)
+
+
+def sum_work(pieces, copies):
+    return pl.pallas_call(
+        lambda *refs: sum_body(copies, *refs),
+        out_shape=jax.ShapeDtypeStruct((copies,) + pieces.shape[1:], BF16),
+        in_specs=[VMEM],
+        out_specs=VMEM,
+        compiler_params=pltpu.CompilerParams(vmem_limit_bytes=4 * 2**20),
+        name="sum_work",
+    )(pieces)
 
 
 def input_body(delta, above, below, w1_hbm, grad_x, ext, ds, w1, sem):
@@ -276,7 +405,7 @@
     for c in TWO
 ]
 COLUMN = [
-    [place(x, zh, y, zb, za, c) for zh in FOUR for zb in TWO]
+    [place(x, zh, y, zb, za, c) for zb in TWO for zh in FOUR]
     for x in FOUR
     for y in FOUR
     for za in TWO
@@ -284,10 +413,6 @@
 ]
 SHARE = [[place(0, 0, y, zb, za, c) for c in TWO for y in FOUR for za in TWO] for zb in TWO]
 QUADS = [[4 * j + b for b in FOUR] for j in range(8)]
-
-
-def added(pieces):
-    return jnp.sum(pieces.astype(F32), axis=0).astype(BF16)
 
 
 def shards(cotangent, inputs, w_first, bias_first, w_second):
@@ -317,29 +442,29 @@
         )
     )
     cot = cot.reshape(8 * 128, C2)
-    delta, delta_first, delta_last, keep, send = main_work(
-        core, above, below, cot, x_flat, w1, bias, w2
+    preact, w1_edge = conv_work(x_flat, w1, bias)
+    boxes, grad_act, w2_edge = boxes_work(cot, w2)
+    delta, delta_first, delta_last, packed, send = main_work(
+        core, above, below, cot, preact, boxes, grad_act, w1_edge, w2_edge, x_flat
     )
     received = lax.ppermute(send, "rows", [(i, i ^ 1) for i in range(32)])
     from_above = lax.ppermute(delta_last, "rows", down)
     from_below = lax.ppermute(delta_first, "rows", up)
 
-    pair = (keep.astype(F32) + received.astype(F32)).astype(BF16)
+    pair = pair_work(core, packed, received)
     block = lax.all_to_all(pair, both, 0, 0, axis_index_groups=BLOCK)
     block, from_above, from_below = lax.optimization_barrier((block, from_above, from_below))
-    block = added(block)
     grad_x = input_work(delta, from_above, from_below, w1)
-    spread = jnp.broadcast_to(block[:, None], (4, 2, PIECE, 128)).reshape(8, PIECE, 128)
+    spread = sum_work(block, 2).reshape(8, PIECE, 128)
     column = lax.all_to_all(spread, both, 0, 0, axis_index_groups=COLUMN)
     column, grad_x = lax.optimization_barrier((column, grad_x))
-    piece = added(column)
-    copies = jnp.broadcast_to(piece[None], (PIECES, PIECE, 128))
-    full = lax.all_to_all(copies, "rows", 0, 0, axis_index_groups=SHARE)
+    full = lax.all_to_all(sum_work(column, PIECES), "rows", 0, 0, axis_index_groups=SHARE)
 
     pixels_low = lax.axis_size("dp") * lax.axis_size("rows") * PIX
     scale_low = pixels_low ** (-0.5)
     scale_high = (4 * pixels_low) ** (-0.5)
-    grad_first, grad_second, grad_bias = results(full.reshape(PACK, 128), scale_low, scale_high)
+    full = pltpu.with_memory_space_constraint(full.reshape(PACK, 128), pltpu.VMEM)
+    grad_first, grad_second, grad_bias = results(full, scale_low, scale_high)
     grad_input = grad_x.reshape(1, ROWS, COLS, C1)
     return grad_input, grad_first, grad_second, grad_bias.reshape(16)
 

time: 99.9 us -> 96 us (0.961)
  waiting for transfers between devices: 36.9 us -> 32.7 us
  Pallas kernels: 7.77 us -> 10.7 us
  other arithmetic: 1.56 us -> 0.03 us
    pallas_call x0 -> x5, Pallas kernels: none -> 5.34 us  [the longest x1 1.86 us: conv_work(): pl.pallas_call(conv_body, out_shape=(jax.ShapeDtypeStruct((PIX, C1), F32)...]
    ppermute x1, waiting for transfers between devices: 6.52 us -> 3.04 us  [shards(): below = lax.ppermute(halo(cot[0:1], x[0]), 'rows', up)]
    pallas_call x1, Pallas kernels: 3.73 us -> 2.21 us  [main_work(): pl.pallas_call(main_body, out_shape=(jax.ShapeDtypeStruct((PIX, C1), BF16...]
    convert_element_type x1 -> x0, other arithmetic: 1.36 us -> none  [shards(): pair = (keep.astype(F32) + received.astype(F32)).astype(BF16)]
  transfers between devices with their start and end apart: 8 -> 8, of which waited for: 6 -> 6; matrix products, arithmetic and copies ran while one was open for 1% -> 1% of each run, Pallas kernels for 2% -> 6%
where the time goes in v3:
time: 96 us; the launch traced here: 95.3 us
  starting transfers between devices  38.6 us (40%)
  waiting for transfers between devices  32.7 us (34%)
  blocking collectives  11.7 us (12%)
  Pallas kernels  10.7 us (11%)
    all_to_all x1, starting transfers between devices, shards(): column = lax.all_to_all(spread, both, 0, 0, axis_index_groups=COLUMN)  12.7 us
    all_to_all x1, blocking collectives, shards(): lax.all_to_all(sum_work(column, PIECES), 'rows', 0, 0, axis_index_groups=...  11.7 us
    all_to_all x1, starting transfers between devices, shards(): cot = lax.all_to_all(cotangent, 'rows', 0, 0, axis_index_groups=QUADS)  10.3 us
    all_to_all x1, waiting for transfers between devices, shards(): column = lax.all_to_all(spread, both, 0, 0, axis_index_groups=COLUMN)  8.99 us
    all_to_all x1, waiting for transfers between devices, shards(): block = lax.all_to_all(pair, both, 0, 0, axis_index_groups=BLOCK)  7.48 us
    ppermute x1, waiting for transfers between devices, shards(): from_above = lax.ppermute(delta_last, 'rows', down)  6.61 us
    all_to_all x1, starting transfers between devices, shards(): block = lax.all_to_all(pair, both, 0, 0, axis_index_groups=BLOCK)  5.29 us
    all_to_all x1, waiting for transfers between devices, shards(): cot = lax.all_to_all(cotangent, 'rows', 0, 0, axis_index_groups=QUADS)  4.35 us
  transfers between devices with their start and end apart: 8, of which 6 were waited for; matrix products, arithmetic and copies ran while one was open for 1% of the time, Pallas kernels for 6%

profile of v3, /device:TPU:1, one launch (start us, length us, event | category | flops | bytes accessed | tf_op | source)
XLA Modules:
  0.0 95.3 jit_solution(17110360500603972747)
XLA Ops:
  0.6 10.3 %all-to-all-start = ((bf16[4,2,128,128]{3,2,1,0:T(8,128)(2,1)}), bf16[4,2,128,128]{3,2,1,0:T(8,128)(2,1)S(1)}, u32[]{:S(2)}, u32[]{:S(2)}) async-start(bf16[4,2,128,128]{3,2,1,0:T(8,128)(2,1)} %param.5), calls=%async_computation | async-start | bytes 524288 | tf_op jit(solution)/shard_map/all_to_all | solution.py:425
  10.9 0.8 slice_bitcast_fusion
  11.7 4.4 %all-to-all-done = bf16[4,2,128,128]{3,2,1,0:T(8,128)(2,1)S(1)} async-done(((bf16[4,2,128,128]{3,2,1,0:T(8,128)(2,1)}), bf16[4,2,128,128]{3,2,1,0:T(8,128)(2,1)S(1)}, u32[]{:S(2)}, u32[]{:S(2)}) %all-to-all-start) | async-done | bytes 262176 | tf_op jit(solution)/shard_map/all_to_all | solution.py:425
  16.1 1.3 %collective-permute-start = (bf16[2,128,128]{2,1,0:T(8,128)(2,1)S(1)}, bf16[2,128,128]{2,1,0:T(8,128)(2,1)S(1)}, u32[]{:S(2)}, u32[]{:S(2)}) collective-permute-start(bf16[2,128,128]{2,1,0:T(8,128)(2,1)S(1)} %pad_maximum_fusion), channel_id=1, source_target_pairs={{0,4},{1,5},{2,6},{3,7},{4,8},{5,9},{6,10},{7,11},{8,12},{9,13},{1... | collective-permute-start | bytes 196616 | tf_op jit(solution)/shard_map/ppermute | solution.py:432
  17.4 1.3 %collective-permute-start.1 = (bf16[2,128,128]{2,1,0:T(8,128)(2,1)S(1)}, bf16[2,128,128]{2,1,0:T(8,128)(2,1)S(1)}, u32[]{:S(2)}, u32[]{:S(2)}) collective-permute-start(bf16[2,128,128]{2,1,0:T(8,128)(2,1)S(1)} %pad_maximum_fusion.1), channel_id=1, source_target_pairs={{4,0},{5,1},{6,2},{7,3},{8,4},{9,5},{10,6},{11,7},{12,8},{13,9},{1... | collective-permute-start | bytes 196616 | tf_op jit(solution)/shard_map/ppermute | solution.py:433
  18.7 1.9 %conv_work.1 = (f32[256,256]{1,0:T(8,128)S(1)}, bf16[6,256,256]{2,1,0:T(8,128)(2,1)S(1)}) custom-call(bf16[256,256]{1,0:T(8,128)(2,1)} %bitcast.25, bf16[9,256,256]{2,1,0:T(8,128)(2,1)} %bitcast.23, f32[1,256]{1,0:T(1,128)} %bitcast.28), custom_call_target="tpu_custom_call" | custom-call | flops 300000000 | bytes 1500000 | tf_op jit(solution)/shard_map/conv_work/pallas_call | solution.py:215
  20.6 1.6 %boxes_work.1 = (bf16[256,1152]{1,0:T(8,128)(2,1)S(1)}, f32[256,256]{1,0:T(8,128)S(1)}, bf16[6,256,128]{2,1,0:T(8,128)(2,1)S(1)}) custom-call(bf16[1024,128]{1,0:T(8,128)(2,1)S(1)} %bitcast.20, bf16[9,256,128]{2,1,0:T(8,128)(2,1)} %bitcast.29), custom_call_target="tpu_custom_call" | custom-call | flops 300000000 | bytes 1500000 | tf_op jit(solution)/shard_map/boxes_work/pallas_call | solution.py:239
  22.2 0.0 collective-permute-done.above
  22.2 3.0 %collective-permute-done.1.below = bf16[2,128,128]{2,1,0:T(8,128)(2,1)S(1)} collective-permute-done((bf16[2,128,128]{2,1,0:T(8,128)(2,1)S(1)}, bf16[2,128,128]{2,1,0:T(8,128)(2,1)S(1)}, u32[]{:S(2)}, u32[]{:S(2)}) %collective-permute-start.1) | collective-permute-done | bytes 65568 | tf_op jit(solution)/shard_map/ppermute | solution.py:433
  25.2 2.2 %main_work.1 = (bf16[256,256]{1,0:T(8,128)(2,1)S(1)}, bf16[64,256]{1,0:T(8,128)(2,1)S(1)}, bf16[64,256]{1,0:T(8,128)(2,1)S(1)}, bf16[2,32,4,32,128]{4,3,2,1,0:T(8,128)(2,1)S(1)}, bf16[32,4,32,128]{3,2,1,0:T(8,128)(2,1)S(1)}) custom-call(s32[1]{0:T(128)} %bitcast.core, bf16[2,128,128]{2,1,0:T(8,128)(2,1)S(1)} %collective-permute-done.above, ...), custom_call_target="tpu_custom_call" | custom-call | flops 600000000 | bytes 5000000 | tf_op jit(solution)/shard_map/main_work/pallas_call | solution.py:261
  27.5 2.8 %collective-permute-start.2 = (bf16[32,4,32,128]{3,2,1,0:T(8,128)(2,1)S(1)}, bf16[32,4,32,128]{3,2,1,0:T(8,128)(2,1)S(1)}, u32[]{:S(2)}, u32[]{:S(2)}) collective-permute-start(bf16[32,4,32,128]{3,2,1,0:T(8,128)(2,1)S(1)} %get-tuple-element.28), channel_id=1, source_target_pairs={{0,1},{1,0},{2,3},{3,2},{4,5},{5,4},{6,7},{7,6},{8,9},{9,8},{10,11... | collective-permute-start | bytes 3145736 | tf_op jit(solution)/shard_map/ppermute | solution.py:450
  30.2 2.3 %collective-permute-done.2.received = bf16[32,4,32,128]{3,2,1,0:T(8,128)(2,1)S(1)} collective-permute-done((bf16[32,4,32,128]{3,2,1,0:T(8,128)(2,1)S(1)}, bf16[32,4,32,128]{3,2,1,0:T(8,128)(2,1)S(1)}, u32[]{:S(2)}, u32[]{:S(2)}) %collective-permute-start.2) | collective-permute-done | bytes 1048608 | tf_op jit(solution)/shard_map/ppermute | solution.py:450
  32.5 1.1 %pair_work.1 = bf16[32,4,32,128]{3,2,1,0:T(8,128)(2,1)} custom-call(s32[1]{0:T(128)} %bitcast.core, bf16[2,32,4,32,128]{4,3,2,1,0:T(8,128)(2,1)S(1)} %get-tuple-element.27.packed, bf16[32,4,32,128]{3,2,1,0:T(8,128)(2,1)S(1)} %collective-permute-done.2.received), custom_call_target="tpu_custom_call" | custom-call | tf_op jit(solution)/shard_map/pair_work/pallas_call | solution.py:300
  33.6 5.3 %all-to-all-start.1 = ((bf16[32,4,32,128]{3,2,1,0:T(8,128)(2,1)}), bf16[32,4,32,128]{3,2,1,0:T(8,128)(2,1)S(1)}, u32[]{:S(2)}, u32[]{:S(2)}) async-start(bf16[32,4,32,128]{3,2,1,0:T(8,128)(2,1)} %pair_work.1), calls=%async_computation.1 | async-start | bytes 2097152 | tf_op jit(solution)/shard_map/all_to_all | solution.py:455
  38.9 3.7 %collective-permute-start.3 = (bf16[64,256]{1,0:T(8,128)(2,1)S(1)}, bf16[64,256]{1,0:T(8,128)(2,1)S(1)}, u32[]{:S(2)}, u32[]{:S(2)}) collective-permute-start(bf16[64,256]{1,0:T(8,128)(2,1)S(1)} %get-tuple-element.29), channel_id=1, source_target_pairs={{0,4},{1,5},{2,6},{3,7},{4,8},{5,9},{6,10},{7,11},{8,12},{9,13},{1... | collective-permute-start | bytes 98312 | tf_op jit(solution)/shard_map/ppermute | solution.py:451
  42.6 1.3 %collective-permute-start.4 = (bf16[64,256]{1,0:T(8,128)(2,1)S(1)}, bf16[64,256]{1,0:T(8,128)(2,1)S(1)}, u32[]{:S(2)}, u32[]{:S(2)}) collective-permute-start(bf16[64,256]{1,0:T(8,128)(2,1)S(1)} %get-tuple-element.30), channel_id=1, source_target_pairs={{4,0},{5,1},{6,2},{7,3},{8,4},{9,5},{10,6},{11,7},{12,8},{13,9},{1... | collective-permute-start | bytes 98312 | tf_op jit(solution)/shard_map/ppermute | solution.py:452
  43.9 6.6 %collective-permute-done.3.above = bf16[64,256]{1,0:T(8,128)(2,1)S(1)} collective-permute-done((bf16[64,256]{1,0:T(8,128)(2,1)S(1)}, bf16[64,256]{1,0:T(8,128)(2,1)S(1)}, u32[]{:S(2)}, u32[]{:S(2)}) %collective-permute-start.3) | collective-permute-done | bytes 32800 | tf_op jit(solution)/shard_map/ppermute | solution.py:451
  50.5 0.0 collective-permute-done.4.below
  50.5 7.5 %all-to-all-done.1.refs_0_ = bf16[32,4,32,128]{3,2,1,0:T(8,128)(2,1)S(1)} async-done(((bf16[32,4,32,128]{3,2,1,0:T(8,128)(2,1)}), bf16[32,4,32,128]{3,2,1,0:T(8,128)(2,1)S(1)}, u32[]{:S(2)}, u32[]{:S(2)}) %all-to-all-start.1) | async-done | bytes 1048608 | tf_op jit(solution)/shard_map/all_to_all | solution.py:455
  58.0 0.8 sum_work.2
  58.7 12.7 %all-to-all-start.2 = ((bf16[8,32,128]{2,1,0:T(8,128)(2,1)}), bf16[8,32,128]{2,1,0:T(8,128)(2,1)S(1)}, u32[]{:S(2)}, u32[]{:S(2)}) async-start(bf16[8,32,128]{2,1,0:T(8,128)(2,1)} %bitcast.11), calls=%async_computation.2 | async-start | bytes 131072 | tf_op jit(solution)/shard_map/all_to_all | solution.py:459
  71.4 2.4 %input_work.1 = bf16[256,256]{1,0:T(8,128)(2,1)} custom-call(bf16[256,256]{1,0:T(8,128)(2,1)S(1)} %get-tuple-element.32.delta, bf16[64,256]{1,0:T(8,128)(2,1)S(1)} %collective-permute-done.3.above, bf16[64,256]{1,0:T(8,128)(2,1)S(1)} %collective-permute-done.4.below, bf16[9,256,256]{2,1,0:T(8,128)(2,1)} %bitcast.24), custom_call_target="tpu_custom_call" | custom-call | flops 300000000 | bytes 2000000 | tf_op jit(solution)/shard_map/input_work/pallas_call | solution.py:350
  73.9 9.0 %all-to-all-done.2.refs_0_ = bf16[8,32,128]{2,1,0:T(8,128)(2,1)S(1)} async-done(((bf16[8,32,128]{2,1,0:T(8,128)(2,1)}), bf16[8,32,128]{2,1,0:T(8,128)(2,1)S(1)}, u32[]{:S(2)}, u32[]{:S(2)}) %all-to-all-start.2) | async-done | bytes 65568 | tf_op jit(solution)/shard_map/all_to_all | solution.py:459
  82.9 11.7 %all_to_all.20 = bf16[16,32,128]{2,1,0:T(8,128)(2,1)S(1)} all-to-all(bf16[16,32,128]{2,1,0:T(8,128)(2,1)S(1)} %sum_work.3), channel_id=1, replica_groups={{0,2,8,10,16,18,24,26,1,3,9,11,17,19,25,27},{4,6,12,14,20,22,28,30,5,7,..., dimensions={0} | all-to-all | bytes 262144 | tf_op jit(solution)/shard_map/all_to_all | solution.py:461
  94.6 0.7 unpack.1
  (7 shorter events, 0.1 us)
Async XLA Ops:
  0.6 15.4 %all-to-all-start = ((bf16[4,2,128,128]{3,2,1,0:T(8,128)(2,1)}), bf16[4,2,128,128]{3,2,1,0:T(8,128)(2,1)S(1)}, u32[]{:S(2)}, u32[]{:S(2)}) async-start(bf16[4,2,128,128]{3,2,1,0:T(8,128)(2,1)} %param.5), calls=%async_computation | async-start | bytes 524288 | tf_op jit(solution)/shard_map/all_to_all | solution.py:425
  16.1 6.1 %collective-permute-start = (bf16[2,128,128]{2,1,0:T(8,128)(2,1)S(1)}, bf16[2,128,128]{2,1,0:T(8,128)(2,1)S(1)}, u32[]{:S(2)}, u32[]{:S(2)}) collective-permute-start(bf16[2,128,128]{2,1,0:T(8,128)(2,1)S(1)} %pad_maximum_fusion), channel_id=1, source_target_pairs={{0,4},{1,5},{2,6},{3,7},{4,8},{5,9},{6,10},{7,11},{8,12},{9,13},{1... | collective-permute-start | bytes 196616 | tf_op jit(solution)/shard_map/ppermute | solution.py:432
  17.4 7.8 %collective-permute-start.1 = (bf16[2,128,128]{2,1,0:T(8,128)(2,1)S(1)}, bf16[2,128,128]{2,1,0:T(8,128)(2,1)S(1)}, u32[]{:S(2)}, u32[]{:S(2)}) collective-permute-start(bf16[2,128,128]{2,1,0:T(8,128)(2,1)S(1)} %pad_maximum_fusion.1), channel_id=1, source_target_pairs={{4,0},{5,1},{6,2},{7,3},{8,4},{9,5},{10,6},{11,7},{12,8},{13,9},{1... | collective-permute-start | bytes 196616 | tf_op jit(solution)/shard_map/ppermute | solution.py:433
  27.5 5.0 %collective-permute-start.2 = (bf16[32,4,32,128]{3,2,1,0:T(8,128)(2,1)S(1)}, bf16[32,4,32,128]{3,2,1,0:T(8,128)(2,1)S(1)}, u32[]{:S(2)}, u32[]{:S(2)}) collective-permute-start(bf16[32,4,32,128]{3,2,1,0:T(8,128)(2,1)S(1)} %get-tuple-element.28), channel_id=1, source_target_pairs={{0,1},{1,0},{2,3},{3,2},{4,5},{5,4},{6,7},{7,6},{8,9},{9,8},{10,11... | collective-permute-start | bytes 3145736 | tf_op jit(solution)/shard_map/ppermute | solution.py:450
  33.6 24.4 %all-to-all-start.1 = ((bf16[32,4,32,128]{3,2,1,0:T(8,128)(2,1)}), bf16[32,4,32,128]{3,2,1,0:T(8,128)(2,1)S(1)}, u32[]{:S(2)}, u32[]{:S(2)}) async-start(bf16[32,4,32,128]{3,2,1,0:T(8,128)(2,1)} %pair_work.1), calls=%async_computation.1 | async-start | bytes 2097152 | tf_op jit(solution)/shard_map/all_to_all | solution.py:455
  38.9 11.6 %collective-permute-start.3 = (bf16[64,256]{1,0:T(8,128)(2,1)S(1)}, bf16[64,256]{1,0:T(8,128)(2,1)S(1)}, u32[]{:S(2)}, u32[]{:S(2)}) collective-permute-start(bf16[64,256]{1,0:T(8,128)(2,1)S(1)} %get-tuple-element.29), channel_id=1, source_target_pairs={{0,4},{1,5},{2,6},{3,7},{4,8},{5,9},{6,10},{7,11},{8,12},{9,13},{1... | collective-permute-start | bytes 98312 | tf_op jit(solution)/shard_map/ppermute | solution.py:451
  42.6 7.9 %collective-permute-start.4 = (bf16[64,256]{1,0:T(8,128)(2,1)S(1)}, bf16[64,256]{1,0:T(8,128)(2,1)S(1)}, u32[]{:S(2)}, u32[]{:S(2)}) collective-permute-start(bf16[64,256]{1,0:T(8,128)(2,1)S(1)} %get-tuple-element.30), channel_id=1, source_target_pairs={{4,0},{5,1},{6,2},{7,3},{8,4},{9,5},{10,6},{11,7},{12,8},{13,9},{1... | collective-permute-start | bytes 98312 | tf_op jit(solution)/shard_map/ppermute | solution.py:452
  58.7 24.1 %all-to-all-start.2 = ((bf16[8,32,128]{2,1,0:T(8,128)(2,1)}), bf16[8,32,128]{2,1,0:T(8,128)(2,1)S(1)}, u32[]{:S(2)}, u32[]{:S(2)}) async-start(bf16[8,32,128]{2,1,0:T(8,128)(2,1)} %bitcast.11), calls=%async_computation.2 | async-start | bytes 131072 | tf_op jit(solution)/shard_map/all_to_all | solution.py:459

commit v4 on v3

--- a/solution.py
+++ b/solution.py
@@ -13,9 +13,11 @@
 ROWS = 4
 PIX = ROWS * COLS
 SLICE = 144
-PIECE = 32
+TILES = 28
+PIECE = (32, 128)
 PIECES = 16
-PACK = PIECE * PIECES
+CHUNK = 16 * TILES // 4
+PARTS = (CHUNK, 32, 128)
 
 
 def dot(a, b, contract):
@@ -35,21 +37,26 @@
     return jnp.where(inside, rolled, 0.0)
 
 
-def spot(d, row):
-    piece, inner = divmod(row, PIECE)
-    half, rest = divmod(piece, PIECES // 2)
+def tiles_of(k, z_hi):
+    return 1 if k % 4 == z_hi else 2
+
+
+def spot(d, tile):
+    half, tile = divmod(tile, TILES // 2)
     x, z_hi = divmod(d, 4)
-    return half, x * (PIECES // 2) + rest, z_hi, inner
+    k = 0
+    while tile >= tiles_of(k, z_hi):
+        tile -= tiles_of(k, z_hi)
+        k += 1
+    before = sum(tiles_of(k, z) for z in range(z_hi)) + tile
+    return half, CHUNK * (x * 8 + k) + 16 * before
 
 
 def put(packed, band, tap, value):
-    row = 0
-    while row < C1:
+    for row in range(0, C1, 16):
         d, inner = divmod(tap * C1 + row, SLICE)
-        half, chunk, z_hi, at = spot(d, band * SLICE + inner)
-        count = min(C1 - row, SLICE - inner, PIECE - at)
-        packed[half, chunk, z_hi, at : at + count, :] = value[row : row + count, :]
-        row += count
+        half, at = spot(d, band * (SLICE // 16) + inner // 16)
+        packed[half, at // 32, at % 32 : at % 32 + 16, :] = value[row : row + 16, :]
 
 
 def pick_columns():
@@ -122,11 +129,11 @@
 
 
 def main_body(
-    core, above, below, cot, preact_in, boxes_in, grad_act_in, w1_edge, w2_edge, x_hbm,
+    code, above, below, cot, preact_in, boxes_in, grad_act_in, w1_edge, w2_edge, x_hbm,
     delta_out, delta_first, delta_last, packed, send,
     x, boxes, ds, preact, grad_act, sems,
 ):
-    x_copy = start(x_hbm, x.at[COLS : COLS + PIX], sems.at[4])
+    x_copy = start(x_hbm, x.at[COLS : COLS + PIX], sems.at[1])
 
     boxes[...] = boxes_in[...]
     grad_act[...] = grad_act_in[...]
@@ -181,14 +188,10 @@
     row = lax.broadcasted_iota(jnp.int32, (16, 16, 128), 1)
     band = jnp.where(row == 0, jnp.broadcast_to(folded[:, None, :], (16, 16, 128)), 0.0)
     band = band.astype(BF16)
-    empty = jnp.zeros((16, 128), BF16)
     for d in range(16):
-        for row in range(3 * SLICE, PACK, 16):
-            half, chunk, z_hi, at = spot(d, row)
-            packed[half, chunk, z_hi, at : at + 16, :] = band[d] if row == 3 * SLICE else empty
-
-    mine = core[0]
-    copies = []
+        half, at = spot(d, TILES - 1)
+        packed[half, at // 32, at % 32 : at % 32 + 16, :] = band[d]
+
     x_copy.wait()
     for p in range(3):
         lhs = x[p * COLS : p * COLS + PIX, :]
@@ -197,12 +200,7 @@
             part = dot(lhs, ds[q], TN).astype(BF16)
             put(packed, 0, tap, part[:, 0:C2])
             put(packed, 1, tap, part[:, C2:C1])
-            if tap in (2, 4, 6, 8):
-                n = tap // 2 - 1
-                chunks = pl.ds(n * (PIECES // 2), PIECES // 2)
-                copies.append(start(packed.at[1 - mine, chunks], send.at[chunks], sems.at[n]))
-    for copy in copies:
-        copy.wait()
+    start(packed.at[1 - code[0] % 2], send, sems.at[0]).wait()
 
 
 VMEM = pl.BlockSpec(memory_space=pltpu.VMEM)
@@ -254,10 +252,7 @@
     )(cot, w2)
 
 
-PARTS = (2 * PIECES, 4, PIECE, 128)
-
-
-def main_work(core, above, below, cot, preact, boxes, grad_act, w1_edge, w2_edge, x):
+def main_work(code, above, below, cot, preact, boxes, grad_act, w1_edge, w2_edge, x):
     return pl.pallas_call(
         main_body,
         out_shape=(
@@ -275,28 +270,28 @@
             pltpu.VMEM((3, PIX, C1), BF16),
             pltpu.VMEM((PIX, C1), F32),
             pltpu.VMEM((PIX, C1), F32),
-            pltpu.SemaphoreType.DMA((5,)),
+            pltpu.SemaphoreType.DMA((2,)),
         ],
         compiler_params=pltpu.CompilerParams(vmem_limit_bytes=16 * 2**20),
         cost_estimate=pl.CostEstimate(
             flops=600_000_000, bytes_accessed=5_000_000, transcendentals=70_000
         ),
         name="main_work",
-    )(core, above, below, cot, preact, boxes, grad_act, w1_edge, w2_edge, x)
-
-
-def pair_body(core, packed, received, pair, total, sems):
-    mine = core[0]
+    )(code, above, below, cot, preact, boxes, grad_act, w1_edge, w2_edge, x)
+
+
+def pair_body(code, packed, received, pair, total, sems):
+    mine = code[0] % 2
     copies = []
     for n in range(4):
-        chunks = pl.ds(n * (PIECES // 2), PIECES // 2)
+        chunks = pl.ds(n * (CHUNK // 4), CHUNK // 4)
         total[chunks] = packed[mine, chunks] + received[chunks]
         copies.append(start(total.at[chunks], pair.at[chunks], sems.at[n]))
     for copy in copies:
         copy.wait()
 
 
-def pair_work(core, packed, received):
+def pair_work(code, packed, received):
     return pl.pallas_call(
         pair_body,
         out_shape=jax.ShapeDtypeStruct(PARTS, BF16),
@@ -305,25 +300,51 @@
         scratch_shapes=[pltpu.VMEM(PARTS, BF16), pltpu.SemaphoreType.DMA((4,))],
         compiler_params=pltpu.CompilerParams(vmem_limit_bytes=8 * 2**20),
         name="pair_work",
-    )(core, packed, received)
-
-
-def sum_body(copies, pieces, out):
+    )(code, packed, received)
+
+
+def block_body(code, pieces, out, total):
+    value = pieces[0].astype(F32)
+    for n in range(1, 32):
+        value = value + pieces[n].astype(F32)
+    tiles = CHUNK // 16
+    total[0:tiles] = value.reshape(tiles, 16, 128)
+    total[tiles] = jnp.zeros((16, 128), F32)
+    single = code[0] // 2 % 4
+    for z_hi in range(4):
+        part = total[pl.ds(2 * z_hi - jnp.where(z_hi > single, 1, 0), 2)]
+        for n in range(2):
+            out[n, z_hi] = part.reshape(PIECE).astype(BF16)
+
+
+def block_work(code, pieces):
+    return pl.pallas_call(
+        block_body,
+        out_shape=jax.ShapeDtypeStruct((2, 4) + PIECE, BF16),
+        in_specs=[SMEM, VMEM],
+        out_specs=VMEM,
+        scratch_shapes=[pltpu.VMEM((TILES // 4 + 1, 16, 128), F32)],
+        compiler_params=pltpu.CompilerParams(vmem_limit_bytes=4 * 2**20),
+        name="block_work",
+    )(code, pieces)
+
+
+def column_body(pieces, out):
     total = pieces[0].astype(F32)
     for n in range(1, pieces.shape[0]):
         total = total + pieces[n].astype(F32)
-    for n in range(copies):
+    for n in range(PIECES):
         out[n] = total.astype(BF16)
 
 
-def sum_work(pieces, copies):
-    return pl.pallas_call(
-        lambda *refs: sum_body(copies, *refs),
-        out_shape=jax.ShapeDtypeStruct((copies,) + pieces.shape[1:], BF16),
+def column_work(pieces):
+    return pl.pallas_call(
+        column_body,
+        out_shape=jax.ShapeDtypeStruct((PIECES,) + PIECE, BF16),
         in_specs=[VMEM],
         out_specs=VMEM,
         compiler_params=pltpu.CompilerParams(vmem_limit_bytes=4 * 2**20),
-        name="sum_work",
+        name="column_work",
     )(pieces)
 
 
@@ -366,17 +387,24 @@
     )(delta, above, below, w1)
 
 
-def unpack(scale_low, scale_high, full, first, second, bias):
-    def rows(start):
-        return full[start : start + SLICE, :].astype(F32)
-
-    first[:, 0:C2] = rows(0) * scale_low
-    first[:, C2:C1] = rows(SLICE) * scale_low
-    second[...] = rows(2 * SLICE) * scale_high
-    bias[...] = full[3 * SLICE : 3 * SLICE + 16, :].astype(F32)[0:1, 0:16] * scale_low
-
-
-def results(full, scale_low, scale_high):
+def unpack(scale_low, scale_high, code, full, first, second, bias, tiles):
+    z_hi = code[0] // 8
+    for half in range(2):
+        for k in range(8):
+            before = 2 * k - (k - z_hi + 3) // 4
+            piece = full[8 * half + k].astype(F32).reshape(2, 16, 128)
+            tiles[pl.ds(half * (TILES // 2) + before, 2)] = piece
+
+    def band(n):
+        return tiles[9 * n : 9 * n + 9].reshape(SLICE, 128)
+
+    first[:, 0:C2] = band(0) * scale_low
+    first[:, C2:C1] = band(1) * scale_low
+    second[...] = band(2) * scale_high
+    bias[...] = tiles[TILES - 1][0:1, 0:16] * scale_low
+
+
+def results(code, full, scale_low, scale_high):
     return pl.pallas_call(
         lambda *refs: unpack(scale_low, scale_high, *refs),
         out_shape=(
@@ -384,10 +412,11 @@
             jax.ShapeDtypeStruct((SLICE, C2), F32),
             jax.ShapeDtypeStruct((1, 16), F32),
         ),
-        in_specs=[pl.BlockSpec(memory_space=pltpu.VMEM)],
-        out_specs=(pl.BlockSpec(memory_space=pltpu.VMEM),) * 3,
+        in_specs=[SMEM, VMEM],
+        out_specs=(VMEM,) * 3,
+        scratch_shapes=[pltpu.VMEM((TILES + 1, 16, 128), F32)],
         name="unpack",
-    )(full)
+    )(code, full)
 
 
 FOUR = range(4)
@@ -431,7 +460,8 @@
 
     above = lax.ppermute(halo(cot[7:8], x[3]), "rows", down)
     below = lax.ppermute(halo(cot[0:1], x[0]), "rows", up)
-    core = (rank % 2).astype(jnp.int32).reshape(1)
+    code = rank % 2 + rank // 2 % 2 * 2 + rank // 8 % 2 * 4 + lax.axis_index("dp") % 4 * 8
+    code = code.astype(jnp.int32).reshape(1)
     x_flat, w1, bias, w2 = (
         pltpu.with_memory_space_constraint(value, pltpu.HBM)
         for value in (
@@ -445,26 +475,27 @@
     preact, w1_edge = conv_work(x_flat, w1, bias)
     boxes, grad_act, w2_edge = boxes_work(cot, w2)
     delta, delta_first, delta_last, packed, send = main_work(
-        core, above, below, cot, preact, boxes, grad_act, w1_edge, w2_edge, x_flat
+        code, above, below, cot, preact, boxes, grad_act, w1_edge, w2_edge, x_flat
     )
     received = lax.ppermute(send, "rows", [(i, i ^ 1) for i in range(32)])
     from_above = lax.ppermute(delta_last, "rows", down)
     from_below = lax.ppermute(delta_first, "rows", up)
 
-    pair = pair_work(core, packed, received)
+    pair = pair_work(code, packed, received)
+    pair = pair.reshape(32, CHUNK, 128)
     block = lax.all_to_all(pair, both, 0, 0, axis_index_groups=BLOCK)
     block, from_above, from_below = lax.optimization_barrier((block, from_above, from_below))
     grad_x = input_work(delta, from_above, from_below, w1)
-    spread = sum_work(block, 2).reshape(8, PIECE, 128)
+    spread = block_work(code, block).reshape((8,) + PIECE)
     column = lax.all_to_all(spread, both, 0, 0, axis_index_groups=COLUMN)
     column, grad_x = lax.optimization_barrier((column, grad_x))
-    full = lax.all_to_all(sum_work(column, PIECES), "rows", 0, 0, axis_index_groups=SHARE)
+    full = lax.all_to_all(column_work(column), "rows", 0, 0, axis_index_groups=SHARE)
 
     pixels_low = lax.axis_size("dp") * lax.axis_size("rows") * PIX
     scale_low = pixels_low ** (-0.5)
     scale_high = (4 * pixels_low) ** (-0.5)
-    full = pltpu.with_memory_space_constraint(full.reshape(PACK, 128), pltpu.VMEM)
-    grad_first, grad_second, grad_bias = results(full, scale_low, scale_high)
+    full = pltpu.with_memory_space_constraint(full, pltpu.VMEM)
+    grad_first, grad_second, grad_bias = results(code, full, scale_low, scale_high)
     grad_input = grad_x.reshape(1, ROWS, COLS, C1)
     return grad_input, grad_first, grad_second, grad_bias.reshape(16)
 

time: 96 us -> 94 us (0.979)
  waiting for transfers between devices: 32.7 us -> 30.5 us
    ppermute x1, waiting for transfers between devices: 6.61 us -> 5.2 us  [shards(): from_above = lax.ppermute(delta_last, 'rows', down)]
where the time goes in v4:
time: 94 us; the launch traced here: 93.3 us
  starting transfers between devices  39.2 us (42%)
  waiting for transfers between devices  30.5 us (32%)
  blocking collectives  11.8 us (13%)
  Pallas kernels  10.2 us (11%)
    all_to_all x1, starting transfers between devices, shards(): column = lax.all_to_all(spread, both, 0, 0, axis_index_groups=COLUMN)  13.3 us
    all_to_all x1, blocking collectives, shards(): lax.all_to_all(column_work(column), 'rows', 0, 0, axis_index_groups=SHARE)  11.8 us
    all_to_all x1, starting transfers between devices, shards(): cot = lax.all_to_all(cotangent, 'rows', 0, 0, axis_index_groups=QUADS)  10.3 us
    all_to_all x1, waiting for transfers between devices, shards(): column = lax.all_to_all(spread, both, 0, 0, axis_index_groups=COLUMN)  8.99 us
    all_to_all x1, waiting for transfers between devices, shards(): block = lax.all_to_all(pair, both, 0, 0, axis_index_groups=BLOCK)  6.88 us
    all_to_all x1, starting transfers between devices, shards(): block = lax.all_to_all(pair, both, 0, 0, axis_index_groups=BLOCK)  5.29 us
    ppermute x1, waiting for transfers between devices, shards(): from_above = lax.ppermute(delta_last, 'rows', down)  5.2 us
    all_to_all x1, waiting for transfers between devices, shards(): cot = lax.all_to_all(cotangent, 'rows', 0, 0, axis_index_groups=QUADS)  4.35 us
  transfers between devices with their start and end apart: 8, of which 6 were waited for; matrix products, arithmetic and copies ran while one was open for 1% of the time, Pallas kernels for 6%

profile of v4, /device:TPU:1, one launch (start us, length us, event | category | flops | bytes accessed | tf_op | source)
XLA Modules:
  0.0 93.3 jit_solution(16119809915364076376)
XLA Ops:
  0.6 10.3 %all-to-all-start = ((bf16[4,2,128,128]{3,2,1,0:T(8,128)(2,1)}), bf16[4,2,128,128]{3,2,1,0:T(8,128)(2,1)S(1)}, u32[]{:S(2)}, u32[]{:S(2)}) async-start(bf16[4,2,128,128]{3,2,1,0:T(8,128)(2,1)} %param.5), calls=%async_computation | async-start | bytes 524288 | tf_op jit(solution)/shard_map/all_to_all | solution.py:454
  10.9 0.8 slice_bitcast_fusion
  11.7 4.4 %all-to-all-done = bf16[4,2,128,128]{3,2,1,0:T(8,128)(2,1)S(1)} async-done(((bf16[4,2,128,128]{3,2,1,0:T(8,128)(2,1)}), bf16[4,2,128,128]{3,2,1,0:T(8,128)(2,1)S(1)}, u32[]{:S(2)}, u32[]{:S(2)}) %all-to-all-start) | async-done | bytes 262176 | tf_op jit(solution)/shard_map/all_to_all | solution.py:454
  16.1 1.3 %collective-permute-start = (bf16[2,128,128]{2,1,0:T(8,128)(2,1)S(1)}, bf16[2,128,128]{2,1,0:T(8,128)(2,1)S(1)}, u32[]{:S(2)}, u32[]{:S(2)}) collective-permute-start(bf16[2,128,128]{2,1,0:T(8,128)(2,1)S(1)} %pad_maximum_fusion), channel_id=1, source_target_pairs={{0,4},{1,5},{2,6},{3,7},{4,8},{5,9},{6,10},{7,11},{8,12},{9,13},{1... | collective-permute-start | bytes 196616 | tf_op jit(solution)/shard_map/ppermute | solution.py:461
  17.4 1.3 %collective-permute-start.1 = (bf16[2,128,128]{2,1,0:T(8,128)(2,1)S(1)}, bf16[2,128,128]{2,1,0:T(8,128)(2,1)S(1)}, u32[]{:S(2)}, u32[]{:S(2)}) collective-permute-start(bf16[2,128,128]{2,1,0:T(8,128)(2,1)S(1)} %pad_maximum_fusion.1), channel_id=1, source_target_pairs={{4,0},{5,1},{6,2},{7,3},{8,4},{9,5},{10,6},{11,7},{12,8},{13,9},{1... | collective-permute-start | bytes 196616 | tf_op jit(solution)/shard_map/ppermute | solution.py:462
  18.8 1.9 %conv_work.1 = (f32[256,256]{1,0:T(8,128)S(1)}, bf16[6,256,256]{2,1,0:T(8,128)(2,1)S(1)}) custom-call(bf16[256,256]{1,0:T(8,128)(2,1)} %bitcast.24, bf16[9,256,256]{2,1,0:T(8,128)(2,1)} %bitcast.22, f32[1,256]{1,0:T(1,128)} %bitcast.27), custom_call_target="tpu_custom_call" | custom-call | flops 300000000 | bytes 1500000 | tf_op jit(solution)/shard_map/conv_work/pallas_call | solution.py:213
  20.6 1.6 %boxes_work.1 = (bf16[256,1152]{1,0:T(8,128)(2,1)S(1)}, f32[256,256]{1,0:T(8,128)S(1)}, bf16[6,256,128]{2,1,0:T(8,128)(2,1)S(1)}) custom-call(bf16[1024,128]{1,0:T(8,128)(2,1)S(1)} %bitcast.20, bf16[9,256,128]{2,1,0:T(8,128)(2,1)} %bitcast.28), custom_call_target="tpu_custom_call" | custom-call | flops 300000000 | bytes 1500000 | tf_op jit(solution)/shard_map/boxes_work/pallas_call | solution.py:237
  22.2 0.0 collective-permute-done.above
  22.2 3.0 %collective-permute-done.1.below = bf16[2,128,128]{2,1,0:T(8,128)(2,1)S(1)} collective-permute-done((bf16[2,128,128]{2,1,0:T(8,128)(2,1)S(1)}, bf16[2,128,128]{2,1,0:T(8,128)(2,1)S(1)}, u32[]{:S(2)}, u32[]{:S(2)}) %collective-permute-start.1) | collective-permute-done | bytes 65568 | tf_op jit(solution)/shard_map/ppermute | solution.py:462
  25.2 1.8 %main_work.1 = (bf16[256,256]{1,0:T(8,128)(2,1)S(1)}, bf16[64,256]{1,0:T(8,128)(2,1)S(1)}, bf16[64,256]{1,0:T(8,128)(2,1)S(1)}, bf16[2,112,32,128]{3,2,1,0:T(8,128)(2,1)S(1)}, bf16[112,32,128]{2,1,0:T(8,128)(2,1)S(1)}) custom-call(s32[1]{0:T(128)} %bitcast.code.refs_0_, bf16[2,128,128]{2,1,0:T(8,128)(2,1)S(1)} %collective-permute-done.above, ...), custom_call_target="tpu_custom_call" | custom-call | flops 600000000 | bytes 5000000 | tf_op jit(solution)/shard_map/main_work/pallas_call | solution.py:256
  27.1 2.8 %collective-permute-start.2 = (bf16[112,32,128]{2,1,0:T(8,128)(2,1)S(1)}, bf16[112,32,128]{2,1,0:T(8,128)(2,1)S(1)}, u32[]{:S(2)}, u32[]{:S(2)}) collective-permute-start(bf16[112,32,128]{2,1,0:T(8,128)(2,1)S(1)} %get-tuple-element.28), channel_id=1, source_target_pairs={{0,1},{1,0},{2,3},{3,2},{4,5},{5,4},{6,7},{7,6},{8,9},{9,8},{10,11... | collective-permute-start | bytes 2752520 | tf_op jit(solution)/shard_map/ppermute | solution.py:480
  29.8 2.1 %collective-permute-done.2.received = bf16[112,32,128]{2,1,0:T(8,128)(2,1)S(1)} collective-permute-done((bf16[112,32,128]{2,1,0:T(8,128)(2,1)S(1)}, bf16[112,32,128]{2,1,0:T(8,128)(2,1)S(1)}, u32[]{:S(2)}, u32[]{:S(2)}) %collective-permute-start.2) | collective-permute-done | bytes 917536 | tf_op jit(solution)/shard_map/ppermute | solution.py:480
  31.9 1.0 %pair_work.1 = bf16[112,32,128]{2,1,0:T(8,128)(2,1)} custom-call(s32[1]{0:T(128)} %bitcast.code.refs_0_, bf16[2,112,32,128]{3,2,1,0:T(8,128)(2,1)S(1)} %get-tuple-element.27.packed, bf16[112,32,128]{2,1,0:T(8,128)(2,1)S(1)} %collective-permute-done.2.received), custom_call_target="tpu_custom_call" | custom-call | tf_op jit(solution)/shard_map/pair_work/pallas_call | solution.py:295
  32.9 5.3 %all-to-all-start.1 = ((bf16[32,112,128]{2,1,0:T(8,128)(2,1)}), bf16[32,112,128]{2,1,0:T(8,128)(2,1)S(1)}, u32[]{:S(2)}, u32[]{:S(2)}) async-start(bf16[32,112,128]{2,1,0:T(8,128)(2,1)} %bitcast.11), calls=%async_computation.1 | async-start | bytes 1835008 | tf_op jit(solution)/shard_map/all_to_all | solution.py:486
  38.2 3.7 %collective-permute-start.3 = (bf16[64,256]{1,0:T(8,128)(2,1)S(1)}, bf16[64,256]{1,0:T(8,128)(2,1)S(1)}, u32[]{:S(2)}, u32[]{:S(2)}) collective-permute-start(bf16[64,256]{1,0:T(8,128)(2,1)S(1)} %get-tuple-element.29), channel_id=1, source_target_pairs={{0,4},{1,5},{2,6},{3,7},{4,8},{5,9},{6,10},{7,11},{8,12},{9,13},{1... | collective-permute-start | bytes 98312 | tf_op jit(solution)/shard_map/ppermute | solution.py:481
  41.9 1.3 %collective-permute-start.4 = (bf16[64,256]{1,0:T(8,128)(2,1)S(1)}, bf16[64,256]{1,0:T(8,128)(2,1)S(1)}, u32[]{:S(2)}, u32[]{:S(2)}) collective-permute-start(bf16[64,256]{1,0:T(8,128)(2,1)S(1)} %get-tuple-element.30), channel_id=1, source_target_pairs={{4,0},{5,1},{6,2},{7,3},{8,4},{9,5},{10,6},{11,7},{12,8},{13,9},{1... | collective-permute-start | bytes 98312 | tf_op jit(solution)/shard_map/ppermute | solution.py:482
  43.2 5.2 %collective-permute-done.3.above = bf16[64,256]{1,0:T(8,128)(2,1)S(1)} collective-permute-done((bf16[64,256]{1,0:T(8,128)(2,1)S(1)}, bf16[64,256]{1,0:T(8,128)(2,1)S(1)}, u32[]{:S(2)}, u32[]{:S(2)}) %collective-permute-start.3) | collective-permute-done | bytes 32800 | tf_op jit(solution)/shard_map/ppermute | solution.py:481
  48.4 0.0 collective-permute-done.4.below
  48.4 6.9 %all-to-all-done.1.pieces = bf16[32,112,128]{2,1,0:T(8,128)(2,1)S(1)} async-done(((bf16[32,112,128]{2,1,0:T(8,128)(2,1)}), bf16[32,112,128]{2,1,0:T(8,128)(2,1)S(1)}, u32[]{:S(2)}, u32[]{:S(2)}) %all-to-all-start.1) | async-done | bytes 917536 | tf_op jit(solution)/shard_map/all_to_all | solution.py:486
  55.3 0.8 block_work.1
  56.1 13.3 %all-to-all-start.2 = ((bf16[8,32,128]{2,1,0:T(8,128)(2,1)}), bf16[8,32,128]{2,1,0:T(8,128)(2,1)S(1)}, u32[]{:S(2)}, u32[]{:S(2)}) async-start(bf16[8,32,128]{2,1,0:T(8,128)(2,1)} %bitcast.12), calls=%async_computation.2 | async-start | bytes 131072 | tf_op jit(solution)/shard_map/all_to_all | solution.py:490
  69.4 2.4 %input_work.1 = bf16[256,256]{1,0:T(8,128)(2,1)} custom-call(bf16[256,256]{1,0:T(8,128)(2,1)S(1)} %get-tuple-element.32.delta, bf16[64,256]{1,0:T(8,128)(2,1)S(1)} %collective-permute-done.3.above, bf16[64,256]{1,0:T(8,128)(2,1)S(1)} %collective-permute-done.4.below, bf16[9,256,256]{2,1,0:T(8,128)(2,1)} %bitcast.23), custom_call_target="tpu_custom_call" | custom-call | flops 300000000 | bytes 2000000 | tf_op jit(solution)/shard_map/input_work/pallas_call | solution.py:371
  71.8 9.0 %all-to-all-done.2.pieces = bf16[8,32,128]{2,1,0:T(8,128)(2,1)S(1)} async-done(((bf16[8,32,128]{2,1,0:T(8,128)(2,1)}), bf16[8,32,128]{2,1,0:T(8,128)(2,1)S(1)}, u32[]{:S(2)}, u32[]{:S(2)}) %all-to-all-start.2) | async-done | bytes 65568 | tf_op jit(solution)/shard_map/all_to_all | solution.py:490
  80.8 11.8 %all_to_all.20.refs_1_ = bf16[16,32,128]{2,1,0:T(8,128)(2,1)S(1)} all-to-all(bf16[16,32,128]{2,1,0:T(8,128)(2,1)S(1)} %column_work.1), channel_id=1, replica_groups={{0,2,8,10,16,18,24,26,1,3,9,11,17,19,25,27},{4,6,12,14,20,22,28,30,5,7,..., dimensions={0} | all-to-all | bytes 262144 | tf_op jit(solution)/shard_map/all_to_all | solution.py:492
  92.6 0.8 unpack.1
  (7 shorter events, 0.1 us)
Async XLA Ops:
  0.6 15.4 %all-to-all-start = ((bf16[4,2,128,128]{3,2,1,0:T(8,128)(2,1)}), bf16[4,2,128,128]{3,2,1,0:T(8,128)(2,1)S(1)}, u32[]{:S(2)}, u32[]{:S(2)}) async-start(bf16[4,2,128,128]{3,2,1,0:T(8,128)(2,1)} %param.5), calls=%async_computation | async-start | bytes 524288 | tf_op jit(solution)/shard_map/all_to_all | solution.py:454
  16.1 6.2 %collective-permute-start = (bf16[2,128,128]{2,1,0:T(8,128)(2,1)S(1)}, bf16[2,128,128]{2,1,0:T(8,128)(2,1)S(1)}, u32[]{:S(2)}, u32[]{:S(2)}) collective-permute-start(bf16[2,128,128]{2,1,0:T(8,128)(2,1)S(1)} %pad_maximum_fusion), channel_id=1, source_target_pairs={{0,4},{1,5},{2,6},{3,7},{4,8},{5,9},{6,10},{7,11},{8,12},{9,13},{1... | collective-permute-start | bytes 196616 | tf_op jit(solution)/shard_map/ppermute | solution.py:461
  17.4 7.8 %collective-permute-start.1 = (bf16[2,128,128]{2,1,0:T(8,128)(2,1)S(1)}, bf16[2,128,128]{2,1,0:T(8,128)(2,1)S(1)}, u32[]{:S(2)}, u32[]{:S(2)}) collective-permute-start(bf16[2,128,128]{2,1,0:T(8,128)(2,1)S(1)} %pad_maximum_fusion.1), channel_id=1, source_target_pairs={{4,0},{5,1},{6,2},{7,3},{8,4},{9,5},{10,6},{11,7},{12,8},{13,9},{1... | collective-permute-start | bytes 196616 | tf_op jit(solution)/shard_map/ppermute | solution.py:462
  27.1 4.9 %collective-permute-start.2 = (bf16[112,32,128]{2,1,0:T(8,128)(2,1)S(1)}, bf16[112,32,128]{2,1,0:T(8,128)(2,1)S(1)}, u32[]{:S(2)}, u32[]{:S(2)}) collective-permute-start(bf16[112,32,128]{2,1,0:T(8,128)(2,1)S(1)} %get-tuple-element.28), channel_id=1, source_target_pairs={{0,1},{1,0},{2,3},{3,2},{4,5},{5,4},{6,7},{7,6},{8,9},{9,8},{10,11... | collective-permute-start | bytes 2752520 | tf_op jit(solution)/shard_map/ppermute | solution.py:480
  32.9 22.4 %all-to-all-start.1 = ((bf16[32,112,128]{2,1,0:T(8,128)(2,1)}), bf16[32,112,128]{2,1,0:T(8,128)(2,1)S(1)}, u32[]{:S(2)}, u32[]{:S(2)}) async-start(bf16[32,112,128]{2,1,0:T(8,128)(2,1)} %bitcast.11), calls=%async_computation.1 | async-start | bytes 1835008 | tf_op jit(solution)/shard_map/all_to_all | solution.py:486
  38.2 10.2 %collective-permute-start.3 = (bf16[64,256]{1,0:T(8,128)(2,1)S(1)}, bf16[64,256]{1,0:T(8,128)(2,1)S(1)}, u32[]{:S(2)}, u32[]{:S(2)}) collective-permute-start(bf16[64,256]{1,0:T(8,128)(2,1)S(1)} %get-tuple-element.29), channel_id=1, source_target_pairs={{0,4},{1,5},{2,6},{3,7},{4,8},{5,9},{6,10},{7,11},{8,12},{9,13},{1... | collective-permute-start | bytes 98312 | tf_op jit(solution)/shard_map/ppermute | solution.py:481
  41.9 6.5 %collective-permute-start.4 = (bf16[64,256]{1,0:T(8,128)(2,1)S(1)}, bf16[64,256]{1,0:T(8,128)(2,1)S(1)}, u32[]{:S(2)}, u32[]{:S(2)}) collective-permute-start(bf16[64,256]{1,0:T(8,128)(2,1)S(1)} %get-tuple-element.30), channel_id=1, source_target_pairs={{4,0},{5,1},{6,2},{7,3},{8,4},{9,5},{10,6},{11,7},{12,8},{13,9},{1... | collective-permute-start | bytes 98312 | tf_op jit(solution)/shard_map/ppermute | solution.py:482
  56.1 24.7 %all-to-all-start.2 = ((bf16[8,32,128]{2,1,0:T(8,128)(2,1)}), bf16[8,32,128]{2,1,0:T(8,128)(2,1)S(1)}, u32[]{:S(2)}, u32[]{:S(2)}) async-start(bf16[8,32,128]{2,1,0:T(8,128)(2,1)} %bitcast.12), calls=%async_computation.2 | async-start | bytes 131072 | tf_op jit(solution)/shard_map/all_to_all | solution.py:490

commit v5 on v4

--- a/solution.py
+++ b/solution.py
@@ -16,6 +16,10 @@
 TILES = 28
 PIECE = (32, 128)
 PIECES = 16
+ORDER = [
+    26, 17, 11, 10, 28, 1, 5, 4, 7, 16, 9, 19, 30, 13, 22, 0,
+    21, 29, 6, 12, 20, 23, 14, 15, 3, 31, 2, 24, 25, 27, 18, 8,
+]
 CHUNK = 16 * TILES // 4
 PARTS = (CHUNK, 32, 128)
 
@@ -49,7 +53,7 @@
         tile -= tiles_of(k, z_hi)
         k += 1
     before = sum(tiles_of(k, z) for z in range(z_hi)) + tile
-    return half, CHUNK * (x * 8 + k) + 16 * before
+    return half, CHUNK * ORDER.index(x * 8 + k) + 16 * before
 
 
 def put(packed, band, tap, value):
@@ -428,7 +432,7 @@
 
 
 BLOCK = [
-    [place(x, zh, y, zb, za, c) for x in FOUR for y in FOUR for za in TWO]
+    [place(n // 8, zh, n // 2 % 4, zb, n % 2, c) for n in ORDER]
     for zh in FOUR
     for zb in TWO
     for c in TWO

time: 94 us -> 92.9 us (0.988)
  waiting for transfers between devices: 30.5 us -> 28.8 us
    all_to_all x1, waiting for transfers between devices: 6.88 us -> 4.64 us  [shards(): block = lax.all_to_all(pair, both, 0, 0, axis_index_groups=BLOCK)]
where the time goes in v5:
time: 92.9 us; the launch traced here: 92.2 us
  starting transfers between devices  39.2 us (42%)
  waiting for transfers between devices  28.8 us (31%)
  blocking collectives  12.3 us (13%)
  Pallas kernels  10.2 us (11%)
    all_to_all x1, starting transfers between devices, shards(): column = lax.all_to_all(spread, both, 0, 0, axis_index_groups=COLUMN)  13.3 us
    all_to_all x1, blocking collectives, shards(): lax.all_to_all(column_work(column), 'rows', 0, 0, axis_index_groups=SHARE)  12.3 us
    all_to_all x1, starting transfers between devices, shards(): cot = lax.all_to_all(cotangent, 'rows', 0, 0, axis_index_groups=QUADS)  10.3 us
    all_to_all x1, waiting for transfers between devices, shards(): column = lax.all_to_all(spread, both, 0, 0, axis_index_groups=COLUMN)  8.98 us
    all_to_all x1, starting transfers between devices, shards(): block = lax.all_to_all(pair, both, 0, 0, axis_index_groups=BLOCK)  6.03 us
    ppermute x1, waiting for transfers between devices, shards(): from_above = lax.ppermute(delta_last, 'rows', down)  5.73 us
    all_to_all x1, waiting for transfers between devices, shards(): block = lax.all_to_all(pair, both, 0, 0, axis_index_groups=BLOCK)  4.64 us
    all_to_all x1, waiting for transfers between devices, shards(): cot = lax.all_to_all(cotangent, 'rows', 0, 0, axis_index_groups=QUADS)  4.35 us
  transfers between devices with their start and end apart: 8, of which 6 were waited for; matrix products, arithmetic and copies ran while one was open for 1% of the time, Pallas kernels for 6%

profile of v5, /device:TPU:1, one launch (start us, length us, event | category | flops | bytes accessed | tf_op | source)
XLA Modules:
  0.0 92.2 jit_solution(6336567665091264554)
XLA Ops:
  0.6 10.3 %all-to-all-start = ((bf16[4,2,128,128]{3,2,1,0:T(8,128)(2,1)}), bf16[4,2,128,128]{3,2,1,0:T(8,128)(2,1)S(1)}, u32[]{:S(2)}, u32[]{:S(2)}) async-start(bf16[4,2,128,128]{3,2,1,0:T(8,128)(2,1)} %param.5), calls=%async_computation | async-start | bytes 524288 | tf_op jit(solution)/shard_map/all_to_all | solution.py:458
  10.9 0.8 slice_bitcast_fusion
  11.7 4.4 %all-to-all-done = bf16[4,2,128,128]{3,2,1,0:T(8,128)(2,1)S(1)} async-done(((bf16[4,2,128,128]{3,2,1,0:T(8,128)(2,1)}), bf16[4,2,128,128]{3,2,1,0:T(8,128)(2,1)S(1)}, u32[]{:S(2)}, u32[]{:S(2)}) %all-to-all-start) | async-done | bytes 262176 | tf_op jit(solution)/shard_map/all_to_all | solution.py:458
  16.1 1.3 %collective-permute-start = (bf16[2,128,128]{2,1,0:T(8,128)(2,1)S(1)}, bf16[2,128,128]{2,1,0:T(8,128)(2,1)S(1)}, u32[]{:S(2)}, u32[]{:S(2)}) collective-permute-start(bf16[2,128,128]{2,1,0:T(8,128)(2,1)S(1)} %pad_maximum_fusion), channel_id=1, source_target_pairs={{0,4},{1,5},{2,6},{3,7},{4,8},{5,9},{6,10},{7,11},{8,12},{9,13},{1... | collective-permute-start | bytes 196616 | tf_op jit(solution)/shard_map/ppermute | solution.py:465
  17.4 1.3 %collective-permute-start.1 = (bf16[2,128,128]{2,1,0:T(8,128)(2,1)S(1)}, bf16[2,128,128]{2,1,0:T(8,128)(2,1)S(1)}, u32[]{:S(2)}, u32[]{:S(2)}) collective-permute-start(bf16[2,128,128]{2,1,0:T(8,128)(2,1)S(1)} %pad_maximum_fusion.1), channel_id=1, source_target_pairs={{4,0},{5,1},{6,2},{7,3},{8,4},{9,5},{10,6},{11,7},{12,8},{13,9},{1... | collective-permute-start | bytes 196616 | tf_op jit(solution)/shard_map/ppermute | solution.py:466
  18.8 1.9 %conv_work.1 = (f32[256,256]{1,0:T(8,128)S(1)}, bf16[6,256,256]{2,1,0:T(8,128)(2,1)S(1)}) custom-call(bf16[256,256]{1,0:T(8,128)(2,1)} %bitcast.24, bf16[9,256,256]{2,1,0:T(8,128)(2,1)} %bitcast.22, f32[1,256]{1,0:T(1,128)} %bitcast.27), custom_call_target="tpu_custom_call" | custom-call | flops 300000000 | bytes 1500000 | tf_op jit(solution)/shard_map/conv_work/pallas_call | solution.py:217
  20.6 1.6 %boxes_work.1 = (bf16[256,1152]{1,0:T(8,128)(2,1)S(1)}, f32[256,256]{1,0:T(8,128)S(1)}, bf16[6,256,128]{2,1,0:T(8,128)(2,1)S(1)}) custom-call(bf16[1024,128]{1,0:T(8,128)(2,1)S(1)} %bitcast.20, bf16[9,256,128]{2,1,0:T(8,128)(2,1)} %bitcast.28), custom_call_target="tpu_custom_call" | custom-call | flops 300000000 | bytes 1500000 | tf_op jit(solution)/shard_map/boxes_work/pallas_call | solution.py:241
  22.2 0.0 collective-permute-done.above
  22.2 3.0 %collective-permute-done.1.below = bf16[2,128,128]{2,1,0:T(8,128)(2,1)S(1)} collective-permute-done((bf16[2,128,128]{2,1,0:T(8,128)(2,1)S(1)}, bf16[2,128,128]{2,1,0:T(8,128)(2,1)S(1)}, u32[]{:S(2)}, u32[]{:S(2)}) %collective-permute-start.1) | collective-permute-done | bytes 65568 | tf_op jit(solution)/shard_map/ppermute | solution.py:466
  25.2 1.8 %main_work.1 = (bf16[256,256]{1,0:T(8,128)(2,1)S(1)}, bf16[64,256]{1,0:T(8,128)(2,1)S(1)}, bf16[64,256]{1,0:T(8,128)(2,1)S(1)}, bf16[2,112,32,128]{3,2,1,0:T(8,128)(2,1)S(1)}, bf16[112,32,128]{2,1,0:T(8,128)(2,1)S(1)}) custom-call(s32[1]{0:T(128)} %bitcast.code.refs_0_, bf16[2,128,128]{2,1,0:T(8,128)(2,1)S(1)} %collective-permute-done.above, ...), custom_call_target="tpu_custom_call" | custom-call | flops 600000000 | bytes 5000000 | tf_op jit(solution)/shard_map/main_work/pallas_call | solution.py:260
  27.1 2.8 %collective-permute-start.2 = (bf16[112,32,128]{2,1,0:T(8,128)(2,1)S(1)}, bf16[112,32,128]{2,1,0:T(8,128)(2,1)S(1)}, u32[]{:S(2)}, u32[]{:S(2)}) collective-permute-start(bf16[112,32,128]{2,1,0:T(8,128)(2,1)S(1)} %get-tuple-element.28), channel_id=1, source_target_pairs={{0,1},{1,0},{2,3},{3,2},{4,5},{5,4},{6,7},{7,6},{8,9},{9,8},{10,11... | collective-permute-start | bytes 2752520 | tf_op jit(solution)/shard_map/ppermute | solution.py:484
  29.8 2.1 %collective-permute-done.2.received = bf16[112,32,128]{2,1,0:T(8,128)(2,1)S(1)} collective-permute-done((bf16[112,32,128]{2,1,0:T(8,128)(2,1)S(1)}, bf16[112,32,128]{2,1,0:T(8,128)(2,1)S(1)}, u32[]{:S(2)}, u32[]{:S(2)}) %collective-permute-start.2) | collective-permute-done | bytes 917536 | tf_op jit(solution)/shard_map/ppermute | solution.py:484
  31.9 1.0 %pair_work.1 = bf16[112,32,128]{2,1,0:T(8,128)(2,1)} custom-call(s32[1]{0:T(128)} %bitcast.code.refs_0_, bf16[2,112,32,128]{3,2,1,0:T(8,128)(2,1)S(1)} %get-tuple-element.27.packed, bf16[112,32,128]{2,1,0:T(8,128)(2,1)S(1)} %collective-permute-done.2.received), custom_call_target="tpu_custom_call" | custom-call | tf_op jit(solution)/shard_map/pair_work/pallas_call | solution.py:299
  32.9 6.0 %all-to-all-start.1 = ((bf16[32,112,128]{2,1,0:T(8,128)(2,1)}), bf16[32,112,128]{2,1,0:T(8,128)(2,1)S(1)}, u32[]{:S(2)}, u32[]{:S(2)}) async-start(bf16[32,112,128]{2,1,0:T(8,128)(2,1)} %bitcast.11), calls=%async_computation.1 | async-start | bytes 1835008 | tf_op jit(solution)/shard_map/all_to_all | solution.py:490
  39.0 3.0 %collective-permute-start.3 = (bf16[64,256]{1,0:T(8,128)(2,1)S(1)}, bf16[64,256]{1,0:T(8,128)(2,1)S(1)}, u32[]{:S(2)}, u32[]{:S(2)}) collective-permute-start(bf16[64,256]{1,0:T(8,128)(2,1)S(1)} %get-tuple-element.29), channel_id=1, source_target_pairs={{0,4},{1,5},{2,6},{3,7},{4,8},{5,9},{6,10},{7,11},{8,12},{9,13},{1... | collective-permute-start | bytes 98312 | tf_op jit(solution)/shard_map/ppermute | solution.py:485
  42.0 1.3 %collective-permute-start.4 = (bf16[64,256]{1,0:T(8,128)(2,1)S(1)}, bf16[64,256]{1,0:T(8,128)(2,1)S(1)}, u32[]{:S(2)}, u32[]{:S(2)}) collective-permute-start(bf16[64,256]{1,0:T(8,128)(2,1)S(1)} %get-tuple-element.30), channel_id=1, source_target_pairs={{4,0},{5,1},{6,2},{7,3},{8,4},{9,5},{10,6},{11,7},{12,8},{13,9},{1... | collective-permute-start | bytes 98312 | tf_op jit(solution)/shard_map/ppermute | solution.py:486
  43.3 5.7 %collective-permute-done.3.above = bf16[64,256]{1,0:T(8,128)(2,1)S(1)} collective-permute-done((bf16[64,256]{1,0:T(8,128)(2,1)S(1)}, bf16[64,256]{1,0:T(8,128)(2,1)S(1)}, u32[]{:S(2)}, u32[]{:S(2)}) %collective-permute-start.3) | collective-permute-done | bytes 32800 | tf_op jit(solution)/shard_map/ppermute | solution.py:485
  49.0 0.0 collective-permute-done.4.below
  49.0 4.6 %all-to-all-done.1.pieces = bf16[32,112,128]{2,1,0:T(8,128)(2,1)S(1)} async-done(((bf16[32,112,128]{2,1,0:T(8,128)(2,1)}), bf16[32,112,128]{2,1,0:T(8,128)(2,1)S(1)}, u32[]{:S(2)}, u32[]{:S(2)}) %all-to-all-start.1) | async-done | bytes 917536 | tf_op jit(solution)/shard_map/all_to_all | solution.py:490
  53.6 0.8 block_work.1
  54.4 13.3 %all-to-all-start.2 = ((bf16[8,32,128]{2,1,0:T(8,128)(2,1)}), bf16[8,32,128]{2,1,0:T(8,128)(2,1)S(1)}, u32[]{:S(2)}, u32[]{:S(2)}) async-start(bf16[8,32,128]{2,1,0:T(8,128)(2,1)} %bitcast.12), calls=%async_computation.2 | async-start | bytes 131072 | tf_op jit(solution)/shard_map/all_to_all | solution.py:494
  67.7 2.4 %input_work.1 = bf16[256,256]{1,0:T(8,128)(2,1)} custom-call(bf16[256,256]{1,0:T(8,128)(2,1)S(1)} %get-tuple-element.32.delta, bf16[64,256]{1,0:T(8,128)(2,1)S(1)} %collective-permute-done.3.above, bf16[64,256]{1,0:T(8,128)(2,1)S(1)} %collective-permute-done.4.below, bf16[9,256,256]{2,1,0:T(8,128)(2,1)} %bitcast.23), custom_call_target="tpu_custom_call" | custom-call | flops 300000000 | bytes 2000000 | tf_op jit(solution)/shard_map/input_work/pallas_call | solution.py:375
  70.1 9.0 %all-to-all-done.2.pieces = bf16[8,32,128]{2,1,0:T(8,128)(2,1)S(1)} async-done(((bf16[8,32,128]{2,1,0:T(8,128)(2,1)}), bf16[8,32,128]{2,1,0:T(8,128)(2,1)S(1)}, u32[]{:S(2)}, u32[]{:S(2)}) %all-to-all-start.2) | async-done | bytes 65568 | tf_op jit(solution)/shard_map/all_to_all | solution.py:494
  79.1 12.3 %all_to_all.20.refs_1_ = bf16[16,32,128]{2,1,0:T(8,128)(2,1)S(1)} all-to-all(bf16[16,32,128]{2,1,0:T(8,128)(2,1)S(1)} %column_work.1), channel_id=1, replica_groups={{0,2,8,10,16,18,24,26,1,3,9,11,17,19,25,27},{4,6,12,14,20,22,28,30,5,7,..., dimensions={0} | all-to-all | bytes 262144 | tf_op jit(solution)/shard_map/all_to_all | solution.py:496
  91.5 0.8 unpack.1
  (7 shorter events, 0.1 us)
Async XLA Ops:
  0.6 15.4 %all-to-all-start = ((bf16[4,2,128,128]{3,2,1,0:T(8,128)(2,1)}), bf16[4,2,128,128]{3,2,1,0:T(8,128)(2,1)S(1)}, u32[]{:S(2)}, u32[]{:S(2)}) async-start(bf16[4,2,128,128]{3,2,1,0:T(8,128)(2,1)} %param.5), calls=%async_computation | async-start | bytes 524288 | tf_op jit(solution)/shard_map/all_to_all | solution.py:458
  16.1 6.2 %collective-permute-start = (bf16[2,128,128]{2,1,0:T(8,128)(2,1)S(1)}, bf16[2,128,128]{2,1,0:T(8,128)(2,1)S(1)}, u32[]{:S(2)}, u32[]{:S(2)}) collective-permute-start(bf16[2,128,128]{2,1,0:T(8,128)(2,1)S(1)} %pad_maximum_fusion), channel_id=1, source_target_pairs={{0,4},{1,5},{2,6},{3,7},{4,8},{5,9},{6,10},{7,11},{8,12},{9,13},{1... | collective-permute-start | bytes 196616 | tf_op jit(solution)/shard_map/ppermute | solution.py:465
  17.4 7.8 %collective-permute-start.1 = (bf16[2,128,128]{2,1,0:T(8,128)(2,1)S(1)}, bf16[2,128,128]{2,1,0:T(8,128)(2,1)S(1)}, u32[]{:S(2)}, u32[]{:S(2)}) collective-permute-start(bf16[2,128,128]{2,1,0:T(8,128)(2,1)S(1)} %pad_maximum_fusion.1), channel_id=1, source_target_pairs={{4,0},{5,1},{6,2},{7,3},{8,4},{9,5},{10,6},{11,7},{12,8},{13,9},{1... | collective-permute-start | bytes 196616 | tf_op jit(solution)/shard_map/ppermute | solution.py:466
  27.1 4.9 %collective-permute-start.2 = (bf16[112,32,128]{2,1,0:T(8,128)(2,1)S(1)}, bf16[112,32,128]{2,1,0:T(8,128)(2,1)S(1)}, u32[]{:S(2)}, u32[]{:S(2)}) collective-permute-start(bf16[112,32,128]{2,1,0:T(8,128)(2,1)S(1)} %get-tuple-element.28), channel_id=1, source_target_pairs={{0,1},{1,0},{2,3},{3,2},{4,5},{5,4},{6,7},{7,6},{8,9},{9,8},{10,11... | collective-permute-start | bytes 2752520 | tf_op jit(solution)/shard_map/ppermute | solution.py:484
  32.9 20.7 %all-to-all-start.1 = ((bf16[32,112,128]{2,1,0:T(8,128)(2,1)}), bf16[32,112,128]{2,1,0:T(8,128)(2,1)S(1)}, u32[]{:S(2)}, u32[]{:S(2)}) async-start(bf16[32,112,128]{2,1,0:T(8,128)(2,1)} %bitcast.11), calls=%async_computation.1 | async-start | bytes 1835008 | tf_op jit(solution)/shard_map/all_to_all | solution.py:490
  39.0 10.0 %collective-permute-start.3 = (bf16[64,256]{1,0:T(8,128)(2,1)S(1)}, bf16[64,256]{1,0:T(8,128)(2,1)S(1)}, u32[]{:S(2)}, u32[]{:S(2)}) collective-permute-start(bf16[64,256]{1,0:T(8,128)(2,1)S(1)} %get-tuple-element.29), channel_id=1, source_target_pairs={{0,4},{1,5},{2,6},{3,7},{4,8},{5,9},{6,10},{7,11},{8,12},{9,13},{1... | collective-permute-start | bytes 98312 | tf_op jit(solution)/shard_map/ppermute | solution.py:485
  42.0 7.0 %collective-permute-start.4 = (bf16[64,256]{1,0:T(8,128)(2,1)S(1)}, bf16[64,256]{1,0:T(8,128)(2,1)S(1)}, u32[]{:S(2)}, u32[]{:S(2)}) collective-permute-start(bf16[64,256]{1,0:T(8,128)(2,1)S(1)} %get-tuple-element.30), channel_id=1, source_target_pairs={{4,0},{5,1},{6,2},{7,3},{8,4},{9,5},{10,6},{11,7},{12,8},{13,9},{1... | collective-permute-start | bytes 98312 | tf_op jit(solution)/shard_map/ppermute | solution.py:486
  54.4 24.7 %all-to-all-start.2 = ((bf16[8,32,128]{2,1,0:T(8,128)(2,1)}), bf16[8,32,128]{2,1,0:T(8,128)(2,1)S(1)}, u32[]{:S(2)}, u32[]{:S(2)}) async-start(bf16[8,32,128]{2,1,0:T(8,128)(2,1)} %bitcast.12), calls=%async_computation.2 | async-start | bytes 131072 | tf_op jit(solution)/shard_map/all_to_all | solution.py:494

commit v6 on v5

--- a/solution.py
+++ b/solution.py
@@ -317,14 +317,15 @@
     single = code[0] // 2 % 4
     for z_hi in range(4):
         part = total[pl.ds(2 * z_hi - jnp.where(z_hi > single, 1, 0), 2)]
-        for n in range(2):
-            out[n, z_hi] = part.reshape(PIECE).astype(BF16)
+        for n, (target, _) in enumerate(Z_ORDER):
+            if target == z_hi:
+                out[n] = part.reshape(PIECE).astype(BF16)
 
 
 def block_work(code, pieces):
     return pl.pallas_call(
         block_body,
-        out_shape=jax.ShapeDtypeStruct((2, 4) + PIECE, BF16),
+        out_shape=jax.ShapeDtypeStruct((8,) + PIECE, BF16),
         in_specs=[SMEM, VMEM],
         out_specs=VMEM,
         scratch_shapes=[pltpu.VMEM((TILES // 4 + 1, 16, 128), F32)],
@@ -437,8 +438,9 @@
     for zb in TWO
     for c in TWO
 ]
+Z_ORDER = [(0, 0), (2, 0), (0, 1), (2, 1), (1, 0), (3, 0), (1, 1), (3, 1)]
 COLUMN = [
-    [place(x, zh, y, zb, za, c) for zb in TWO for zh in FOUR]
+    [place(x, zh, y, zb, za, c) for zh, zb in Z_ORDER]
     for x in FOUR
     for y in FOUR
     for za in TWO
@@ -490,7 +492,7 @@
     block = lax.all_to_all(pair, both, 0, 0, axis_index_groups=BLOCK)
     block, from_above, from_below = lax.optimization_barrier((block, from_above, from_below))
     grad_x = input_work(delta, from_above, from_below, w1)
-    spread = block_work(code, block).reshape((8,) + PIECE)
+    spread = block_work(code, block)
     column = lax.all_to_all(spread, both, 0, 0, axis_index_groups=COLUMN)
     column, grad_x = lax.optimization_barrier((column, grad_x))
     full = lax.all_to_all(column_work(column), "rows", 0, 0, axis_index_groups=SHARE)

time: 92.9 us -> 92.5 us (level)
  no operation moved by 1% of the time
where the time goes in v6:
time: 92.5 us; the launch traced here: 91.8 us
  starting transfers between devices  39.2 us (42%)
  waiting for transfers between devices  28.8 us (31%)
  blocking collectives  11.9 us (13%)
  Pallas kernels  10.2 us (11%)
    all_to_all x1, starting transfers between devices, shards(): column = lax.all_to_all(spread, both, 0, 0, axis_index_groups=COLUMN)  13.3 us
    all_to_all x1, blocking collectives, shards(): lax.all_to_all(column_work(column), 'rows', 0, 0, axis_index_groups=SHARE)  11.9 us
    all_to_all x1, starting transfers between devices, shards(): cot = lax.all_to_all(cotangent, 'rows', 0, 0, axis_index_groups=QUADS)  10.3 us
    all_to_all x1, waiting for transfers between devices, shards(): column = lax.all_to_all(spread, both, 0, 0, axis_index_groups=COLUMN)  8.98 us
    all_to_all x1, starting transfers between devices, shards(): block = lax.all_to_all(pair, both, 0, 0, axis_index_groups=BLOCK)  6.03 us
    ppermute x1, waiting for transfers between devices, shards(): from_above = lax.ppermute(delta_last, 'rows', down)  5.73 us
    all_to_all x1, waiting for transfers between devices, shards(): block = lax.all_to_all(pair, both, 0, 0, axis_index_groups=BLOCK)  4.64 us
    all_to_all x1, waiting for transfers between devices, shards(): cot = lax.all_to_all(cotangent, 'rows', 0, 0, axis_index_groups=QUADS)  4.35 us
  transfers between devices with their start and end apart: 8, of which 6 were waited for; matrix products, arithmetic and copies ran while one was open for 1% of the time, Pallas kernels for 6%

profile of v6, /device:TPU:1, one launch (start us, length us, event | category | flops | bytes accessed | tf_op | source)
XLA Modules:
  0.0 91.8 jit_solution(4416345404727906582)
XLA Ops:
  0.6 10.3 %all-to-all-start = ((bf16[4,2,128,128]{3,2,1,0:T(8,128)(2,1)}), bf16[4,2,128,128]{3,2,1,0:T(8,128)(2,1)S(1)}, u32[]{:S(2)}, u32[]{:S(2)}) async-start(bf16[4,2,128,128]{3,2,1,0:T(8,128)(2,1)} %param.5), calls=%async_computation | async-start | bytes 524288 | tf_op jit(solution)/shard_map/all_to_all | solution.py:460
  10.9 0.8 slice_bitcast_fusion
  11.7 4.4 %all-to-all-done = bf16[4,2,128,128]{3,2,1,0:T(8,128)(2,1)S(1)} async-done(((bf16[4,2,128,128]{3,2,1,0:T(8,128)(2,1)}), bf16[4,2,128,128]{3,2,1,0:T(8,128)(2,1)S(1)}, u32[]{:S(2)}, u32[]{:S(2)}) %all-to-all-start) | async-done | bytes 262176 | tf_op jit(solution)/shard_map/all_to_all | solution.py:460
  16.1 1.3 %collective-permute-start = (bf16[2,128,128]{2,1,0:T(8,128)(2,1)S(1)}, bf16[2,128,128]{2,1,0:T(8,128)(2,1)S(1)}, u32[]{:S(2)}, u32[]{:S(2)}) collective-permute-start(bf16[2,128,128]{2,1,0:T(8,128)(2,1)S(1)} %pad_maximum_fusion), channel_id=1, source_target_pairs={{0,4},{1,5},{2,6},{3,7},{4,8},{5,9},{6,10},{7,11},{8,12},{9,13},{1... | collective-permute-start | bytes 196616 | tf_op jit(solution)/shard_map/ppermute | solution.py:467
  17.4 1.3 %collective-permute-start.1 = (bf16[2,128,128]{2,1,0:T(8,128)(2,1)S(1)}, bf16[2,128,128]{2,1,0:T(8,128)(2,1)S(1)}, u32[]{:S(2)}, u32[]{:S(2)}) collective-permute-start(bf16[2,128,128]{2,1,0:T(8,128)(2,1)S(1)} %pad_maximum_fusion.1), channel_id=1, source_target_pairs={{4,0},{5,1},{6,2},{7,3},{8,4},{9,5},{10,6},{11,7},{12,8},{13,9},{1... | collective-permute-start | bytes 196616 | tf_op jit(solution)/shard_map/ppermute | solution.py:468
  18.8 1.9 %conv_work.1 = (f32[256,256]{1,0:T(8,128)S(1)}, bf16[6,256,256]{2,1,0:T(8,128)(2,1)S(1)}) custom-call(bf16[256,256]{1,0:T(8,128)(2,1)} %bitcast.23, bf16[9,256,256]{2,1,0:T(8,128)(2,1)} %bitcast.21, f32[1,256]{1,0:T(1,128)} %bitcast.26), custom_call_target="tpu_custom_call" | custom-call | flops 300000000 | bytes 1500000 | tf_op jit(solution)/shard_map/conv_work/pallas_call | solution.py:217
  20.6 1.6 %boxes_work.1 = (bf16[256,1152]{1,0:T(8,128)(2,1)S(1)}, f32[256,256]{1,0:T(8,128)S(1)}, bf16[6,256,128]{2,1,0:T(8,128)(2,1)S(1)}) custom-call(bf16[1024,128]{1,0:T(8,128)(2,1)S(1)} %bitcast.19, bf16[9,256,128]{2,1,0:T(8,128)(2,1)} %bitcast.27), custom_call_target="tpu_custom_call" | custom-call | flops 300000000 | bytes 1500000 | tf_op jit(solution)/shard_map/boxes_work/pallas_call | solution.py:241
  22.2 0.0 collective-permute-done.above
  22.2 3.0 %collective-permute-done.1.below = bf16[2,128,128]{2,1,0:T(8,128)(2,1)S(1)} collective-permute-done((bf16[2,128,128]{2,1,0:T(8,128)(2,1)S(1)}, bf16[2,128,128]{2,1,0:T(8,128)(2,1)S(1)}, u32[]{:S(2)}, u32[]{:S(2)}) %collective-permute-start.1) | collective-permute-done | bytes 65568 | tf_op jit(solution)/shard_map/ppermute | solution.py:468
  25.2 1.8 %main_work.1 = (bf16[256,256]{1,0:T(8,128)(2,1)S(1)}, bf16[64,256]{1,0:T(8,128)(2,1)S(1)}, bf16[64,256]{1,0:T(8,128)(2,1)S(1)}, bf16[2,112,32,128]{3,2,1,0:T(8,128)(2,1)S(1)}, bf16[112,32,128]{2,1,0:T(8,128)(2,1)S(1)}) custom-call(s32[1]{0:T(128)} %bitcast.code.refs_0_, bf16[2,128,128]{2,1,0:T(8,128)(2,1)S(1)} %collective-permute-done.above, ...), custom_call_target="tpu_custom_call" | custom-call | flops 600000000 | bytes 5000000 | tf_op jit(solution)/shard_map/main_work/pallas_call | solution.py:260
  27.1 2.8 %collective-permute-start.2 = (bf16[112,32,128]{2,1,0:T(8,128)(2,1)S(1)}, bf16[112,32,128]{2,1,0:T(8,128)(2,1)S(1)}, u32[]{:S(2)}, u32[]{:S(2)}) collective-permute-start(bf16[112,32,128]{2,1,0:T(8,128)(2,1)S(1)} %get-tuple-element.28), channel_id=1, source_target_pairs={{0,1},{1,0},{2,3},{3,2},{4,5},{5,4},{6,7},{7,6},{8,9},{9,8},{10,11... | collective-permute-start | bytes 2752520 | tf_op jit(solution)/shard_map/ppermute | solution.py:486
  29.8 2.1 %collective-permute-done.2.received = bf16[112,32,128]{2,1,0:T(8,128)(2,1)S(1)} collective-permute-done((bf16[112,32,128]{2,1,0:T(8,128)(2,1)S(1)}, bf16[112,32,128]{2,1,0:T(8,128)(2,1)S(1)}, u32[]{:S(2)}, u32[]{:S(2)}) %collective-permute-start.2) | collective-permute-done | bytes 917536 | tf_op jit(solution)/shard_map/ppermute | solution.py:486
  31.9 1.0 %pair_work.1 = bf16[112,32,128]{2,1,0:T(8,128)(2,1)} custom-call(s32[1]{0:T(128)} %bitcast.code.refs_0_, bf16[2,112,32,128]{3,2,1,0:T(8,128)(2,1)S(1)} %get-tuple-element.27.packed, bf16[112,32,128]{2,1,0:T(8,128)(2,1)S(1)} %collective-permute-done.2.received), custom_call_target="tpu_custom_call" | custom-call | tf_op jit(solution)/shard_map/pair_work/pallas_call | solution.py:299
  32.9 6.0 %all-to-all-start.1 = ((bf16[32,112,128]{2,1,0:T(8,128)(2,1)}), bf16[32,112,128]{2,1,0:T(8,128)(2,1)S(1)}, u32[]{:S(2)}, u32[]{:S(2)}) async-start(bf16[32,112,128]{2,1,0:T(8,128)(2,1)} %bitcast.11), calls=%async_computation.1 | async-start | bytes 1835008 | tf_op jit(solution)/shard_map/all_to_all | solution.py:492
  39.0 3.0 %collective-permute-start.3 = (bf16[64,256]{1,0:T(8,128)(2,1)S(1)}, bf16[64,256]{1,0:T(8,128)(2,1)S(1)}, u32[]{:S(2)}, u32[]{:S(2)}) collective-permute-start(bf16[64,256]{1,0:T(8,128)(2,1)S(1)} %get-tuple-element.29), channel_id=1, source_target_pairs={{0,4},{1,5},{2,6},{3,7},{4,8},{5,9},{6,10},{7,11},{8,12},{9,13},{1... | collective-permute-start | bytes 98312 | tf_op jit(solution)/shard_map/ppermute | solution.py:487
  42.0 1.3 %collective-permute-start.4 = (bf16[64,256]{1,0:T(8,128)(2,1)S(1)}, bf16[64,256]{1,0:T(8,128)(2,1)S(1)}, u32[]{:S(2)}, u32[]{:S(2)}) collective-permute-start(bf16[64,256]{1,0:T(8,128)(2,1)S(1)} %get-tuple-element.30), channel_id=1, source_target_pairs={{4,0},{5,1},{6,2},{7,3},{8,4},{9,5},{10,6},{11,7},{12,8},{13,9},{1... | collective-permute-start | bytes 98312 | tf_op jit(solution)/shard_map/ppermute | solution.py:488
  43.3 5.7 %collective-permute-done.3.above = bf16[64,256]{1,0:T(8,128)(2,1)S(1)} collective-permute-done((bf16[64,256]{1,0:T(8,128)(2,1)S(1)}, bf16[64,256]{1,0:T(8,128)(2,1)S(1)}, u32[]{:S(2)}, u32[]{:S(2)}) %collective-permute-start.3) | collective-permute-done | bytes 32800 | tf_op jit(solution)/shard_map/ppermute | solution.py:487
  49.0 0.0 collective-permute-done.4.below
  49.0 4.6 %all-to-all-done.1.pieces = bf16[32,112,128]{2,1,0:T(8,128)(2,1)S(1)} async-done(((bf16[32,112,128]{2,1,0:T(8,128)(2,1)}), bf16[32,112,128]{2,1,0:T(8,128)(2,1)S(1)}, u32[]{:S(2)}, u32[]{:S(2)}) %all-to-all-start.1) | async-done | bytes 917536 | tf_op jit(solution)/shard_map/all_to_all | solution.py:492
  53.6 0.8 block_work.1
  54.4 13.3 %all-to-all-start.2 = ((bf16[8,32,128]{2,1,0:T(8,128)(2,1)}), bf16[8,32,128]{2,1,0:T(8,128)(2,1)S(1)}, u32[]{:S(2)}, u32[]{:S(2)}) async-start(bf16[8,32,128]{2,1,0:T(8,128)(2,1)} %block_work.1), calls=%async_computation.2 | async-start | bytes 131072 | tf_op jit(solution)/shard_map/all_to_all | solution.py:496
  67.7 2.4 %input_work.1 = bf16[256,256]{1,0:T(8,128)(2,1)} custom-call(bf16[256,256]{1,0:T(8,128)(2,1)S(1)} %get-tuple-element.32.delta, bf16[64,256]{1,0:T(8,128)(2,1)S(1)} %collective-permute-done.3.above, bf16[64,256]{1,0:T(8,128)(2,1)S(1)} %collective-permute-done.4.below, bf16[9,256,256]{2,1,0:T(8,128)(2,1)} %bitcast.22), custom_call_target="tpu_custom_call" | custom-call | flops 300000000 | bytes 2000000 | tf_op jit(solution)/shard_map/input_work/pallas_call | solution.py:376
  70.1 9.0 %all-to-all-done.2.pieces = bf16[8,32,128]{2,1,0:T(8,128)(2,1)S(1)} async-done(((bf16[8,32,128]{2,1,0:T(8,128)(2,1)}), bf16[8,32,128]{2,1,0:T(8,128)(2,1)S(1)}, u32[]{:S(2)}, u32[]{:S(2)}) %all-to-all-start.2) | async-done | bytes 65568 | tf_op jit(solution)/shard_map/all_to_all | solution.py:496
  79.1 11.9 %all_to_all.20.refs_1_ = bf16[16,32,128]{2,1,0:T(8,128)(2,1)S(1)} all-to-all(bf16[16,32,128]{2,1,0:T(8,128)(2,1)S(1)} %column_work.1), channel_id=1, replica_groups={{0,2,8,10,16,18,24,26,1,3,9,11,17,19,25,27},{4,6,12,14,20,22,28,30,5,7,..., dimensions={0} | all-to-all | bytes 262144 | tf_op jit(solution)/shard_map/all_to_all | solution.py:498
  91.0 0.8 unpack.1
  (7 shorter events, 0.1 us)
Async XLA Ops:
  0.6 15.4 %all-to-all-start = ((bf16[4,2,128,128]{3,2,1,0:T(8,128)(2,1)}), bf16[4,2,128,128]{3,2,1,0:T(8,128)(2,1)S(1)}, u32[]{:S(2)}, u32[]{:S(2)}) async-start(bf16[4,2,128,128]{3,2,1,0:T(8,128)(2,1)} %param.5), calls=%async_computation | async-start | bytes 524288 | tf_op jit(solution)/shard_map/all_to_all | solution.py:460
  16.1 6.2 %collective-permute-start = (bf16[2,128,128]{2,1,0:T(8,128)(2,1)S(1)}, bf16[2,128,128]{2,1,0:T(8,128)(2,1)S(1)}, u32[]{:S(2)}, u32[]{:S(2)}) collective-permute-start(bf16[2,128,128]{2,1,0:T(8,128)(2,1)S(1)} %pad_maximum_fusion), channel_id=1, source_target_pairs={{0,4},{1,5},{2,6},{3,7},{4,8},{5,9},{6,10},{7,11},{8,12},{9,13},{1... | collective-permute-start | bytes 196616 | tf_op jit(solution)/shard_map/ppermute | solution.py:467
  17.4 7.8 %collective-permute-start.1 = (bf16[2,128,128]{2,1,0:T(8,128)(2,1)S(1)}, bf16[2,128,128]{2,1,0:T(8,128)(2,1)S(1)}, u32[]{:S(2)}, u32[]{:S(2)}) collective-permute-start(bf16[2,128,128]{2,1,0:T(8,128)(2,1)S(1)} %pad_maximum_fusion.1), channel_id=1, source_target_pairs={{4,0},{5,1},{6,2},{7,3},{8,4},{9,5},{10,6},{11,7},{12,8},{13,9},{1... | collective-permute-start | bytes 196616 | tf_op jit(solution)/shard_map/ppermute | solution.py:468
  27.1 4.9 %collective-permute-start.2 = (bf16[112,32,128]{2,1,0:T(8,128)(2,1)S(1)}, bf16[112,32,128]{2,1,0:T(8,128)(2,1)S(1)}, u32[]{:S(2)}, u32[]{:S(2)}) collective-permute-start(bf16[112,32,128]{2,1,0:T(8,128)(2,1)S(1)} %get-tuple-element.28), channel_id=1, source_target_pairs={{0,1},{1,0},{2,3},{3,2},{4,5},{5,4},{6,7},{7,6},{8,9},{9,8},{10,11... | collective-permute-start | bytes 2752520 | tf_op jit(solution)/shard_map/ppermute | solution.py:486
  32.9 20.7 %all-to-all-start.1 = ((bf16[32,112,128]{2,1,0:T(8,128)(2,1)}), bf16[32,112,128]{2,1,0:T(8,128)(2,1)S(1)}, u32[]{:S(2)}, u32[]{:S(2)}) async-start(bf16[32,112,128]{2,1,0:T(8,128)(2,1)} %bitcast.11), calls=%async_computation.1 | async-start | bytes 1835008 | tf_op jit(solution)/shard_map/all_to_all | solution.py:492
  39.0 10.0 %collective-permute-start.3 = (bf16[64,256]{1,0:T(8,128)(2,1)S(1)}, bf16[64,256]{1,0:T(8,128)(2,1)S(1)}, u32[]{:S(2)}, u32[]{:S(2)}) collective-permute-start(bf16[64,256]{1,0:T(8,128)(2,1)S(1)} %get-tuple-element.29), channel_id=1, source_target_pairs={{0,4},{1,5},{2,6},{3,7},{4,8},{5,9},{6,10},{7,11},{8,12},{9,13},{1... | collective-permute-start | bytes 98312 | tf_op jit(solution)/shard_map/ppermute | solution.py:487
  42.0 7.0 %collective-permute-start.4 = (bf16[64,256]{1,0:T(8,128)(2,1)S(1)}, bf16[64,256]{1,0:T(8,128)(2,1)S(1)}, u32[]{:S(2)}, u32[]{:S(2)}) collective-permute-start(bf16[64,256]{1,0:T(8,128)(2,1)S(1)} %get-tuple-element.30), channel_id=1, source_target_pairs={{4,0},{5,1},{6,2},{7,3},{8,4},{9,5},{10,6},{11,7},{12,8},{13,9},{1... | collective-permute-start | bytes 98312 | tf_op jit(solution)/shard_map/ppermute | solution.py:488
  54.4 24.7 %all-to-all-start.2 = ((bf16[8,32,128]{2,1,0:T(8,128)(2,1)}), bf16[8,32,128]{2,1,0:T(8,128)(2,1)S(1)}, u32[]{:S(2)}, u32[]{:S(2)}) async-start(bf16[8,32,128]{2,1,0:T(8,128)(2,1)} %block_work.1), calls=%async_computation.2 | async-start | bytes 131072 | tf_op jit(solution)/shard_map/all_to_all | solution.py:496

commit v7 on v6

--- a/solution.py
+++ b/solution.py
@@ -460,14 +460,6 @@
     cot = lax.all_to_all(cotangent, "rows", 0, 0, axis_index_groups=QUADS)
     cot = cot.reshape(8, 128, C2)
 
-    def halo(cot_rows, x_row):
-        row = jnp.concatenate([x_row[:, :C2], x_row[:, C2:]], axis=0)
-        return jnp.concatenate([cot_rows, row[None]])
-
-    above = lax.ppermute(halo(cot[7:8], x[3]), "rows", down)
-    below = lax.ppermute(halo(cot[0:1], x[0]), "rows", up)
-    code = rank % 2 + rank // 2 % 2 * 2 + rank // 8 % 2 * 4 + lax.axis_index("dp") % 4 * 8
-    code = code.astype(jnp.int32).reshape(1)
     x_flat, w1, bias, w2 = (
         pltpu.with_memory_space_constraint(value, pltpu.HBM)
         for value in (
@@ -477,8 +469,18 @@
             w_second.reshape(9, C1, C2),
         )
     )
+    preact, w1_edge = conv_work(x_flat, w1, bias)
+    cot, preact = lax.optimization_barrier((cot, preact))
+
+    def halo(cot_rows, x_row):
+        row = jnp.concatenate([x_row[:, :C2], x_row[:, C2:]], axis=0)
+        return jnp.concatenate([cot_rows, row[None]])
+
+    above = lax.ppermute(halo(cot[7:8], x[3]), "rows", down)
+    below = lax.ppermute(halo(cot[0:1], x[0]), "rows", up)
+    code = rank % 2 + rank // 2 % 2 * 2 + rank // 8 % 2 * 4 + lax.axis_index("dp") % 4 * 8
+    code = code.astype(jnp.int32).reshape(1)
     cot = cot.reshape(8 * 128, C2)
-    preact, w1_edge = conv_work(x_flat, w1, bias)
     boxes, grad_act, w2_edge = boxes_work(cot, w2)
     delta, delta_first, delta_last, packed, send = main_work(
         code, above, below, cot, preact, boxes, grad_act, w1_edge, w2_edge, x_flat

time: 92.5 us -> 92.5 us (level)
    ppermute x1, waiting for transfers between devices: 2.99 us -> 4.86 us  [shards(): below = lax.ppermute(halo(cot[0:1], x[0]), 'rows', up)]
    all_to_all x1, waiting for transfers between devices: 4.35 us -> 3.24 us  [shards(): cot = lax.all_to_all(cotangent, 'rows', 0, 0, axis_index_groups=QUADS)]
  transfers between devices with their start and end apart: 8 -> 8, of which waited for: 6 -> 6; matrix products, arithmetic and copies ran while one was open for 1% -> 0% of each run, Pallas kernels for 6% -> 6%
where the time goes in v7:
time: 92.5 us; the launch traced here: 91.8 us
  starting transfers between devices  39.3 us (42%)
  waiting for transfers between devices  29.5 us (32%)
  blocking collectives  11.9 us (13%)
  Pallas kernels  10.3 us (11%)
    all_to_all x1, starting transfers between devices, shards(): column = lax.all_to_all(spread, both, 0, 0, axis_index_groups=COLUMN)  13.2 us
    all_to_all x1, blocking collectives, shards(): lax.all_to_all(column_work(column), 'rows', 0, 0, axis_index_groups=SHARE)  11.9 us
    all_to_all x1, starting transfers between devices, shards(): cot = lax.all_to_all(cotangent, 'rows', 0, 0, axis_index_groups=QUADS)  10.4 us
    all_to_all x1, waiting for transfers between devices, shards(): column = lax.all_to_all(spread, both, 0, 0, axis_index_groups=COLUMN)  8.98 us
    all_to_all x1, starting transfers between devices, shards(): block = lax.all_to_all(pair, both, 0, 0, axis_index_groups=BLOCK)  6.03 us
    ppermute x1, waiting for transfers between devices, shards(): from_above = lax.ppermute(delta_last, 'rows', down)  5.73 us
    ppermute x1, waiting for transfers between devices, shards(): below = lax.ppermute(halo(cot[0:1], x[0]), 'rows', up)  4.86 us
    all_to_all x1, waiting for transfers between devices, shards(): block = lax.all_to_all(pair, both, 0, 0, axis_index_groups=BLOCK)  4.64 us
  transfers between devices with their start and end apart: 8, of which 6 were waited for; matrix products, arithmetic and copies ran while one was open for 0% of the time, Pallas kernels for 6%

profile of v7, /device:TPU:1, one launch (start us, length us, event | category | flops | bytes accessed | tf_op | source)
XLA Modules:
  0.0 91.8 jit_solution(15406638250084452553)
XLA Ops:
  0.6 0.0 copy-start
  0.6 10.4 %all-to-all-start = ((bf16[4,2,128,128]{3,2,1,0:T(8,128)(2,1)}), bf16[4,2,128,128]{3,2,1,0:T(8,128)(2,1)S(1)}, u32[]{:S(2)}, u32[]{:S(2)}) async-start(bf16[4,2,128,128]{3,2,1,0:T(8,128)(2,1)} %param.5), calls=%async_computation | async-start | bytes 524288 | tf_op jit(solution)/shard_map/all_to_all | solution.py:460
  11.0 1.9 %conv_work.1 = (f32[256,256]{1,0:T(8,128)S(1)}, bf16[6,256,256]{2,1,0:T(8,128)(2,1)S(1)}) custom-call(bf16[256,256]{1,0:T(8,128)(2,1)} %bitcast.23, bf16[9,256,256]{2,1,0:T(8,128)(2,1)} %bitcast.21, f32[1,256]{1,0:T(1,128)} %bitcast.26), custom_call_target="tpu_custom_call" | custom-call | flops 300000000 | bytes 1500000 | tf_op jit(solution)/shard_map/conv_work/pallas_call | solution.py:217
  12.9 0.0 copy-done
  13.0 3.2 %all-to-all-done = bf16[4,2,128,128]{3,2,1,0:T(8,128)(2,1)S(1)} async-done(((bf16[4,2,128,128]{3,2,1,0:T(8,128)(2,1)}), bf16[4,2,128,128]{3,2,1,0:T(8,128)(2,1)S(1)}, u32[]{:S(2)}, u32[]{:S(2)}) %all-to-all-start) | async-done | bytes 262176 | tf_op jit(solution)/shard_map/all_to_all | solution.py:460
  16.2 1.3 %collective-permute-start = (bf16[2,128,128]{2,1,0:T(8,128)(2,1)S(1)}, bf16[2,128,128]{2,1,0:T(8,128)(2,1)S(1)}, u32[]{:S(2)}, u32[]{:S(2)}) collective-permute-start(bf16[2,128,128]{2,1,0:T(8,128)(2,1)S(1)} %pad_maximum_fusion), channel_id=1, source_target_pairs={{0,4},{1,5},{2,6},{3,7},{4,8},{5,9},{6,10},{7,11},{8,12},{9,13},{1... | collective-permute-start | bytes 196616 | tf_op jit(solution)/shard_map/ppermute | solution.py:479
  17.5 1.3 %collective-permute-start.1 = (bf16[2,128,128]{2,1,0:T(8,128)(2,1)S(1)}, bf16[2,128,128]{2,1,0:T(8,128)(2,1)S(1)}, u32[]{:S(2)}, u32[]{:S(2)}) collective-permute-start(bf16[2,128,128]{2,1,0:T(8,128)(2,1)S(1)} %pad_maximum_fusion.1), channel_id=1, source_target_pairs={{4,0},{5,1},{6,2},{7,3},{8,4},{9,5},{10,6},{11,7},{12,8},{13,9},{1... | collective-permute-start | bytes 196616 | tf_op jit(solution)/shard_map/ppermute | solution.py:480
  18.9 1.6 %boxes_work.1 = (bf16[256,1152]{1,0:T(8,128)(2,1)S(1)}, f32[256,256]{1,0:T(8,128)S(1)}, bf16[6,256,128]{2,1,0:T(8,128)(2,1)S(1)}) custom-call(bf16[1024,128]{1,0:T(8,128)(2,1)S(1)} %bitcast.19, bf16[9,256,128]{2,1,0:T(8,128)(2,1)} %bitcast.27), custom_call_target="tpu_custom_call" | custom-call | flops 300000000 | bytes 1500000 | tf_op jit(solution)/shard_map/boxes_work/pallas_call | solution.py:241
  20.5 0.0 collective-permute-done.above
  20.5 4.9 %collective-permute-done.1.below = bf16[2,128,128]{2,1,0:T(8,128)(2,1)S(1)} collective-permute-done((bf16[2,128,128]{2,1,0:T(8,128)(2,1)S(1)}, bf16[2,128,128]{2,1,0:T(8,128)(2,1)S(1)}, u32[]{:S(2)}, u32[]{:S(2)}) %collective-permute-start.1) | collective-permute-done | bytes 65568 | tf_op jit(solution)/shard_map/ppermute | solution.py:480
  25.4 1.8 %main_work.1 = (bf16[256,256]{1,0:T(8,128)(2,1)S(1)}, bf16[64,256]{1,0:T(8,128)(2,1)S(1)}, bf16[64,256]{1,0:T(8,128)(2,1)S(1)}, bf16[2,112,32,128]{3,2,1,0:T(8,128)(2,1)S(1)}, bf16[112,32,128]{2,1,0:T(8,128)(2,1)S(1)}) custom-call(s32[1]{0:T(128)} %bitcast.code.refs_0_, bf16[2,128,128]{2,1,0:T(8,128)(2,1)S(1)} %collective-permute-done.above, ...), custom_call_target="tpu_custom_call" | custom-call | flops 600000000 | bytes 5000000 | tf_op jit(solution)/shard_map/main_work/pallas_call | solution.py:260
  27.2 2.8 %collective-permute-start.2 = (bf16[112,32,128]{2,1,0:T(8,128)(2,1)S(1)}, bf16[112,32,128]{2,1,0:T(8,128)(2,1)S(1)}, u32[]{:S(2)}, u32[]{:S(2)}) collective-permute-start(bf16[112,32,128]{2,1,0:T(8,128)(2,1)S(1)} %get-tuple-element.32), channel_id=1, source_target_pairs={{0,1},{1,0},{2,3},{3,2},{4,5},{5,4},{6,7},{7,6},{8,9},{9,8},{10,11... | collective-permute-start | bytes 2752520 | tf_op jit(solution)/shard_map/ppermute | solution.py:488
  30.0 2.1 %collective-permute-done.2.received = bf16[112,32,128]{2,1,0:T(8,128)(2,1)S(1)} collective-permute-done((bf16[112,32,128]{2,1,0:T(8,128)(2,1)S(1)}, bf16[112,32,128]{2,1,0:T(8,128)(2,1)S(1)}, u32[]{:S(2)}, u32[]{:S(2)}) %collective-permute-start.2) | collective-permute-done | bytes 917536 | tf_op jit(solution)/shard_map/ppermute | solution.py:488
  32.1 1.0 %pair_work.1 = bf16[112,32,128]{2,1,0:T(8,128)(2,1)} custom-call(s32[1]{0:T(128)} %bitcast.code.refs_0_, bf16[2,112,32,128]{3,2,1,0:T(8,128)(2,1)S(1)} %get-tuple-element.31.packed, bf16[112,32,128]{2,1,0:T(8,128)(2,1)S(1)} %collective-permute-done.2.received), custom_call_target="tpu_custom_call" | custom-call | tf_op jit(solution)/shard_map/pair_work/pallas_call | solution.py:299
  33.1 6.0 %all-to-all-start.1 = ((bf16[32,112,128]{2,1,0:T(8,128)(2,1)}), bf16[32,112,128]{2,1,0:T(8,128)(2,1)S(1)}, u32[]{:S(2)}, u32[]{:S(2)}) async-start(bf16[32,112,128]{2,1,0:T(8,128)(2,1)} %bitcast.11), calls=%async_computation.1 | async-start | bytes 1835008 | tf_op jit(solution)/shard_map/all_to_all | solution.py:494
  39.1 3.0 %collective-permute-start.3 = (bf16[64,256]{1,0:T(8,128)(2,1)S(1)}, bf16[64,256]{1,0:T(8,128)(2,1)S(1)}, u32[]{:S(2)}, u32[]{:S(2)}) collective-permute-start(bf16[64,256]{1,0:T(8,128)(2,1)S(1)} %get-tuple-element.33), channel_id=1, source_target_pairs={{0,4},{1,5},{2,6},{3,7},{4,8},{5,9},{6,10},{7,11},{8,12},{9,13},{1... | collective-permute-start | bytes 98312 | tf_op jit(solution)/shard_map/ppermute | solution.py:489
  42.1 1.3 %collective-permute-start.4 = (bf16[64,256]{1,0:T(8,128)(2,1)S(1)}, bf16[64,256]{1,0:T(8,128)(2,1)S(1)}, u32[]{:S(2)}, u32[]{:S(2)}) collective-permute-start(bf16[64,256]{1,0:T(8,128)(2,1)S(1)} %get-tuple-element.34), channel_id=1, source_target_pairs={{4,0},{5,1},{6,2},{7,3},{8,4},{9,5},{10,6},{11,7},{12,8},{13,9},{1... | collective-permute-start | bytes 98312 | tf_op jit(solution)/shard_map/ppermute | solution.py:490
  43.4 5.7 %collective-permute-done.3.above = bf16[64,256]{1,0:T(8,128)(2,1)S(1)} collective-permute-done((bf16[64,256]{1,0:T(8,128)(2,1)S(1)}, bf16[64,256]{1,0:T(8,128)(2,1)S(1)}, u32[]{:S(2)}, u32[]{:S(2)}) %collective-permute-start.3) | collective-permute-done | bytes 32800 | tf_op jit(solution)/shard_map/ppermute | solution.py:489
  49.1 0.0 collective-permute-done.4.below
  49.1 4.6 %all-to-all-done.1.pieces = bf16[32,112,128]{2,1,0:T(8,128)(2,1)S(1)} async-done(((bf16[32,112,128]{2,1,0:T(8,128)(2,1)}), bf16[32,112,128]{2,1,0:T(8,128)(2,1)S(1)}, u32[]{:S(2)}, u32[]{:S(2)}) %all-to-all-start.1) | async-done | bytes 917536 | tf_op jit(solution)/shard_map/all_to_all | solution.py:494
  53.8 0.8 block_work.1
  54.5 13.2 %all-to-all-start.2 = ((bf16[8,32,128]{2,1,0:T(8,128)(2,1)}), bf16[8,32,128]{2,1,0:T(8,128)(2,1)S(1)}, u32[]{:S(2)}, u32[]{:S(2)}) async-start(bf16[8,32,128]{2,1,0:T(8,128)(2,1)} %block_work.1), calls=%async_computation.2 | async-start | bytes 131072 | tf_op jit(solution)/shard_map/all_to_all | solution.py:498
  67.8 2.4 %input_work.1 = bf16[256,256]{1,0:T(8,128)(2,1)} custom-call(bf16[256,256]{1,0:T(8,128)(2,1)S(1)} %get-tuple-element.36.delta, bf16[64,256]{1,0:T(8,128)(2,1)S(1)} %collective-permute-done.3.above, bf16[64,256]{1,0:T(8,128)(2,1)S(1)} %collective-permute-done.4.below, bf16[9,256,256]{2,1,0:T(8,128)(2,1)} %bitcast.22), custom_call_target="tpu_custom_call" | custom-call | flops 300000000 | bytes 2000000 | tf_op jit(solution)/shard_map/input_work/pallas_call | solution.py:376
  70.2 9.0 %all-to-all-done.2.pieces = bf16[8,32,128]{2,1,0:T(8,128)(2,1)S(1)} async-done(((bf16[8,32,128]{2,1,0:T(8,128)(2,1)}), bf16[8,32,128]{2,1,0:T(8,128)(2,1)S(1)}, u32[]{:S(2)}, u32[]{:S(2)}) %all-to-all-start.2) | async-done | bytes 65568 | tf_op jit(solution)/shard_map/all_to_all | solution.py:498
  79.2 11.9 %all_to_all.20.refs_1_ = bf16[16,32,128]{2,1,0:T(8,128)(2,1)S(1)} all-to-all(bf16[16,32,128]{2,1,0:T(8,128)(2,1)S(1)} %column_work.1), channel_id=1, replica_groups={{0,2,8,10,16,18,24,26,1,3,9,11,17,19,25,27},{4,6,12,14,20,22,28,30,5,7,..., dimensions={0} | all-to-all | bytes 262144 | tf_op jit(solution)/shard_map/all_to_all | solution.py:500
  91.1 0.8 unpack.1
  (8 shorter events, 0.1 us)
Async XLA Ops:
  0.6 12.3 %copy-start = (bf16[1,4,64,256]{3,2,1,0:T(8,128)(2,1)S(1)}, bf16[1,4,64,256]{3,2,1,0:T(8,128)(2,1)}, u32[]{:S(2)}) copy-start(bf16[1,4,64,256]{3,2,1,0:T(8,128)(2,1)} %param.6) | copy-start | bytes 393220
  0.6 15.6 %all-to-all-start = ((bf16[4,2,128,128]{3,2,1,0:T(8,128)(2,1)}), bf16[4,2,128,128]{3,2,1,0:T(8,128)(2,1)S(1)}, u32[]{:S(2)}, u32[]{:S(2)}) async-start(bf16[4,2,128,128]{3,2,1,0:T(8,128)(2,1)} %param.5), calls=%async_computation | async-start | bytes 524288 | tf_op jit(solution)/shard_map/all_to_all | solution.py:460
  16.2 4.3 %collective-permute-start = (bf16[2,128,128]{2,1,0:T(8,128)(2,1)S(1)}, bf16[2,128,128]{2,1,0:T(8,128)(2,1)S(1)}, u32[]{:S(2)}, u32[]{:S(2)}) collective-permute-start(bf16[2,128,128]{2,1,0:T(8,128)(2,1)S(1)} %pad_maximum_fusion), channel_id=1, source_target_pairs={{0,4},{1,5},{2,6},{3,7},{4,8},{5,9},{6,10},{7,11},{8,12},{9,13},{1... | collective-permute-start | bytes 196616 | tf_op jit(solution)/shard_map/ppermute | solution.py:479
  17.5 7.8 %collective-permute-start.1 = (bf16[2,128,128]{2,1,0:T(8,128)(2,1)S(1)}, bf16[2,128,128]{2,1,0:T(8,128)(2,1)S(1)}, u32[]{:S(2)}, u32[]{:S(2)}) collective-permute-start(bf16[2,128,128]{2,1,0:T(8,128)(2,1)S(1)} %pad_maximum_fusion.1), channel_id=1, source_target_pairs={{4,0},{5,1},{6,2},{7,3},{8,4},{9,5},{10,6},{11,7},{12,8},{13,9},{1... | collective-permute-start | bytes 196616 | tf_op jit(solution)/shard_map/ppermute | solution.py:480
  27.2 4.9 %collective-permute-start.2 = (bf16[112,32,128]{2,1,0:T(8,128)(2,1)S(1)}, bf16[112,32,128]{2,1,0:T(8,128)(2,1)S(1)}, u32[]{:S(2)}, u32[]{:S(2)}) collective-permute-start(bf16[112,32,128]{2,1,0:T(8,128)(2,1)S(1)} %get-tuple-element.32), channel_id=1, source_target_pairs={{0,1},{1,0},{2,3},{3,2},{4,5},{5,4},{6,7},{7,6},{8,9},{9,8},{10,11... | collective-permute-start | bytes 2752520 | tf_op jit(solution)/shard_map/ppermute | solution.py:488
  33.1 20.7 %all-to-all-start.1 = ((bf16[32,112,128]{2,1,0:T(8,128)(2,1)}), bf16[32,112,128]{2,1,0:T(8,128)(2,1)S(1)}, u32[]{:S(2)}, u32[]{:S(2)}) async-start(bf16[32,112,128]{2,1,0:T(8,128)(2,1)} %bitcast.11), calls=%async_computation.1 | async-start | bytes 1835008 | tf_op jit(solution)/shard_map/all_to_all | solution.py:494
  39.1 10.0 %collective-permute-start.3 = (bf16[64,256]{1,0:T(8,128)(2,1)S(1)}, bf16[64,256]{1,0:T(8,128)(2,1)S(1)}, u32[]{:S(2)}, u32[]{:S(2)}) collective-permute-start(bf16[64,256]{1,0:T(8,128)(2,1)S(1)} %get-tuple-element.33), channel_id=1, source_target_pairs={{0,4},{1,5},{2,6},{3,7},{4,8},{5,9},{6,10},{7,11},{8,12},{9,13},{1... | collective-permute-start | bytes 98312 | tf_op jit(solution)/shard_map/ppermute | solution.py:489
  42.1 7.0 %collective-permute-start.4 = (bf16[64,256]{1,0:T(8,128)(2,1)S(1)}, bf16[64,256]{1,0:T(8,128)(2,1)S(1)}, u32[]{:S(2)}, u32[]{:S(2)}) collective-permute-start(bf16[64,256]{1,0:T(8,128)(2,1)S(1)} %get-tuple-element.34), channel_id=1, source_target_pairs={{4,0},{5,1},{6,2},{7,3},{8,4},{9,5},{10,6},{11,7},{12,8},{13,9},{1... | collective-permute-start | bytes 98312 | tf_op jit(solution)/shard_map/ppermute | solution.py:490
  54.5 24.6 %all-to-all-start.2 = ((bf16[8,32,128]{2,1,0:T(8,128)(2,1)}), bf16[8,32,128]{2,1,0:T(8,128)(2,1)S(1)}, u32[]{:S(2)}, u32[]{:S(2)}) async-start(bf16[8,32,128]{2,1,0:T(8,128)(2,1)} %block_work.1), calls=%async_computation.2 | async-start | bytes 131072 | tf_op jit(solution)/shard_map/all_to_all | solution.py:498

commit v8 on v6

--- a/solution.py
+++ b/solution.py
@@ -491,15 +491,16 @@
     pair = pair.reshape(32, CHUNK, 128)
     block = lax.all_to_all(pair, both, 0, 0, axis_index_groups=BLOCK)
     block, from_above, from_below = lax.optimization_barrier((block, from_above, from_below))
-    grad_x = input_work(delta, from_above, from_below, w1)
     spread = block_work(code, block)
     column = lax.all_to_all(spread, both, 0, 0, axis_index_groups=COLUMN)
-    column, grad_x = lax.optimization_barrier((column, grad_x))
+    column, delta = lax.optimization_barrier((column, delta))
+    grad_x = input_work(delta, from_above, from_below, w1)
     full = lax.all_to_all(column_work(column), "rows", 0, 0, axis_index_groups=SHARE)
 
     pixels_low = lax.axis_size("dp") * lax.axis_size("rows") * PIX
     scale_low = pixels_low ** (-0.5)
     scale_high = (4 * pixels_low) ** (-0.5)
+    full, grad_x = lax.optimization_barrier((full, grad_x))
     full = pltpu.with_memory_space_constraint(full, pltpu.VMEM)
     grad_first, grad_second, grad_bias = results(code, full, scale_low, scale_high)
     grad_input = grad_x.reshape(1, ROWS, COLS, C1)

time: 92.5 us -> 92.7 us (level)
  blocking collectives: 11.9 us -> 24.5 us
  starting transfers between devices: 39.2 us -> 32.5 us
  waiting for transfers between devices: 28.8 us -> 23.1 us
    all_to_all x1, blocking collectives: 11.9 us -> 24.5 us  [shards(): column = lax.all_to_all(spread, both, 0, 0, axis_index_groups=COLUMN)]
    all_to_all x1, starting transfers between devices: 13.3 us -> 6.6 us  [shards(): lax.all_to_all(column_work(column), 'rows', 0, 0, axis_index_groups=SHARE)]
    all_to_all x1, waiting for transfers between devices: 8.98 us -> 3.31 us  [shards(): lax.all_to_all(column_work(column), 'rows', 0, 0, axis_index_groups=SHARE)]
where the time goes in v8:
time: 92.7 us; the launch traced here: 92.1 us
  starting transfers between devices  32.5 us (35%)
  blocking collectives  24.5 us (26%)
  waiting for transfers between devices  23.1 us (25%)
  Pallas kernels  10.3 us (11%)
    all_to_all x1, blocking collectives, shards(): column = lax.all_to_all(spread, both, 0, 0, axis_index_groups=COLUMN)  24.5 us
    all_to_all x1, starting transfers between devices, shards(): cot = lax.all_to_all(cotangent, 'rows', 0, 0, axis_index_groups=QUADS)  10.3 us
    all_to_all x1, starting transfers between devices, shards(): lax.all_to_all(column_work(column), 'rows', 0, 0, axis_index_groups=SHARE)  6.6 us
    all_to_all x1, starting transfers between devices, shards(): block = lax.all_to_all(pair, both, 0, 0, axis_index_groups=BLOCK)  6.03 us
    ppermute x1, waiting for transfers between devices, shards(): from_above = lax.ppermute(delta_last, 'rows', down)  5.73 us
    all_to_all x1, waiting for transfers between devices, shards(): block = lax.all_to_all(pair, both, 0, 0, axis_index_groups=BLOCK)  4.64 us
    all_to_all x1, waiting for transfers between devices, shards(): cot = lax.all_to_all(cotangent, 'rows', 0, 0, axis_index_groups=QUADS)  4.35 us
    all_to_all x1, waiting for transfers between devices, shards(): lax.all_to_all(column_work(column), 'rows', 0, 0, axis_index_groups=SHARE)  3.31 us
  transfers between devices with their start and end apart: 8, of which 6 were waited for; matrix products, arithmetic and copies ran while one was open for 1% of the time, Pallas kernels for 6%

profile of v8, /device:TPU:1, one launch (start us, length us, event | category | flops | bytes accessed | tf_op | source)
XLA Modules:
  0.0 92.1 jit_solution(14611775105815675455)
XLA Ops:
  0.6 10.3 %all-to-all-start = ((bf16[4,2,128,128]{3,2,1,0:T(8,128)(2,1)}), bf16[4,2,128,128]{3,2,1,0:T(8,128)(2,1)S(1)}, u32[]{:S(2)}, u32[]{:S(2)}) async-start(bf16[4,2,128,128]{3,2,1,0:T(8,128)(2,1)} %param.5), calls=%async_computation | async-start | bytes 524288 | tf_op jit(solution)/shard_map/all_to_all | solution.py:460
  10.9 0.8 slice_bitcast_fusion
  11.7 4.4 %all-to-all-done = bf16[4,2,128,128]{3,2,1,0:T(8,128)(2,1)S(1)} async-done(((bf16[4,2,128,128]{3,2,1,0:T(8,128)(2,1)}), bf16[4,2,128,128]{3,2,1,0:T(8,128)(2,1)S(1)}, u32[]{:S(2)}, u32[]{:S(2)}) %all-to-all-start) | async-done | bytes 262176 | tf_op jit(solution)/shard_map/all_to_all | solution.py:460
  16.1 1.3 %collective-permute-start = (bf16[2,128,128]{2,1,0:T(8,128)(2,1)S(1)}, bf16[2,128,128]{2,1,0:T(8,128)(2,1)S(1)}, u32[]{:S(2)}, u32[]{:S(2)}) collective-permute-start(bf16[2,128,128]{2,1,0:T(8,128)(2,1)S(1)} %pad_maximum_fusion), channel_id=1, source_target_pairs={{0,4},{1,5},{2,6},{3,7},{4,8},{5,9},{6,10},{7,11},{8,12},{9,13},{1... | collective-permute-start | bytes 196616 | tf_op jit(solution)/shard_map/ppermute | solution.py:467
  17.4 1.3 %collective-permute-start.1 = (bf16[2,128,128]{2,1,0:T(8,128)(2,1)S(1)}, bf16[2,128,128]{2,1,0:T(8,128)(2,1)S(1)}, u32[]{:S(2)}, u32[]{:S(2)}) collective-permute-start(bf16[2,128,128]{2,1,0:T(8,128)(2,1)S(1)} %pad_maximum_fusion.1), channel_id=1, source_target_pairs={{4,0},{5,1},{6,2},{7,3},{8,4},{9,5},{10,6},{11,7},{12,8},{13,9},{1... | collective-permute-start | bytes 196616 | tf_op jit(solution)/shard_map/ppermute | solution.py:468
  18.8 1.9 %conv_work.1 = (f32[256,256]{1,0:T(8,128)S(1)}, bf16[6,256,256]{2,1,0:T(8,128)(2,1)S(1)}) custom-call(bf16[256,256]{1,0:T(8,128)(2,1)} %bitcast.23, bf16[9,256,256]{2,1,0:T(8,128)(2,1)} %bitcast.21, f32[1,256]{1,0:T(1,128)} %bitcast.26), custom_call_target="tpu_custom_call" | custom-call | flops 300000000 | bytes 1500000 | tf_op jit(solution)/shard_map/conv_work/pallas_call | solution.py:217
  20.6 1.6 %boxes_work.1 = (bf16[256,1152]{1,0:T(8,128)(2,1)S(1)}, f32[256,256]{1,0:T(8,128)S(1)}, bf16[6,256,128]{2,1,0:T(8,128)(2,1)S(1)}) custom-call(bf16[1024,128]{1,0:T(8,128)(2,1)S(1)} %bitcast.19, bf16[9,256,128]{2,1,0:T(8,128)(2,1)} %bitcast.27), custom_call_target="tpu_custom_call" | custom-call | flops 300000000 | bytes 1500000 | tf_op jit(solution)/shard_map/boxes_work/pallas_call | solution.py:241
  22.2 0.0 collective-permute-done.above
  22.2 3.0 %collective-permute-done.1.below = bf16[2,128,128]{2,1,0:T(8,128)(2,1)S(1)} collective-permute-done((bf16[2,128,128]{2,1,0:T(8,128)(2,1)S(1)}, bf16[2,128,128]{2,1,0:T(8,128)(2,1)S(1)}, u32[]{:S(2)}, u32[]{:S(2)}) %collective-permute-start.1) | collective-permute-done | bytes 65568 | tf_op jit(solution)/shard_map/ppermute | solution.py:468
  25.2 1.8 %main_work.1 = (bf16[256,256]{1,0:T(8,128)(2,1)S(1)}, bf16[64,256]{1,0:T(8,128)(2,1)S(1)}, bf16[64,256]{1,0:T(8,128)(2,1)S(1)}, bf16[2,112,32,128]{3,2,1,0:T(8,128)(2,1)S(1)}, bf16[112,32,128]{2,1,0:T(8,128)(2,1)S(1)}) custom-call(s32[1]{0:T(128)} %bitcast.code.refs_0_, bf16[2,128,128]{2,1,0:T(8,128)(2,1)S(1)} %collective-permute-done.above, ...), custom_call_target="tpu_custom_call" | custom-call | flops 600000000 | bytes 5000000 | tf_op jit(solution)/shard_map/main_work/pallas_call | solution.py:260
  27.1 2.8 %collective-permute-start.2 = (bf16[112,32,128]{2,1,0:T(8,128)(2,1)S(1)}, bf16[112,32,128]{2,1,0:T(8,128)(2,1)S(1)}, u32[]{:S(2)}, u32[]{:S(2)}) collective-permute-start(bf16[112,32,128]{2,1,0:T(8,128)(2,1)S(1)} %get-tuple-element.30), channel_id=1, source_target_pairs={{0,1},{1,0},{2,3},{3,2},{4,5},{5,4},{6,7},{7,6},{8,9},{9,8},{10,11... | collective-permute-start | bytes 2752520 | tf_op jit(solution)/shard_map/ppermute | solution.py:486
  29.8 2.1 %collective-permute-done.2.received = bf16[112,32,128]{2,1,0:T(8,128)(2,1)S(1)} collective-permute-done((bf16[112,32,128]{2,1,0:T(8,128)(2,1)S(1)}, bf16[112,32,128]{2,1,0:T(8,128)(2,1)S(1)}, u32[]{:S(2)}, u32[]{:S(2)}) %collective-permute-start.2) | collective-permute-done | bytes 917536 | tf_op jit(solution)/shard_map/ppermute | solution.py:486
  31.9 1.0 %pair_work.1 = bf16[112,32,128]{2,1,0:T(8,128)(2,1)} custom-call(s32[1]{0:T(128)} %bitcast.code.refs_0_, bf16[2,112,32,128]{3,2,1,0:T(8,128)(2,1)S(1)} %get-tuple-element.29.packed, bf16[112,32,128]{2,1,0:T(8,128)(2,1)S(1)} %collective-permute-done.2.received), custom_call_target="tpu_custom_call" | custom-call | tf_op jit(solution)/shard_map/pair_work/pallas_call | solution.py:299
  32.9 6.0 %all-to-all-start.1 = ((bf16[32,112,128]{2,1,0:T(8,128)(2,1)}), bf16[32,112,128]{2,1,0:T(8,128)(2,1)S(1)}, u32[]{:S(2)}, u32[]{:S(2)}) async-start(bf16[32,112,128]{2,1,0:T(8,128)(2,1)} %bitcast.11), calls=%async_computation.1 | async-start | bytes 1835008 | tf_op jit(solution)/shard_map/all_to_all | solution.py:492
  39.0 3.0 %collective-permute-start.3 = (bf16[64,256]{1,0:T(8,128)(2,1)S(1)}, bf16[64,256]{1,0:T(8,128)(2,1)S(1)}, u32[]{:S(2)}, u32[]{:S(2)}) collective-permute-start(bf16[64,256]{1,0:T(8,128)(2,1)S(1)} %get-tuple-element.31), channel_id=1, source_target_pairs={{0,4},{1,5},{2,6},{3,7},{4,8},{5,9},{6,10},{7,11},{8,12},{9,13},{1... | collective-permute-start | bytes 98312 | tf_op jit(solution)/shard_map/ppermute | solution.py:487
  42.0 1.3 %collective-permute-start.4 = (bf16[64,256]{1,0:T(8,128)(2,1)S(1)}, bf16[64,256]{1,0:T(8,128)(2,1)S(1)}, u32[]{:S(2)}, u32[]{:S(2)}) collective-permute-start(bf16[64,256]{1,0:T(8,128)(2,1)S(1)} %get-tuple-element.32), channel_id=1, source_target_pairs={{4,0},{5,1},{6,2},{7,3},{8,4},{9,5},{10,6},{11,7},{12,8},{13,9},{1... | collective-permute-start | bytes 98312 | tf_op jit(solution)/shard_map/ppermute | solution.py:488
  43.3 5.7 %collective-permute-done.3.above = bf16[64,256]{1,0:T(8,128)(2,1)S(1)} collective-permute-done((bf16[64,256]{1,0:T(8,128)(2,1)S(1)}, bf16[64,256]{1,0:T(8,128)(2,1)S(1)}, u32[]{:S(2)}, u32[]{:S(2)}) %collective-permute-start.3) | collective-permute-done | bytes 32800 | tf_op jit(solution)/shard_map/ppermute | solution.py:487
  49.0 0.0 collective-permute-done.4.below
  49.0 4.6 %all-to-all-done.1.pieces = bf16[32,112,128]{2,1,0:T(8,128)(2,1)S(1)} async-done(((bf16[32,112,128]{2,1,0:T(8,128)(2,1)}), bf16[32,112,128]{2,1,0:T(8,128)(2,1)S(1)}, u32[]{:S(2)}, u32[]{:S(2)}) %all-to-all-start.1) | async-done | bytes 917536 | tf_op jit(solution)/shard_map/all_to_all | solution.py:492
  53.6 0.1 block_work.1
  53.8 24.5 %all_to_all.20.pieces = bf16[8,32,128]{2,1,0:T(8,128)(2,1)S(1)} all-to-all(bf16[8,32,128]{2,1,0:T(8,128)(2,1)S(1)} %block_work.1), channel_id=1, replica_groups={{0,64,4,68,32,96,36,100},{1,65,5,69,33,97,37,101},{2,66,6,70,34,98,38,1..., dimensions={0} | all-to-all | bytes 131072 | tf_op jit(solution)/shard_map/all_to_all | solution.py:495
  78.3 0.7 column_work.1
  79.0 6.6 %all-to-all-start.3 = ((bf16[16,32,128]{2,1,0:T(8,128)(2,1)}), bf16[16,32,128]{2,1,0:T(8,128)(2,1)S(1)}, u32[]{:S(2)}, u32[]{:S(2)}) async-start(bf16[16,32,128]{2,1,0:T(8,128)(2,1)} %column_work.1), calls=%async_computation.3 | async-start | bytes 262144 | tf_op jit(solution)/shard_map/all_to_all | solution.py:498
  85.6 2.4 %input_work.1 = bf16[256,256]{1,0:T(8,128)(2,1)} custom-call(bf16[256,256]{1,0:T(8,128)(2,1)S(1)} %get-tuple-element.36.delta, bf16[64,256]{1,0:T(8,128)(2,1)S(1)} %collective-permute-done.3.above, bf16[64,256]{1,0:T(8,128)(2,1)S(1)} %collective-permute-done.4.below, bf16[9,256,256]{2,1,0:T(8,128)(2,1)} %bitcast.22), custom_call_target="tpu_custom_call" | custom-call | flops 300000000 | bytes 2000000 | tf_op jit(solution)/shard_map/input_work/pallas_call | solution.py:376
  88.0 3.3 %all-to-all-done.3.refs_1_ = bf16[16,32,128]{2,1,0:T(8,128)(2,1)S(1)} async-done(((bf16[16,32,128]{2,1,0:T(8,128)(2,1)}), bf16[16,32,128]{2,1,0:T(8,128)(2,1)S(1)}, u32[]{:S(2)}, u32[]{:S(2)}) %all-to-all-start.3) | async-done | bytes 131104 | tf_op jit(solution)/shard_map/all_to_all | solution.py:498
  91.3 0.8 unpack.1
  (6 shorter events, 0.0 us)
Async XLA Ops:
  0.6 15.4 %all-to-all-start = ((bf16[4,2,128,128]{3,2,1,0:T(8,128)(2,1)}), bf16[4,2,128,128]{3,2,1,0:T(8,128)(2,1)S(1)}, u32[]{:S(2)}, u32[]{:S(2)}) async-start(bf16[4,2,128,128]{3,2,1,0:T(8,128)(2,1)} %param.5), calls=%async_computation | async-start | bytes 524288 | tf_op jit(solution)/shard_map/all_to_all | solution.py:460
  16.1 6.2 %collective-permute-start = (bf16[2,128,128]{2,1,0:T(8,128)(2,1)S(1)}, bf16[2,128,128]{2,1,0:T(8,128)(2,1)S(1)}, u32[]{:S(2)}, u32[]{:S(2)}) collective-permute-start(bf16[2,128,128]{2,1,0:T(8,128)(2,1)S(1)} %pad_maximum_fusion), channel_id=1, source_target_pairs={{0,4},{1,5},{2,6},{3,7},{4,8},{5,9},{6,10},{7,11},{8,12},{9,13},{1... | collective-permute-start | bytes 196616 | tf_op jit(solution)/shard_map/ppermute | solution.py:467
  17.4 7.8 %collective-permute-start.1 = (bf16[2,128,128]{2,1,0:T(8,128)(2,1)S(1)}, bf16[2,128,128]{2,1,0:T(8,128)(2,1)S(1)}, u32[]{:S(2)}, u32[]{:S(2)}) collective-permute-start(bf16[2,128,128]{2,1,0:T(8,128)(2,1)S(1)} %pad_maximum_fusion.1), channel_id=1, source_target_pairs={{4,0},{5,1},{6,2},{7,3},{8,4},{9,5},{10,6},{11,7},{12,8},{13,9},{1... | collective-permute-start | bytes 196616 | tf_op jit(solution)/shard_map/ppermute | solution.py:468
  27.1 4.9 %collective-permute-start.2 = (bf16[112,32,128]{2,1,0:T(8,128)(2,1)S(1)}, bf16[112,32,128]{2,1,0:T(8,128)(2,1)S(1)}, u32[]{:S(2)}, u32[]{:S(2)}) collective-permute-start(bf16[112,32,128]{2,1,0:T(8,128)(2,1)S(1)} %get-tuple-element.30), channel_id=1, source_target_pairs={{0,1},{1,0},{2,3},{3,2},{4,5},{5,4},{6,7},{7,6},{8,9},{9,8},{10,11... | collective-permute-start | bytes 2752520 | tf_op jit(solution)/shard_map/ppermute | solution.py:486
  32.9 20.7 %all-to-all-start.1 = ((bf16[32,112,128]{2,1,0:T(8,128)(2,1)}), bf16[32,112,128]{2,1,0:T(8,128)(2,1)S(1)}, u32[]{:S(2)}, u32[]{:S(2)}) async-start(bf16[32,112,128]{2,1,0:T(8,128)(2,1)} %bitcast.11), calls=%async_computation.1 | async-start | bytes 1835008 | tf_op jit(solution)/shard_map/all_to_all | solution.py:492
  39.0 10.0 %collective-permute-start.3 = (bf16[64,256]{1,0:T(8,128)(2,1)S(1)}, bf16[64,256]{1,0:T(8,128)(2,1)S(1)}, u32[]{:S(2)}, u32[]{:S(2)}) collective-permute-start(bf16[64,256]{1,0:T(8,128)(2,1)S(1)} %get-tuple-element.31), channel_id=1, source_target_pairs={{0,4},{1,5},{2,6},{3,7},{4,8},{5,9},{6,10},{7,11},{8,12},{9,13},{1... | collective-permute-start | bytes 98312 | tf_op jit(solution)/shard_map/ppermute | solution.py:487
  42.0 7.0 %collective-permute-start.4 = (bf16[64,256]{1,0:T(8,128)(2,1)S(1)}, bf16[64,256]{1,0:T(8,128)(2,1)S(1)}, u32[]{:S(2)}, u32[]{:S(2)}) collective-permute-start(bf16[64,256]{1,0:T(8,128)(2,1)S(1)} %get-tuple-element.32), channel_id=1, source_target_pairs={{4,0},{5,1},{6,2},{7,3},{8,4},{9,5},{10,6},{11,7},{12,8},{13,9},{1... | collective-permute-start | bytes 98312 | tf_op jit(solution)/shard_map/ppermute | solution.py:488
  79.0 12.3 %all-to-all-start.3 = ((bf16[16,32,128]{2,1,0:T(8,128)(2,1)}), bf16[16,32,128]{2,1,0:T(8,128)(2,1)S(1)}, u32[]{:S(2)}, u32[]{:S(2)}) async-start(bf16[16,32,128]{2,1,0:T(8,128)(2,1)} %column_work.1), calls=%async_computation.3 | async-start | bytes 262144 | tf_op jit(solution)/shard_map/all_to_all | solution.py:498

commit v9 on v6

--- a/solution.py
+++ b/solution.py
@@ -397,7 +397,7 @@
     for half in range(2):
         for k in range(8):
             before = 2 * k - (k - z_hi + 3) // 4
-            piece = full[8 * half + k].astype(F32).reshape(2, 16, 128)
+            piece = full[2 * k + half].astype(F32).reshape(2, 16, 128)
             tiles[pl.ds(half * (TILES // 2) + before, 2)] = piece
 
     def band(n):
@@ -446,7 +446,7 @@
     for za in TWO
     for c in TWO
 ]
-SHARE = [[place(0, 0, y, zb, za, c) for c in TWO for y in FOUR for za in TWO] for zb in TWO]
+SHARE = [[place(0, 0, y, zb, za, c) for y in FOUR for za in TWO for c in TWO] for zb in TWO]
 QUADS = [[4 * j + b for b in FOUR] for j in range(8)]
 
 

time: 92.5 us -> 92.8 us (level)
  no operation moved by 1% of the time
where the time goes in v9:
time: 92.8 us; the launch traced here: 92.1 us
  starting transfers between devices  39.2 us (42%)
  waiting for transfers between devices  28.8 us (31%)
  blocking collectives  12.2 us (13%)
  Pallas kernels  10.2 us (11%)
    all_to_all x1, starting transfers between devices, shards(): column = lax.all_to_all(spread, both, 0, 0, axis_index_groups=COLUMN)  13.3 us
    all_to_all x1, blocking collectives, shards(): lax.all_to_all(column_work(column), 'rows', 0, 0, axis_index_groups=SHARE)  12.2 us
    all_to_all x1, starting transfers between devices, shards(): cot = lax.all_to_all(cotangent, 'rows', 0, 0, axis_index_groups=QUADS)  10.3 us
    all_to_all x1, waiting for transfers between devices, shards(): column = lax.all_to_all(spread, both, 0, 0, axis_index_groups=COLUMN)  8.98 us
    all_to_all x1, starting transfers between devices, shards(): block = lax.all_to_all(pair, both, 0, 0, axis_index_groups=BLOCK)  6.03 us
    ppermute x1, waiting for transfers between devices, shards(): from_above = lax.ppermute(delta_last, 'rows', down)  5.73 us
    all_to_all x1, waiting for transfers between devices, shards(): block = lax.all_to_all(pair, both, 0, 0, axis_index_groups=BLOCK)  4.64 us
    all_to_all x1, waiting for transfers between devices, shards(): cot = lax.all_to_all(cotangent, 'rows', 0, 0, axis_index_groups=QUADS)  4.35 us
  transfers between devices with their start and end apart: 8, of which 6 were waited for; matrix products, arithmetic and copies ran while one was open for 1% of the time, Pallas kernels for 6%

profile of v9, /device:TPU:1, one launch (start us, length us, event | category | flops | bytes accessed | tf_op | source)
XLA Modules:
  0.0 92.1 jit_solution(7054666221002913341)
XLA Ops:
  0.6 10.3 %all-to-all-start = ((bf16[4,2,128,128]{3,2,1,0:T(8,128)(2,1)}), bf16[4,2,128,128]{3,2,1,0:T(8,128)(2,1)S(1)}, u32[]{:S(2)}, u32[]{:S(2)}) async-start(bf16[4,2,128,128]{3,2,1,0:T(8,128)(2,1)} %param.5), calls=%async_computation | async-start | bytes 524288 | tf_op jit(solution)/shard_map/all_to_all | solution.py:460
  10.9 0.8 slice_bitcast_fusion
  11.7 4.4 %all-to-all-done = bf16[4,2,128,128]{3,2,1,0:T(8,128)(2,1)S(1)} async-done(((bf16[4,2,128,128]{3,2,1,0:T(8,128)(2,1)}), bf16[4,2,128,128]{3,2,1,0:T(8,128)(2,1)S(1)}, u32[]{:S(2)}, u32[]{:S(2)}) %all-to-all-start) | async-done | bytes 262176 | tf_op jit(solution)/shard_map/all_to_all | solution.py:460
  16.1 1.3 %collective-permute-start = (bf16[2,128,128]{2,1,0:T(8,128)(2,1)S(1)}, bf16[2,128,128]{2,1,0:T(8,128)(2,1)S(1)}, u32[]{:S(2)}, u32[]{:S(2)}) collective-permute-start(bf16[2,128,128]{2,1,0:T(8,128)(2,1)S(1)} %pad_maximum_fusion), channel_id=1, source_target_pairs={{0,4},{1,5},{2,6},{3,7},{4,8},{5,9},{6,10},{7,11},{8,12},{9,13},{1... | collective-permute-start | bytes 196616 | tf_op jit(solution)/shard_map/ppermute | solution.py:467
  17.4 1.3 %collective-permute-start.1 = (bf16[2,128,128]{2,1,0:T(8,128)(2,1)S(1)}, bf16[2,128,128]{2,1,0:T(8,128)(2,1)S(1)}, u32[]{:S(2)}, u32[]{:S(2)}) collective-permute-start(bf16[2,128,128]{2,1,0:T(8,128)(2,1)S(1)} %pad_maximum_fusion.1), channel_id=1, source_target_pairs={{4,0},{5,1},{6,2},{7,3},{8,4},{9,5},{10,6},{11,7},{12,8},{13,9},{1... | collective-permute-start | bytes 196616 | tf_op jit(solution)/shard_map/ppermute | solution.py:468
  18.8 1.9 %conv_work.1 = (f32[256,256]{1,0:T(8,128)S(1)}, bf16[6,256,256]{2,1,0:T(8,128)(2,1)S(1)}) custom-call(bf16[256,256]{1,0:T(8,128)(2,1)} %bitcast.23, bf16[9,256,256]{2,1,0:T(8,128)(2,1)} %bitcast.21, f32[1,256]{1,0:T(1,128)} %bitcast.26), custom_call_target="tpu_custom_call" | custom-call | flops 300000000 | bytes 1500000 | tf_op jit(solution)/shard_map/conv_work/pallas_call | solution.py:217
  20.6 1.6 %boxes_work.1 = (bf16[256,1152]{1,0:T(8,128)(2,1)S(1)}, f32[256,256]{1,0:T(8,128)S(1)}, bf16[6,256,128]{2,1,0:T(8,128)(2,1)S(1)}) custom-call(bf16[1024,128]{1,0:T(8,128)(2,1)S(1)} %bitcast.19, bf16[9,256,128]{2,1,0:T(8,128)(2,1)} %bitcast.27), custom_call_target="tpu_custom_call" | custom-call | flops 300000000 | bytes 1500000 | tf_op jit(solution)/shard_map/boxes_work/pallas_call | solution.py:241
  22.2 0.0 collective-permute-done.above
  22.2 3.0 %collective-permute-done.1.below = bf16[2,128,128]{2,1,0:T(8,128)(2,1)S(1)} collective-permute-done((bf16[2,128,128]{2,1,0:T(8,128)(2,1)S(1)}, bf16[2,128,128]{2,1,0:T(8,128)(2,1)S(1)}, u32[]{:S(2)}, u32[]{:S(2)}) %collective-permute-start.1) | collective-permute-done | bytes 65568 | tf_op jit(solution)/shard_map/ppermute | solution.py:468
  25.2 1.8 %main_work.1 = (bf16[256,256]{1,0:T(8,128)(2,1)S(1)}, bf16[64,256]{1,0:T(8,128)(2,1)S(1)}, bf16[64,256]{1,0:T(8,128)(2,1)S(1)}, bf16[2,112,32,128]{3,2,1,0:T(8,128)(2,1)S(1)}, bf16[112,32,128]{2,1,0:T(8,128)(2,1)S(1)}) custom-call(s32[1]{0:T(128)} %bitcast.code.refs_0_, bf16[2,128,128]{2,1,0:T(8,128)(2,1)S(1)} %collective-permute-done.above, ...), custom_call_target="tpu_custom_call" | custom-call | flops 600000000 | bytes 5000000 | tf_op jit(solution)/shard_map/main_work/pallas_call | solution.py:260
  27.1 2.8 %collective-permute-start.2 = (bf16[112,32,128]{2,1,0:T(8,128)(2,1)S(1)}, bf16[112,32,128]{2,1,0:T(8,128)(2,1)S(1)}, u32[]{:S(2)}, u32[]{:S(2)}) collective-permute-start(bf16[112,32,128]{2,1,0:T(8,128)(2,1)S(1)} %get-tuple-element.28), channel_id=1, source_target_pairs={{0,1},{1,0},{2,3},{3,2},{4,5},{5,4},{6,7},{7,6},{8,9},{9,8},{10,11... | collective-permute-start | bytes 2752520 | tf_op jit(solution)/shard_map/ppermute | solution.py:486
  29.8 2.1 %collective-permute-done.2.received = bf16[112,32,128]{2,1,0:T(8,128)(2,1)S(1)} collective-permute-done((bf16[112,32,128]{2,1,0:T(8,128)(2,1)S(1)}, bf16[112,32,128]{2,1,0:T(8,128)(2,1)S(1)}, u32[]{:S(2)}, u32[]{:S(2)}) %collective-permute-start.2) | collective-permute-done | bytes 917536 | tf_op jit(solution)/shard_map/ppermute | solution.py:486
  31.9 1.0 %pair_work.1 = bf16[112,32,128]{2,1,0:T(8,128)(2,1)} custom-call(s32[1]{0:T(128)} %bitcast.code.refs_0_, bf16[2,112,32,128]{3,2,1,0:T(8,128)(2,1)S(1)} %get-tuple-element.27.packed, bf16[112,32,128]{2,1,0:T(8,128)(2,1)S(1)} %collective-permute-done.2.received), custom_call_target="tpu_custom_call" | custom-call | tf_op jit(solution)/shard_map/pair_work/pallas_call | solution.py:299
  32.9 6.0 %all-to-all-start.1 = ((bf16[32,112,128]{2,1,0:T(8,128)(2,1)}), bf16[32,112,128]{2,1,0:T(8,128)(2,1)S(1)}, u32[]{:S(2)}, u32[]{:S(2)}) async-start(bf16[32,112,128]{2,1,0:T(8,128)(2,1)} %bitcast.11), calls=%async_computation.1 | async-start | bytes 1835008 | tf_op jit(solution)/shard_map/all_to_all | solution.py:492
  39.0 3.0 %collective-permute-start.3 = (bf16[64,256]{1,0:T(8,128)(2,1)S(1)}, bf16[64,256]{1,0:T(8,128)(2,1)S(1)}, u32[]{:S(2)}, u32[]{:S(2)}) collective-permute-start(bf16[64,256]{1,0:T(8,128)(2,1)S(1)} %get-tuple-element.29), channel_id=1, source_target_pairs={{0,4},{1,5},{2,6},{3,7},{4,8},{5,9},{6,10},{7,11},{8,12},{9,13},{1... | collective-permute-start | bytes 98312 | tf_op jit(solution)/shard_map/ppermute | solution.py:487
  42.0 1.3 %collective-permute-start.4 = (bf16[64,256]{1,0:T(8,128)(2,1)S(1)}, bf16[64,256]{1,0:T(8,128)(2,1)S(1)}, u32[]{:S(2)}, u32[]{:S(2)}) collective-permute-start(bf16[64,256]{1,0:T(8,128)(2,1)S(1)} %get-tuple-element.30), channel_id=1, source_target_pairs={{4,0},{5,1},{6,2},{7,3},{8,4},{9,5},{10,6},{11,7},{12,8},{13,9},{1... | collective-permute-start | bytes 98312 | tf_op jit(solution)/shard_map/ppermute | solution.py:488
  43.3 5.7 %collective-permute-done.3.above = bf16[64,256]{1,0:T(8,128)(2,1)S(1)} collective-permute-done((bf16[64,256]{1,0:T(8,128)(2,1)S(1)}, bf16[64,256]{1,0:T(8,128)(2,1)S(1)}, u32[]{:S(2)}, u32[]{:S(2)}) %collective-permute-start.3) | collective-permute-done | bytes 32800 | tf_op jit(solution)/shard_map/ppermute | solution.py:487
  49.0 0.0 collective-permute-done.4.below
  49.0 4.6 %all-to-all-done.1.pieces = bf16[32,112,128]{2,1,0:T(8,128)(2,1)S(1)} async-done(((bf16[32,112,128]{2,1,0:T(8,128)(2,1)}), bf16[32,112,128]{2,1,0:T(8,128)(2,1)S(1)}, u32[]{:S(2)}, u32[]{:S(2)}) %all-to-all-start.1) | async-done | bytes 917536 | tf_op jit(solution)/shard_map/all_to_all | solution.py:492
  53.6 0.8 block_work.1
  54.4 13.3 %all-to-all-start.2 = ((bf16[8,32,128]{2,1,0:T(8,128)(2,1)}), bf16[8,32,128]{2,1,0:T(8,128)(2,1)S(1)}, u32[]{:S(2)}, u32[]{:S(2)}) async-start(bf16[8,32,128]{2,1,0:T(8,128)(2,1)} %block_work.1), calls=%async_computation.2 | async-start | bytes 131072 | tf_op jit(solution)/shard_map/all_to_all | solution.py:496
  67.7 2.4 %input_work.1 = bf16[256,256]{1,0:T(8,128)(2,1)} custom-call(bf16[256,256]{1,0:T(8,128)(2,1)S(1)} %get-tuple-element.32.delta, bf16[64,256]{1,0:T(8,128)(2,1)S(1)} %collective-permute-done.3.above, bf16[64,256]{1,0:T(8,128)(2,1)S(1)} %collective-permute-done.4.below, bf16[9,256,256]{2,1,0:T(8,128)(2,1)} %bitcast.22), custom_call_target="tpu_custom_call" | custom-call | flops 300000000 | bytes 2000000 | tf_op jit(solution)/shard_map/input_work/pallas_call | solution.py:376
  70.1 9.0 %all-to-all-done.2.pieces = bf16[8,32,128]{2,1,0:T(8,128)(2,1)S(1)} async-done(((bf16[8,32,128]{2,1,0:T(8,128)(2,1)}), bf16[8,32,128]{2,1,0:T(8,128)(2,1)S(1)}, u32[]{:S(2)}, u32[]{:S(2)}) %all-to-all-start.2) | async-done | bytes 65568 | tf_op jit(solution)/shard_map/all_to_all | solution.py:496
  79.1 12.2 %all_to_all.20.refs_1_ = bf16[16,32,128]{2,1,0:T(8,128)(2,1)S(1)} all-to-all(bf16[16,32,128]{2,1,0:T(8,128)(2,1)S(1)} %column_work.1), channel_id=1, replica_groups={{0,1,2,3,8,9,10,11,16,17,18,19,24,25,26,27},{4,5,6,7,12,13,14,15,20,21,..., dimensions={0} | all-to-all | bytes 262144 | tf_op jit(solution)/shard_map/all_to_all | solution.py:498
  91.4 0.8 unpack.1
  (7 shorter events, 0.1 us)
Async XLA Ops:
  0.6 15.4 %all-to-all-start = ((bf16[4,2,128,128]{3,2,1,0:T(8,128)(2,1)}), bf16[4,2,128,128]{3,2,1,0:T(8,128)(2,1)S(1)}, u32[]{:S(2)}, u32[]{:S(2)}) async-start(bf16[4,2,128,128]{3,2,1,0:T(8,128)(2,1)} %param.5), calls=%async_computation | async-start | bytes 524288 | tf_op jit(solution)/shard_map/all_to_all | solution.py:460
  16.1 6.2 %collective-permute-start = (bf16[2,128,128]{2,1,0:T(8,128)(2,1)S(1)}, bf16[2,128,128]{2,1,0:T(8,128)(2,1)S(1)}, u32[]{:S(2)}, u32[]{:S(2)}) collective-permute-start(bf16[2,128,128]{2,1,0:T(8,128)(2,1)S(1)} %pad_maximum_fusion), channel_id=1, source_target_pairs={{0,4},{1,5},{2,6},{3,7},{4,8},{5,9},{6,10},{7,11},{8,12},{9,13},{1... | collective-permute-start | bytes 196616 | tf_op jit(solution)/shard_map/ppermute | solution.py:467
  17.4 7.8 %collective-permute-start.1 = (bf16[2,128,128]{2,1,0:T(8,128)(2,1)S(1)}, bf16[2,128,128]{2,1,0:T(8,128)(2,1)S(1)}, u32[]{:S(2)}, u32[]{:S(2)}) collective-permute-start(bf16[2,128,128]{2,1,0:T(8,128)(2,1)S(1)} %pad_maximum_fusion.1), channel_id=1, source_target_pairs={{4,0},{5,1},{6,2},{7,3},{8,4},{9,5},{10,6},{11,7},{12,8},{13,9},{1... | collective-permute-start | bytes 196616 | tf_op jit(solution)/shard_map/ppermute | solution.py:468
  27.1 4.9 %collective-permute-start.2 = (bf16[112,32,128]{2,1,0:T(8,128)(2,1)S(1)}, bf16[112,32,128]{2,1,0:T(8,128)(2,1)S(1)}, u32[]{:S(2)}, u32[]{:S(2)}) collective-permute-start(bf16[112,32,128]{2,1,0:T(8,128)(2,1)S(1)} %get-tuple-element.28), channel_id=1, source_target_pairs={{0,1},{1,0},{2,3},{3,2},{4,5},{5,4},{6,7},{7,6},{8,9},{9,8},{10,11... | collective-permute-start | bytes 2752520 | tf_op jit(solution)/shard_map/ppermute | solution.py:486
  32.9 20.7 %all-to-all-start.1 = ((bf16[32,112,128]{2,1,0:T(8,128)(2,1)}), bf16[32,112,128]{2,1,0:T(8,128)(2,1)S(1)}, u32[]{:S(2)}, u32[]{:S(2)}) async-start(bf16[32,112,128]{2,1,0:T(8,128)(2,1)} %bitcast.11), calls=%async_computation.1 | async-start | bytes 1835008 | tf_op jit(solution)/shard_map/all_to_all | solution.py:492
  39.0 10.0 %collective-permute-start.3 = (bf16[64,256]{1,0:T(8,128)(2,1)S(1)}, bf16[64,256]{1,0:T(8,128)(2,1)S(1)}, u32[]{:S(2)}, u32[]{:S(2)}) collective-permute-start(bf16[64,256]{1,0:T(8,128)(2,1)S(1)} %get-tuple-element.29), channel_id=1, source_target_pairs={{0,4},{1,5},{2,6},{3,7},{4,8},{5,9},{6,10},{7,11},{8,12},{9,13},{1... | collective-permute-start | bytes 98312 | tf_op jit(solution)/shard_map/ppermute | solution.py:487
  42.0 7.0 %collective-permute-start.4 = (bf16[64,256]{1,0:T(8,128)(2,1)S(1)}, bf16[64,256]{1,0:T(8,128)(2,1)S(1)}, u32[]{:S(2)}, u32[]{:S(2)}) collective-permute-start(bf16[64,256]{1,0:T(8,128)(2,1)S(1)} %get-tuple-element.30), channel_id=1, source_target_pairs={{4,0},{5,1},{6,2},{7,3},{8,4},{9,5},{10,6},{11,7},{12,8},{13,9},{1... | collective-permute-start | bytes 98312 | tf_op jit(solution)/shard_map/ppermute | solution.py:488
  54.4 24.7 %all-to-all-start.2 = ((bf16[8,32,128]{2,1,0:T(8,128)(2,1)}), bf16[8,32,128]{2,1,0:T(8,128)(2,1)S(1)}, u32[]{:S(2)}, u32[]{:S(2)}) async-start(bf16[8,32,128]{2,1,0:T(8,128)(2,1)} %block_work.1), calls=%async_computation.2 | async-start | bytes 131072 | tf_op jit(solution)/shard_map/all_to_all | solution.py:496
